TPU v7x, 256 devices: a whole 4x4x8 slice. The times are simulated.
256 devices in a mesh: tm: 32 (over y, x, core), head: 8 (over z).
Axes of the slice: x: 4, y: 4, z: 8, core: 2. Of those that a mesh axis runs over, the one named last changes fastest.
Arguments:
- queries: bfloat16 [16384, 3072], P('tm', 'head'), may hold values from -700 to 700
- key_rows: bfloat16 [16384, 3072], P('tm', 'head'), may hold values from -700 to 700
- value_rows: bfloat16 [16384, 3072], P('tm', 'head'), may hold values from -6 to 6
- query_gain: float32 [3072], P('head'), may hold values from 0.1 to 1.9
- key_gain: float32 [3072], P('head'), may hold values from 0.1 to 1.9
- block_mask: int32 [32, 7, 4, 4], replicated, may hold values from 0 to 1, as said below
- out_grad: bfloat16 [16384, 3072], P('tm', 'head'), may hold values from -6 to 6
Outputs:
- attended: bfloat16 [16384, 3072], P('tm', 'head')
- query_grad: bfloat16 [16384, 3072], P('tm', 'head')
- key_grad: bfloat16 [16384, 3072], P('tm', 'head')
- value_grad: bfloat16 [16384, 3072], P('tm', 'head')
Inputs may be any that keep to these rules, and one draw needn't show every extreme that they name: block_mask[f, 3] is all ones; for every f and j some entry of block_mask[f, j] is one.
All inputs are finite; a program needn't handle non-finite values.
Results may differ from a plain program's by a relative error of at most 0.022.
Values may be sent and summed in bfloat16 or wider, within the bound.
No kernel may reach another device: no remote copies, remote signals or barrier semaphores. Data moves between devices by JAX's collectives and lax.ppermute only.
A program may use at most 128 MiB of HBM per device.

v0:
```python
import jax
import jax.numpy as jnp
from jax import lax
from jax.sharding import PartitionSpec as P

HEAD_DIM = 128
BLK = 128
REACH = 3


epsilon = 1e-06


def shifted(value, axis, steps):
    count = lax.axis_size(axis)
    initial, last = (max(0, -steps), min(count, count - steps))
    return lax.ppermute(value, axis, [(source, source + steps) for source in range(initial, last)])


def head_cut(matrix, head_index):
    return lax.dynamic_slice_in_dim(matrix, head_index * HEAD_DIM, HEAD_DIM, 1)


def head_paste(buffer, piece, head_index):
    return lax.dynamic_update_slice_in_dim(
        buffer, piece.astype(buffer.dtype), head_index * HEAD_DIM, 1
    )


def masked_scores(query_part, key_part, live_mask, score_scale):
    scores = (
        jnp.einsum("qd,kd->qk", query_part, key_part, preferred_element_type=jnp.float32)
        * score_scale
    )
    return jnp.where(live_mask, scores, -jnp.inf)


def expand_live(mask_rows, is_valid):
    band_size = mask_rows.shape[0]
    blocks = mask_rows.shape[1]
    live_blocks = (mask_rows > 0) & is_valid[:, None, None]
    expanded = jnp.broadcast_to(
        live_blocks[:, :, None, :, None], (band_size, blocks, BLK, blocks, BLK)
    )
    expanded = expanded.reshape(band_size, blocks * BLK, blocks * BLK)
    return jnp.transpose(expanded, (1, 0, 2)).reshape(blocks * BLK, band_size * blocks * BLK)


def query_side(query_norm, key_band, value_band, out_grad, live_mask, score_scale):
    row_count, column_count = query_norm.shape
    heads_here = column_count // HEAD_DIM

    def one_head(head_index, buffers):
        query_part = head_cut(query_norm, head_index)
        key_part = head_cut(key_band, head_index)
        value_part = head_cut(value_band, head_index)
        grad_part = head_cut(out_grad, head_index)
        scores = masked_scores(query_part, key_part, live_mask, score_scale)
        row_top = jnp.max(scores, axis=1, keepdims=True)
        log_total = row_top + jnp.log(jnp.sum(jnp.exp(scores - row_top), axis=1, keepdims=True))
        weights = jnp.exp(scores - log_total)
        weights_low = weights.astype(jnp.bfloat16)
        attended = jnp.dot(weights_low, value_part, preferred_element_type=jnp.float32).astype(
            jnp.bfloat16
        )
        row_delta = jnp.sum(
            grad_part.astype(jnp.float32) * attended.astype(jnp.float32), axis=1, keepdims=True
        )
        grad_weights = jnp.einsum(
            "qd,kd->qk", grad_part, value_part, preferred_element_type=jnp.float32
        )
        grad_scores = (score_scale * weights * (grad_weights - row_delta)).astype(jnp.bfloat16)
        grad_query = jnp.dot(grad_scores, key_part, preferred_element_type=jnp.float32)
        result = [
            head_paste(buffers[0], attended, head_index),
            head_paste(buffers[1], grad_query, head_index),
        ]
        grad_key = jnp.einsum(
            "qk,qd->kd", grad_scores, query_part, preferred_element_type=jnp.float32
        )
        grad_value = jnp.einsum(
            "qk,qd->kd", weights_low, grad_part, preferred_element_type=jnp.float32
        )
        result.append(head_paste(buffers[2], grad_key, head_index))
        result.append(head_paste(buffers[3], grad_value, head_index))
        return tuple(result)

    start = [
        jnp.zeros((row_count, column_count), jnp.bfloat16),
        jnp.zeros((row_count, column_count), jnp.float32),
    ]
    start.append(jnp.zeros(key_band.shape, jnp.bfloat16))
    start.append(jnp.zeros(key_band.shape, jnp.bfloat16))
    return lax.fori_loop(0, heads_here, one_head, tuple(start))


def local(queries, key_rows, value_rows, query_gain, key_gain, block_mask, out_grad):
    row_count, column_count = queries.shape
    frame_index = lax.axis_index("tm")
    frame_count = lax.axis_size("tm")
    full_width = column_count * lax.axis_size("head")
    score_scale = HEAD_DIM ** (-0.5)
    band_size = 2 * REACH + 1
    query_float = queries.astype(jnp.float32)
    key_float = key_rows.astype(jnp.float32)
    query_square, key_square = lax.psum(
        (jnp.sum(query_float * query_float, axis=1), jnp.sum(key_float * key_float, axis=1)), "head"
    )
    query_rate = lax.rsqrt(query_square / full_width + epsilon)[:, None]
    key_rate = lax.rsqrt(key_square / full_width + epsilon)[:, None]
    query_norm = (query_float * query_rate * query_gain).astype(jnp.bfloat16)
    key_norm = (key_float * key_rate * key_gain).astype(jnp.bfloat16)
    paired = jnp.stack([key_norm, value_rows])
    band_list = [
        paired if offset == 0 else shifted(paired, "tm", -offset)
        for offset in range(-REACH, REACH + 1)
    ]
    stacked = jnp.stack(band_list)
    key_band = stacked[:, 0].reshape(band_size * row_count, column_count)
    value_band = stacked[:, 1].reshape(band_size * row_count, column_count)
    offsets = jnp.arange(band_size, dtype=jnp.int32) - REACH
    mask_rows = lax.dynamic_index_in_dim(block_mask, frame_index, 0, keepdims=False)
    is_valid = (frame_index + offsets >= 0) & (frame_index + offsets < frame_count)
    live_mask = expand_live(mask_rows, is_valid)
    attended, grad_qnorm, key_terms, value_terms = query_side(
        query_norm, key_band, value_band, out_grad, live_mask, score_scale
    )
    both_terms = jnp.stack(
        [
            key_terms.reshape(band_size, row_count, column_count),
            value_terms.reshape(band_size, row_count, column_count),
        ],
        axis=1,
    )
    summed = both_terms[REACH].astype(jnp.float32)
    for offset in range(-REACH, REACH + 1):
        if offset != 0:
            arrived = shifted(both_terms[REACH + offset], "tm", offset)
            summed = summed + arrived.astype(jnp.float32)
    grad_knorm = summed[0]
    value_sum = summed[1]
    query_dot, key_dot = lax.psum(
        (
            jnp.sum(query_float * query_gain * grad_qnorm, axis=1),
            jnp.sum(key_float * key_gain * grad_knorm, axis=1),
        ),
        "head",
    )
    query_grad = (
        query_rate * query_gain * grad_qnorm
        - query_float * query_rate**3 * query_dot[:, None] / full_width
    )
    key_grad = (
        key_rate * key_gain * grad_knorm - key_float * key_rate**3 * key_dot[:, None] / full_width
    )
    return (
        attended,
        query_grad.astype(jnp.bfloat16),
        key_grad.astype(jnp.bfloat16),
        value_sum.astype(jnp.bfloat16),
    )


def solution(mesh):
    return jax.shard_map(
        local,
        mesh=mesh,
        in_specs=(
            P("tm", "head"),
            P("tm", "head"),
            P("tm", "head"),
            P("head"),
            P("head"),
            P(),
            P("tm", "head"),
        ),
        out_specs=(P("tm", "head"), P("tm", "head"), P("tm", "head"), P("tm", "head")),
        check_vma=False,
    )
```

profile of v0, /device:TPU:8, one launch (start us, length us, event | category | flops | bytes accessed | tf_op | source)
XLA Modules:
  0.0 275.7 jit_solution(4754300717281592673)
XLA Ops:
  3.0 20.0 %all-reduce.1 = (f32[512]{0:T(512)S(1)}, f32[512]{0:T(512)S(1)}) all-reduce(f32[512]{0:T(512)S(1)} %fusion.23, f32[512]{0:T(512)S(1)} %fusion.32), channel_id=1, replica_groups=mesh['tm'=32,'head'=8] {'head'}, use_global_device_ids=true, to_apply=%region_1.0 | all-reduce | flops 1024 | bytes 8192 | tf_op jit(solution)/shard_map/psum | solution.py:106
  27.2 4.6 %collective-permute-start.4 = (bf16[2,512,384]{2,1,0:T(8,128)(2,1)S(1)}, bf16[2,512,384]{2,1,0:T(8,128)(2,1)S(1)}, u32[]{:S(2)}, u32[]{:S(2)}) collective-permute-start(bf16[2,512,384]{2,1,0:T(8,128)(2,1)S(1)} %pad_maximum_fusion.1), channel_id=1, source_target_pairs={{16,0},{24,8},{32,16},{40,24},{48,32},{56,40},{64,48},{72,56},{80,... | collective-permute-start | bytes 2359304 | tf_op jit(solution)/shard_map/ppermute | solution.py:17
  31.8 4.0 %collective-permute-start.3 = (bf16[2,512,384]{2,1,0:T(8,128)(2,1)S(1)}, bf16[2,512,384]{2,1,0:T(8,128)(2,1)}, u32[]{:S(2)}, u32[]{:S(2)}) collective-permute-start(bf16[2,512,384]{2,1,0:T(8,128)(2,1)S(1)} %pad_maximum_fusion.1), channel_id=1, source_target_pairs={{8,0},{16,8},{24,16},{32,24},{40,32},{48,40},{56,48},{64,56},{72,6... | collective-permute-start | bytes 2359304 | tf_op jit(solution)/shard_map/ppermute | solution.py:17
  35.9 2.0 collective-permute-start.2
  37.9 3.5 %collective-permute-start.1 = (bf16[2,512,384]{2,1,0:T(8,128)(2,1)S(1)}, bf16[2,512,384]{2,1,0:T(8,128)(2,1)}, u32[]{:S(2)}, u32[]{:S(2)}) collective-permute-start(bf16[2,512,384]{2,1,0:T(8,128)(2,1)S(1)} %pad_maximum_fusion.1), channel_id=1, source_target_pairs={{0,16},{8,24},{16,32},{24,40},{32,48},{40,56},{48,64},{56,72},{64,... | collective-permute-start | bytes 2359304 | tf_op jit(solution)/shard_map/ppermute | solution.py:17
  43.1 6.5 %collective-permute-done = bf16[2,512,384]{2,1,0:T(8,128)(2,1)} collective-permute-done((bf16[2,512,384]{2,1,0:T(8,128)(2,1)S(1)}, bf16[2,512,384]{2,1,0:T(8,128)(2,1)}, u32[]{:S(2)}, u32[]{:S(2)}) %collective-permute-start) | collective-permute-done | bytes 786464 | tf_op jit(solution)/shard_map/ppermute | solution.py:17
  52.7 17.3 %collective-permute-done.1 = bf16[2,512,384]{2,1,0:T(8,128)(2,1)} collective-permute-done((bf16[2,512,384]{2,1,0:T(8,128)(2,1)S(1)}, bf16[2,512,384]{2,1,0:T(8,128)(2,1)}, u32[]{:S(2)}, u32[]{:S(2)}) %collective-permute-start.1) | collective-permute-done | bytes 786464 | tf_op jit(solution)/shard_map/ppermute | solution.py:17
  72.7 6.8 %collective-permute-done.3 = bf16[2,512,384]{2,1,0:T(8,128)(2,1)} collective-permute-done((bf16[2,512,384]{2,1,0:T(8,128)(2,1)S(1)}, bf16[2,512,384]{2,1,0:T(8,128)(2,1)}, u32[]{:S(2)}, u32[]{:S(2)}) %collective-permute-start.3) | collective-permute-done | bytes 786464 | tf_op jit(solution)/shard_map/ppermute | solution.py:17
  81.6 3.0 %fusion.56 = (bf16[7,1,512,384]{3,2,1,0:T(8,128)(2,1)}, bf16[7,1,512,384]{3,2,1,0:T(8,128)(2,1)}) fusion(bf16[7,2,512,384]{3,2,1,0:T(8,128)(2,1)S(1)} %bitcast_dynamic-update-slice_fusion), kind=kLoop, calls=%fused_computation.104 | loop fusion | bytes 11010048 | tf_op jit(solution)/shard_map/slice | solution.py:120
  89.9 104.2 %while.20 = (s32[]{:T(128)}, bf16[512,384]{1,0:T(8,128)(2,1)}, f32[512,384]{1,0:T(8,128)}, bf16[3584,384]{1,0:T(8,128)(2,1)}, bf16[3584,384]{1,0:T(8,128)(2,1)},...) while((s32[]{:T(128)}, bf16[512,384]{1,0:T(8,128)(2,1)}, ...), condition=%wide.region_8.9_spmd.clone, body=%wide.region_4.8_spmd.clone.sunk | while | flops 2845506560 | bytes 142896576 | solution.py:94
  90.0 2.2 broadcast_in_dim.50
  92.3 6.1 %reshape.71 = pred[7,512,512]{2,1,0:T(32,128)(4,1)S(1)} reshape(pred[7,4,128,4,128]{4,3,2,1,0:T(4,128)(4,1)} %broadcast_in_dim.50) | data formatting | bytes 3670016 | tf_op jit(solution)/shard_map/reshape | solution.py:45
  100.4 2.0 copy.37
  102.4 2.8 %fusion.74 = (f32[512]{0:T(512)S(1)}, f32[512,3584]{1,0:T(8,128)S(1)}) fusion(pred[512,3584]{1,0:T(32,128)(4,1)S(1)} %copy.37, bf16[3584,384]{1,0:T(8,128)(2,1)} %get-tuple-element.390, s32[]{:T(128)S(6)} %select_n.31, bf16[512,384]{1,0:T(8,128)(2,1)S(1)} %get-tuple-element.389), kind=kOutput, calls=%fused_computation.103.clone.1 | convolution fusion | flops 475266560 | bytes 10226688 | tf_op jit(solution)/shard_map/while/body/eval_jaxpr/qd,kd->qk/dot_general | solution.py:32
  106.3 2.3 copy-done.1
  111.3 5.8 %fusion.76 = bf16[3584,384]{1,0:T(8,128)(2,1)} fusion(bf16[3584,384]{1,0:T(8,128)(2,1)} %get-tuple-element.374, s32[]{:T(128)S(6)} %select_n.31, bf16[512,384]{1,0:T(8,128)(2,1)S(1)} %get-tuple-element.392, f32[512,3584]{1,0:T(8,128)} %copy-done.1, f32[512]{0:T(512)S(1)} %log_add_fusion.2), kind=kOutput, calls=%fused_computation.7.clone.1 | convolution fusion | flops 473890816 | bytes 8391680 | tf_op jit(solution)/shard_map/while/body/eval_jaxpr/qk,qd->kd/dot_general | solution.py:81
  117.0 2.4 multiply_convert_fusion.2
  119.4 3.1 %convolution_dynamic-update-slice_fusion.2 = f32[512,384]{1,0:T(8,128)} fusion(f32[512,384]{1,0:T(8,128)} %get-tuple-element.372, s32[]{:T(128)S(6)} %select_n.31, bf16[512,3584]{1,0:T(8,128)(2,1)S(1)} %multiply_convert_fusion.2, bf16[3584,384]{1,0:T(8,128)(2,1)} %get-tuple-element.390), kind=kOutput, calls=%fused_computation.10.clone.1 | convolution fusion | flops 469762048 | bytes 4850688 | tf_op jit(solution)/shard_map/while/body/eval_jaxpr/dot_general | solution.py:73
  122.5 2.2 fusion.75
  124.8 2.2 broadcast_in_dim.50
  127.1 6.1 %reshape.71 = pred[7,512,512]{2,1,0:T(32,128)(4,1)S(1)} reshape(pred[7,4,128,4,128]{4,3,2,1,0:T(4,128)(4,1)} %broadcast_in_dim.50) | data formatting | bytes 3670016 | tf_op jit(solution)/shard_map/reshape | solution.py:45
  135.2 2.0 copy.37
  137.2 2.8 %fusion.74 = (f32[512]{0:T(512)S(1)}, f32[512,3584]{1,0:T(8,128)S(1)}) fusion(pred[512,3584]{1,0:T(32,128)(4,1)S(1)} %copy.37, bf16[3584,384]{1,0:T(8,128)(2,1)} %get-tuple-element.390, s32[]{:T(128)S(6)} %select_n.31, bf16[512,384]{1,0:T(8,128)(2,1)S(1)} %get-tuple-element.389), kind=kOutput, calls=%fused_computation.103.clone.1 | convolution fusion | flops 475266560 | bytes 10226688 | tf_op jit(solution)/shard_map/while/body/eval_jaxpr/qd,kd->qk/dot_general | solution.py:32
  141.1 2.3 copy-done.1
  146.1 5.7 %fusion.76 = bf16[3584,384]{1,0:T(8,128)(2,1)} fusion(bf16[3584,384]{1,0:T(8,128)(2,1)} %get-tuple-element.374, s32[]{:T(128)S(6)} %select_n.31, bf16[512,384]{1,0:T(8,128)(2,1)S(1)} %get-tuple-element.392, f32[512,3584]{1,0:T(8,128)} %copy-done.1, f32[512]{0:T(512)S(1)} %log_add_fusion.2), kind=kOutput, calls=%fused_computation.7.clone.1 | convolution fusion | flops 473890816 | bytes 8391680 | tf_op jit(solution)/shard_map/while/body/eval_jaxpr/qk,qd->kd/dot_general | solution.py:81
  151.8 2.3 multiply_convert_fusion.2
  154.1 3.1 %convolution_dynamic-update-slice_fusion.2 = f32[512,384]{1,0:T(8,128)} fusion(f32[512,384]{1,0:T(8,128)} %get-tuple-element.372, s32[]{:T(128)S(6)} %select_n.31, bf16[512,3584]{1,0:T(8,128)(2,1)S(1)} %multiply_convert_fusion.2, bf16[3584,384]{1,0:T(8,128)(2,1)} %get-tuple-element.390), kind=kOutput, calls=%fused_computation.10.clone.1 | convolution fusion | flops 469762048 | bytes 4850688 | tf_op jit(solution)/shard_map/while/body/eval_jaxpr/dot_general | solution.py:73
  157.2 2.2 fusion.75
  159.5 2.2 broadcast_in_dim.50
  161.8 6.1 %reshape.71 = pred[7,512,512]{2,1,0:T(32,128)(4,1)S(1)} reshape(pred[7,4,128,4,128]{4,3,2,1,0:T(4,128)(4,1)} %broadcast_in_dim.50) | data formatting | bytes 3670016 | tf_op jit(solution)/shard_map/reshape | solution.py:45
  169.9 2.0 copy.37
  171.9 2.8 %fusion.74 = (f32[512]{0:T(512)S(1)}, f32[512,3584]{1,0:T(8,128)S(1)}) fusion(pred[512,3584]{1,0:T(32,128)(4,1)S(1)} %copy.37, bf16[3584,384]{1,0:T(8,128)(2,1)} %get-tuple-element.390, s32[]{:T(128)S(6)} %select_n.31, bf16[512,384]{1,0:T(8,128)(2,1)S(1)} %get-tuple-element.389), kind=kOutput, calls=%fused_computation.103.clone.1 | convolution fusion | flops 475266560 | bytes 10226688 | tf_op jit(solution)/shard_map/while/body/eval_jaxpr/qd,kd->qk/dot_general | solution.py:32
  175.8 2.3 copy-done.1
  180.8 5.7 %fusion.76 = bf16[3584,384]{1,0:T(8,128)(2,1)} fusion(bf16[3584,384]{1,0:T(8,128)(2,1)} %get-tuple-element.374, s32[]{:T(128)S(6)} %select_n.31, bf16[512,384]{1,0:T(8,128)(2,1)S(1)} %get-tuple-element.392, f32[512,3584]{1,0:T(8,128)} %copy-done.1, f32[512]{0:T(512)S(1)} %log_add_fusion.2), kind=kOutput, calls=%fused_computation.7.clone.1 | convolution fusion | flops 473890816 | bytes 8391680 | tf_op jit(solution)/shard_map/while/body/eval_jaxpr/qk,qd->kd/dot_general | solution.py:81
  186.5 2.4 multiply_convert_fusion.2
  188.9 3.1 %convolution_dynamic-update-slice_fusion.2 = f32[512,384]{1,0:T(8,128)} fusion(f32[512,384]{1,0:T(8,128)} %get-tuple-element.372, s32[]{:T(128)S(6)} %select_n.31, bf16[512,3584]{1,0:T(8,128)(2,1)S(1)} %multiply_convert_fusion.2, bf16[3584,384]{1,0:T(8,128)(2,1)} %get-tuple-element.390), kind=kOutput, calls=%fused_computation.10.clone.1 | convolution fusion | flops 469762048 | bytes 4850688 | tf_op jit(solution)/shard_map/while/body/eval_jaxpr/dot_general | solution.py:73
  192.0 2.1 fusion.75
  194.1 2.9 %fusion.51 = (bf16[2,512,384]{2,1,0:T(8,128)(2,1)S(1)}, bf16[2,512,384]{2,1,0:T(8,128)(2,1)S(1)}, bf16[2,512,384]{2,1,0:T(8,128)(2,1)S(1)}, bf16[2,512,384]{2,1,...) fusion(bf16[7,1,512,384]{3,2,1,0:T(8,128)(2,1)} %bitcast.62, ...), kind=kLoop, calls=%fused_computation.92 | loop fusion | flops 2359296 | bytes 10223616 | tf_op jit(solution)/shard_map/squeeze | solution.py:138
  197.0 6.3 %collective-permute-start.6 = (bf16[2,512,384]{2,1,0:T(8,128)(2,1)S(1)}, bf16[2,512,384]{2,1,0:T(8,128)(2,1)S(1)}, u32[]{:S(2)}, u32[]{:S(2)}) collective-permute-start(bf16[2,512,384]{2,1,0:T(8,128)(2,1)S(1)} %get-tuple-element.273), channel_id=1, source_target_pairs={{24,0},{32,8},{40,16},{48,24},{56,32},{64,40},{72,48},{80,56},{88,... | collective-permute-start | bytes 2359304 | tf_op jit(solution)/shard_map/ppermute | solution.py:17
  203.3 3.5 %collective-permute-start.7 = (bf16[2,512,384]{2,1,0:T(8,128)(2,1)S(1)}, bf16[2,512,384]{2,1,0:T(8,128)(2,1)S(1)}, u32[]{:S(2)}, u32[]{:S(2)}) collective-permute-start(bf16[2,512,384]{2,1,0:T(8,128)(2,1)S(1)} %get-tuple-element.274), channel_id=1, source_target_pairs={{16,0},{24,8},{32,16},{40,24},{48,32},{56,40},{64,48},{72,56},{80,... | collective-permute-start | bytes 2359304 | tf_op jit(solution)/shard_map/ppermute | solution.py:17
  208.7 2.4 collective-permute-start.9
  211.1 3.9 %collective-permute-start.11 = (bf16[2,512,384]{2,1,0:T(8,128)(2,1)S(1)}, bf16[2,512,384]{2,1,0:T(8,128)(2,1)S(1)}, u32[]{:S(2)}, u32[]{:S(2)}) collective-permute-start(bf16[2,512,384]{2,1,0:T(8,128)(2,1)S(1)} %get-tuple-element.277), channel_id=1, source_target_pairs={{0,24},{8,32},{16,40},{24,48},{32,56},{40,64},{48,72},{56,80},{64,... | collective-permute-start | bytes 2359304 | tf_op jit(solution)/shard_map/ppermute | solution.py:17
  215.0 3.3 %collective-permute-done.6 = bf16[2,512,384]{2,1,0:T(8,128)(2,1)S(1)} collective-permute-done((bf16[2,512,384]{2,1,0:T(8,128)(2,1)S(1)}, bf16[2,512,384]{2,1,0:T(8,128)(2,1)S(1)}, u32[]{:S(2)}, u32[]{:S(2)}) %collective-permute-start.6) | collective-permute-done | bytes 786464 | tf_op jit(solution)/shard_map/ppermute | solution.py:17
  218.3 10.7 %collective-permute-start.10 = (bf16[2,512,384]{2,1,0:T(8,128)(2,1)S(1)}, bf16[2,512,384]{2,1,0:T(8,128)(2,1)S(1)}, u32[]{:S(2)}, u32[]{:S(2)}) collective-permute-start(bf16[2,512,384]{2,1,0:T(8,128)(2,1)S(1)} %get-tuple-element.278), channel_id=1, source_target_pairs={{0,16},{8,24},{16,32},{24,40},{32,48},{40,56},{48,64},{56,72},{64,... | collective-permute-start | bytes 2359304 | tf_op jit(solution)/shard_map/ppermute | solution.py:17
  229.3 11.2 %collective-permute-done.7 = bf16[2,512,384]{2,1,0:T(8,128)(2,1)S(1)} collective-permute-done((bf16[2,512,384]{2,1,0:T(8,128)(2,1)S(1)}, bf16[2,512,384]{2,1,0:T(8,128)(2,1)S(1)}, u32[]{:S(2)}, u32[]{:S(2)}) %collective-permute-start.7) | collective-permute-done | bytes 786464 | tf_op jit(solution)/shard_map/ppermute | solution.py:17
  240.5 14.7 %collective-permute-done.8 = bf16[2,512,384]{2,1,0:T(8,128)(2,1)S(1)} collective-permute-done((bf16[2,512,384]{2,1,0:T(8,128)(2,1)S(1)}, bf16[2,512,384]{2,1,0:T(8,128)(2,1)S(1)}, u32[]{:S(2)}, u32[]{:S(2)}) %collective-permute-start.8) | collective-permute-done | bytes 786464 | tf_op jit(solution)/shard_map/ppermute | solution.py:17
  255.2 2.7 collective-permute-done.10
  259.5 14.1 %all-reduce = (f32[512]{0:T(512)S(1)}, f32[512]{0:T(512)S(1)}) all-reduce(f32[512]{0:T(512)S(1)} %fusion.31, f32[512]{0:T(512)S(1)} %fusion.40), channel_id=1, replica_groups=mesh['tm'=32,'head'=8] {'head'}, use_global_device_ids=true, to_apply=%region_10.11 | all-reduce | flops 1024 | bytes 8192 | tf_op jit(solution)/shard_map/psum | solution.py:142
  (107 shorter events, 44.8 us)
Async XLA Ops:
  0.6 40.8 %copy-start = (s32[32,7,4,4]{0,3,2,1:T(4,128)S(1)}, s32[32,7,4,4]{0,3,2,1:T(4,128)}, u32[]{:S(2)}) copy-start(s32[32,7,4,4]{0,3,2,1:T(4,128)} %param.14) | copy-start | bytes 43012
  24.1 48.4 %copy-start.12 = (bf16[512,384]{1,0:T(8,128)(2,1)S(1)}, bf16[512,384]{1,0:T(8,128)(2,1)}, u32[]{:S(2)}) copy-start(bf16[512,384]{1,0:T(8,128)(2,1)} %param.11) | copy-start | bytes 1179652
  25.3 24.2 %collective-permute-start = (bf16[2,512,384]{2,1,0:T(8,128)(2,1)S(1)}, bf16[2,512,384]{2,1,0:T(8,128)(2,1)}, u32[]{:S(2)}, u32[]{:S(2)}) collective-permute-start(bf16[2,512,384]{2,1,0:T(8,128)(2,1)S(1)} %pad_maximum_fusion.1), channel_id=1, source_target_pairs={{0,24},{8,32},{16,40},{24,48},{32,56},{40,64},{48,72},{56,80},{64,... | collective-permute-start | bytes 2359304 | tf_op jit(solution)/shard_map/ppermute | solution.py:17
  27.2 53.5 %collective-permute-start.4 = (bf16[2,512,384]{2,1,0:T(8,128)(2,1)S(1)}, bf16[2,512,384]{2,1,0:T(8,128)(2,1)S(1)}, u32[]{:S(2)}, u32[]{:S(2)}) collective-permute-start(bf16[2,512,384]{2,1,0:T(8,128)(2,1)S(1)} %pad_maximum_fusion.1), channel_id=1, source_target_pairs={{16,0},{24,8},{32,16},{40,24},{48,32},{56,40},{64,48},{72,56},{80,... | collective-permute-start | bytes 2359304 | tf_op jit(solution)/shard_map/ppermute | solution.py:17
  31.8 47.6 %collective-permute-start.3 = (bf16[2,512,384]{2,1,0:T(8,128)(2,1)S(1)}, bf16[2,512,384]{2,1,0:T(8,128)(2,1)}, u32[]{:S(2)}, u32[]{:S(2)}) collective-permute-start(bf16[2,512,384]{2,1,0:T(8,128)(2,1)S(1)} %pad_maximum_fusion.1), channel_id=1, source_target_pairs={{8,0},{16,8},{24,16},{32,24},{40,32},{48,40},{56,48},{64,56},{72,6... | collective-permute-start | bytes 2359304 | tf_op jit(solution)/shard_map/ppermute | solution.py:17
  35.9 35.4 %collective-permute-start.2 = (bf16[2,512,384]{2,1,0:T(8,128)(2,1)S(1)}, bf16[2,512,384]{2,1,0:T(8,128)(2,1)}, u32[]{:S(2)}, u32[]{:S(2)}) collective-permute-start(bf16[2,512,384]{2,1,0:T(8,128)(2,1)S(1)} %pad_maximum_fusion.1), channel_id=1, source_target_pairs={{0,8},{8,16},{16,24},{24,32},{32,40},{40,48},{48,56},{56,64},{64,7... | collective-permute-start | bytes 2359304 | tf_op jit(solution)/shard_map/ppermute | solution.py:17
  37.9 32.0 %collective-permute-start.1 = (bf16[2,512,384]{2,1,0:T(8,128)(2,1)S(1)}, bf16[2,512,384]{2,1,0:T(8,128)(2,1)}, u32[]{:S(2)}, u32[]{:S(2)}) collective-permute-start(bf16[2,512,384]{2,1,0:T(8,128)(2,1)S(1)} %pad_maximum_fusion.1), channel_id=1, source_target_pairs={{0,16},{8,24},{16,32},{24,40},{32,48},{40,56},{48,64},{56,72},{64,... | collective-permute-start | bytes 2359304 | tf_op jit(solution)/shard_map/ppermute | solution.py:17
  49.5 31.9 %collective-permute-start.5 = (bf16[2,512,384]{2,1,0:T(8,128)(2,1)S(1)}, bf16[2,512,384]{2,1,0:T(8,128)(2,1)S(1)}, u32[]{:S(2)}, u32[]{:S(2)}) collective-permute-start(bf16[2,512,384]{2,1,0:T(8,128)(2,1)S(1)} %pad_maximum_fusion.1), channel_id=1, source_target_pairs={{24,0},{32,8},{40,16},{48,24},{56,32},{64,40},{72,48},{80,56},{88,... | collective-permute-start | bytes 2359304 | tf_op jit(solution)/shard_map/ppermute | solution.py:17
  84.6 5.2 %copy-start.6 = (bf16[512,384]{1,0:T(8,128)(2,1)S(1)}, bf16[512,384]{1,0:T(8,128)(2,1)}, u32[]{:S(2)}) copy-start(bf16[512,384]{1,0:T(8,128)(2,1)} %param.15) | copy-start | bytes 1179652
  89.9 12.5 %copy-start.7 = (bf16[512,384]{1,0:T(8,128)(2,1)}, bf16[512,384]{1,0:T(8,128)(2,1)S(1)}, u32[]{:S(2)}) copy-start(bf16[512,384]{1,0:T(8,128)(2,1)S(1)} %get-tuple-element.389) | copy-start | bytes 1179652 | tf_op jit(solution)/shard_map/while
  105.2 3.4 %copy-start.1 = (f32[512,3584]{1,0:T(8,128)}, f32[512,3584]{1,0:T(8,128)S(1)}, u32[]{:S(2)}) copy-start(f32[512,3584]{1,0:T(8,128)S(1)} %get-tuple-element.352) | copy-start | bytes 22020100 | tf_op jit(solution)/shard_map/while
  105.2 3.8 %copy-start.3 = (bf16[3584,384]{1,0:T(8,128)(2,1)S(1)}, bf16[3584,384]{1,0:T(8,128)(2,1)}, u32[]{:S(2)}) copy-start(bf16[3584,384]{1,0:T(8,128)(2,1)} %get-tuple-element.391) | copy-start | bytes 8257540 | tf_op jit(solution)/shard_map/while
  111.3 5.8 %copy-start.2 = (f32[512,3584]{1,0:T(8,128)S(1)}, f32[512,3584]{1,0:T(8,128)}, u32[]{:S(2)}) copy-start(f32[512,3584]{1,0:T(8,128)} %copy-done.1) | copy-start | bytes 22020100 | tf_op jit(solution)/shard_map/while
  119.4 3.1 %copy-start.8 = (bf16[512,384]{1,0:T(8,128)(2,1)S(1)}, bf16[512,384]{1,0:T(8,128)(2,1)}, u32[]{:S(2)}) copy-start(bf16[512,384]{1,0:T(8,128)(2,1)} %copy-done.7) | copy-start | bytes 1179652 | tf_op jit(solution)/shard_map/while
  124.7 12.5 %copy-start.7 = (bf16[512,384]{1,0:T(8,128)(2,1)}, bf16[512,384]{1,0:T(8,128)(2,1)S(1)}, u32[]{:S(2)}) copy-start(bf16[512,384]{1,0:T(8,128)(2,1)S(1)} %get-tuple-element.389) | copy-start | bytes 1179652 | tf_op jit(solution)/shard_map/while
  140.0 3.4 %copy-start.1 = (f32[512,3584]{1,0:T(8,128)}, f32[512,3584]{1,0:T(8,128)S(1)}, u32[]{:S(2)}) copy-start(f32[512,3584]{1,0:T(8,128)S(1)} %get-tuple-element.352) | copy-start | bytes 22020100 | tf_op jit(solution)/shard_map/while
  140.0 3.8 %copy-start.3 = (bf16[3584,384]{1,0:T(8,128)(2,1)S(1)}, bf16[3584,384]{1,0:T(8,128)(2,1)}, u32[]{:S(2)}) copy-start(bf16[3584,384]{1,0:T(8,128)(2,1)} %get-tuple-element.391) | copy-start | bytes 8257540 | tf_op jit(solution)/shard_map/while
  146.0 5.8 %copy-start.2 = (f32[512,3584]{1,0:T(8,128)S(1)}, f32[512,3584]{1,0:T(8,128)}, u32[]{:S(2)}) copy-start(f32[512,3584]{1,0:T(8,128)} %copy-done.1) | copy-start | bytes 22020100 | tf_op jit(solution)/shard_map/while
  154.1 3.1 %copy-start.8 = (bf16[512,384]{1,0:T(8,128)(2,1)S(1)}, bf16[512,384]{1,0:T(8,128)(2,1)}, u32[]{:S(2)}) copy-start(bf16[512,384]{1,0:T(8,128)(2,1)} %copy-done.7) | copy-start | bytes 1179652 | tf_op jit(solution)/shard_map/while
  159.4 12.5 %copy-start.7 = (bf16[512,384]{1,0:T(8,128)(2,1)}, bf16[512,384]{1,0:T(8,128)(2,1)S(1)}, u32[]{:S(2)}) copy-start(bf16[512,384]{1,0:T(8,128)(2,1)S(1)} %get-tuple-element.389) | copy-start | bytes 1179652 | tf_op jit(solution)/shard_map/while
  174.7 3.4 %copy-start.1 = (f32[512,3584]{1,0:T(8,128)}, f32[512,3584]{1,0:T(8,128)S(1)}, u32[]{:S(2)}) copy-start(f32[512,3584]{1,0:T(8,128)S(1)} %get-tuple-element.352) | copy-start | bytes 22020100 | tf_op jit(solution)/shard_map/while
  174.7 3.8 %copy-start.3 = (bf16[3584,384]{1,0:T(8,128)(2,1)S(1)}, bf16[3584,384]{1,0:T(8,128)(2,1)}, u32[]{:S(2)}) copy-start(bf16[3584,384]{1,0:T(8,128)(2,1)} %get-tuple-element.391) | copy-start | bytes 8257540 | tf_op jit(solution)/shard_map/while
  180.8 5.7 %copy-start.2 = (f32[512,3584]{1,0:T(8,128)S(1)}, f32[512,3584]{1,0:T(8,128)}, u32[]{:S(2)}) copy-start(f32[512,3584]{1,0:T(8,128)} %copy-done.1) | copy-start | bytes 22020100 | tf_op jit(solution)/shard_map/while
  188.9 3.1 %copy-start.8 = (bf16[512,384]{1,0:T(8,128)(2,1)S(1)}, bf16[512,384]{1,0:T(8,128)(2,1)}, u32[]{:S(2)}) copy-start(bf16[512,384]{1,0:T(8,128)(2,1)} %copy-done.7) | copy-start | bytes 1179652 | tf_op jit(solution)/shard_map/while
  194.1 34.9 %copy-start.9 = (f32[512,384]{1,0:T(8,128)S(1)}, f32[512,384]{1,0:T(8,128)}, u32[]{:S(2)}) copy-start(f32[512,384]{1,0:T(8,128)} %get-tuple-element.177) | copy-start | bytes 2359300
  194.1 34.9 %copy-start.10 = (bf16[512,384]{1,0:T(8,128)(2,1)S(1)}, bf16[512,384]{1,0:T(8,128)(2,1)}, u32[]{:S(2)}) copy-start(bf16[512,384]{1,0:T(8,128)(2,1)} %param.9) | copy-start | bytes 1179652
  194.1 34.9 %copy-start.13 = (f32[384]{0:T(512)S(1)}, f32[384]{0:T(512)}, u32[]{:S(2)}) copy-start(f32[384]{0:T(512)} %param.12) | copy-start | bytes 4612
  194.1 63.7 %copy-start.4 = (bf16[3584,384]{1,0:T(8,128)(2,1)S(1)}, bf16[3584,384]{1,0:T(8,128)(2,1)}, u32[]{:S(2)}) copy-start(bf16[3584,384]{1,0:T(8,128)(2,1)} %get-tuple-element.179) | copy-start | bytes 8257540
  194.1 63.7 %copy-start.5 = (bf16[3584,384]{1,0:T(8,128)(2,1)S(1)}, bf16[3584,384]{1,0:T(8,128)(2,1)}, u32[]{:S(2)}) copy-start(bf16[3584,384]{1,0:T(8,128)(2,1)} %get-tuple-element.178) | copy-start | bytes 8257540
  197.0 21.3 %collective-permute-start.6 = (bf16[2,512,384]{2,1,0:T(8,128)(2,1)S(1)}, bf16[2,512,384]{2,1,0:T(8,128)(2,1)S(1)}, u32[]{:S(2)}, u32[]{:S(2)}) collective-permute-start(bf16[2,512,384]{2,1,0:T(8,128)(2,1)S(1)} %get-tuple-element.273), channel_id=1, source_target_pairs={{24,0},{32,8},{40,16},{48,24},{56,32},{64,40},{72,48},{80,56},{88,... | collective-permute-start | bytes 2359304 | tf_op jit(solution)/shard_map/ppermute | solution.py:17
  203.3 37.2 %collective-permute-start.7 = (bf16[2,512,384]{2,1,0:T(8,128)(2,1)S(1)}, bf16[2,512,384]{2,1,0:T(8,128)(2,1)S(1)}, u32[]{:S(2)}, u32[]{:S(2)}) collective-permute-start(bf16[2,512,384]{2,1,0:T(8,128)(2,1)S(1)} %get-tuple-element.274), channel_id=1, source_target_pairs={{16,0},{24,8},{32,16},{40,24},{48,32},{56,40},{64,48},{72,56},{80,... | collective-permute-start | bytes 2359304 | tf_op jit(solution)/shard_map/ppermute | solution.py:17
  206.8 48.4 %collective-permute-start.8 = (bf16[2,512,384]{2,1,0:T(8,128)(2,1)S(1)}, bf16[2,512,384]{2,1,0:T(8,128)(2,1)S(1)}, u32[]{:S(2)}, u32[]{:S(2)}) collective-permute-start(bf16[2,512,384]{2,1,0:T(8,128)(2,1)S(1)} %get-tuple-element.275), channel_id=1, source_target_pairs={{8,0},{16,8},{24,16},{32,24},{40,32},{48,40},{56,48},{64,56},{72,6... | collective-permute-start | bytes 2359304 | tf_op jit(solution)/shard_map/ppermute | solution.py:17
  208.7 46.5 %collective-permute-start.9 = (bf16[2,512,384]{2,1,0:T(8,128)(2,1)S(1)}, bf16[2,512,384]{2,1,0:T(8,128)(2,1)S(1)}, u32[]{:S(2)}, u32[]{:S(2)}) collective-permute-start(bf16[2,512,384]{2,1,0:T(8,128)(2,1)S(1)} %get-tuple-element.276), channel_id=1, source_target_pairs={{0,8},{8,16},{16,24},{24,32},{32,40},{40,48},{48,56},{56,64},{64,7... | collective-permute-start | bytes 2359304 | tf_op jit(solution)/shard_map/ppermute | solution.py:17
  211.1 44.0 %collective-permute-start.11 = (bf16[2,512,384]{2,1,0:T(8,128)(2,1)S(1)}, bf16[2,512,384]{2,1,0:T(8,128)(2,1)S(1)}, u32[]{:S(2)}, u32[]{:S(2)}) collective-permute-start(bf16[2,512,384]{2,1,0:T(8,128)(2,1)S(1)} %get-tuple-element.277), channel_id=1, source_target_pairs={{0,24},{8,32},{16,40},{24,48},{32,56},{40,64},{48,72},{56,80},{64,... | collective-permute-start | bytes 2359304 | tf_op jit(solution)/shard_map/ppermute | solution.py:17
  218.3 39.5 %collective-permute-start.10 = (bf16[2,512,384]{2,1,0:T(8,128)(2,1)S(1)}, bf16[2,512,384]{2,1,0:T(8,128)(2,1)S(1)}, u32[]{:S(2)}, u32[]{:S(2)}) collective-permute-start(bf16[2,512,384]{2,1,0:T(8,128)(2,1)S(1)} %get-tuple-element.278), channel_id=1, source_target_pairs={{0,16},{8,24},{16,32},{24,40},{32,48},{40,56},{48,64},{56,72},{64,... | collective-permute-start | bytes 2359304 | tf_op jit(solution)/shard_map/ppermute | solution.py:17
  229.2 29.3 %copy-start.11 = (bf16[512,384]{1,0:T(8,128)(2,1)S(1)}, bf16[512,384]{1,0:T(8,128)(2,1)}, u32[]{:S(2)}) copy-start(bf16[512,384]{1,0:T(8,128)(2,1)} %param.10) | copy-start | bytes 1179652
  229.2 29.3 %copy-start.14 = (f32[384]{0:T(512)S(1)}, f32[384]{0:T(512)}, u32[]{:S(2)}) copy-start(f32[384]{0:T(512)} %param.13) | copy-start | bytes 4612
where the time goes:
time: 279 us; the launch traced here: 276 us
  waiting for transfers between devices  62.9 us (23%)
  local copies, waits for them, and re-layouts  62.7 us (22%)
  matrix products  52.7 us (19%)
  starting transfers between devices  46.7 us (17%)
  blocking collectives  34.1 us (12%)
  other arithmetic  15.3 us (5%)
    ppermute x12, waiting for transfers between devices, shifted(): lax.ppermute(value, axis, [(source, source + steps) for source in range(i...  62.9 us
    ppermute x12, starting transfers between devices, shifted(): lax.ppermute(value, axis, [(source, source + steps) for source in range(i...  46.7 us
    psum x1, blocking collectives, local(): lax.psum((jnp.sum(query_float * query_float, axis=1), jnp.sum(key_float *...  20 us
    reshape x3, local copies, waits for them, and re-layouts, expand_live(): expanded = expanded.reshape(band_size, blocks * BLK, blocks * BLK)  18.3 us
    dot_general x3, matrix products, one_head(): jnp.einsum('qk,qd->kd', weights_low, grad_part, preferred_element_type=jn...  17.2 us
    psum x1, blocking collectives, local(): lax.psum((jnp.sum(query_float * query_gain * grad_qnorm, axis=1), jnp.sum...  14.1 us
    dot_general x3, matrix products, one_head(): jnp.dot(grad_scores, key_part, preferred_element_type=jnp.float32)  9.23 us
    dot_general x3, matrix products, masked_scores(): jnp.einsum('qd,kd->qk', query_part, key_part, preferred_element_type=jnp....  8.37 us
  transfers between devices with their start and end apart: 12, of which 8 were waited for; matrix products, arithmetic and copies ran while one was open for 3% of the time, Pallas kernels for 0%

commit v1 on v0

v1 whole, which is shorter than its diff:
```python
import functools
import jax, jax.numpy as jnp
from jax import lax
from jax.sharding import PartitionSpec as P
from jax.experimental import pallas as pl
from jax.experimental.pallas import tpu as pltpu

LOG2E = 1.4426950408889634
LN2 = 0.6931471805599453
SCALE = 128 ** -0.5
NEG = -1e30
BLK = 128
FT = 512
SLOTS = 7
KEYS = SLOTS * FT


def head_kernel(bias_ref, rate_ref, gain_ref, *refs):
    key_refs = refs[:SLOTS]
    value_refs = refs[SLOTS:2 * SLOTS]
    q_ref, g_ref, att_ref, gq_ref = refs[2 * SLOTS:2 * SLOTS + 4]
    term_refs = refs[2 * SLOTS + 4:4 * SLOTS + 4]
    kb, kt, vb, st = refs[4 * SLOTS + 4:]
    f32, bf = jnp.float32, jnp.bfloat16
    q = q_ref[...]
    g = g_ref[...]
    qt = q.T
    gt = g.T

    def fold(x, op):
        return op(x.reshape(-1, 8, FT), axis=0)

    m8 = jnp.full((8, FT), NEG, f32)
    for s in range(SLOTS):
        cols = slice(s * FT, (s + 1) * FT)
        normed = (key_refs[s][...].T.astype(f32) * rate_ref[s:s + 1, :] * gain_ref[...]).astype(bf)
        kb[cols, :] = normed.T
        vb[cols, :] = value_refs[s][...]
    for lo, hi in [(0, 2), (2, 4), (4, 6), (6, 7)]:
        cols = slice(lo * FT, hi * FT)
        x = jnp.dot(kb[cols, :], qt, preferred_element_type=f32)
        for b in range(4 * (hi - lo)):
            y = x[b * BLK:(b + 1) * BLK] + bias_ref[4 * lo + b:4 * lo + b + 1, :]
            st[lo * FT + b * BLK:lo * FT + (b + 1) * BLK, :] = y
            m8 = jnp.maximum(m8, fold(y, jnp.max))
    top = jnp.max(m8, axis=0, keepdims=True)

    l8 = jnp.zeros((8, FT), f32)
    ot = jnp.zeros((BLK, FT), f32)
    for lo, hi in [(0, 2), (2, 4), (4, 6), (6, 7)]:
        cols = slice(lo * FT, hi * FT)
        e = jnp.exp2(st[cols, :] - top)
        l8 = l8 + fold(e, jnp.sum)
        ot = ot + lax.dot_general(vb[cols, :], e.astype(bf), (((0,), (0,)), ((), ())), preferred_element_type=f32)
    total = jnp.sum(l8, axis=0, keepdims=True)
    lse = top + jnp.log2(total)
    att = (ot / total).astype(bf)
    delta = jnp.sum(gt.astype(f32) * att.astype(f32), axis=0, keepdims=True)
    att_ref[...] = att.T

    dqt = jnp.zeros((BLK, FT), f32)
    for lo, hi in [(0, 2), (2, 4), (4, 6), (6, 7)]:
        cols = slice(lo * FT, hi * FT)
        w = jnp.exp2(st[cols, :] - lse)
        gw = jnp.dot(vb[cols, :], gt, preferred_element_type=f32)
        ds = (w * (gw - delta)).astype(bf)
        dqt = dqt + lax.dot_general(kb[cols, :], ds, (((0,), (0,)), ((), ())), preferred_element_type=f32)
        dk = (jnp.dot(ds, q, preferred_element_type=f32) * LN2).astype(bf)
        dv = jnp.dot(w.astype(bf), g, preferred_element_type=f32).astype(bf)
        for s in range(lo, hi):
            part = slice((s - lo) * FT, (s - lo + 1) * FT)
            term_refs[s][...] = dk[part]
            term_refs[SLOTS + s][...] = dv[part]
    gq_ref[...] = dqt.T * SCALE


def square_kernel(*refs):
    out_ref = refs[-1]
    ones = jnp.ones((8, refs[0].shape[1]), jnp.bfloat16)
    contract = (((1,), (1,)), ((), ()))
    for i, ref in enumerate(refs[:-1]):
        x = ref[...].astype(jnp.float32)
        square = x * x
        high = square.astype(jnp.bfloat16)
        low = (square - high.astype(jnp.float32)).astype(jnp.bfloat16)
        total = lax.dot_general(ones, high, contract, preferred_element_type=jnp.float32)
        total = total + lax.dot_general(ones, low, contract, preferred_element_type=jnp.float32)
        out_ref[i:i + 1, :] = total[0:1, :]


def square_call(parts):
    return pl.pallas_call(
        square_kernel,
        out_shape=jax.ShapeDtypeStruct((len(parts), FT), jnp.float32),
        compiler_params=pltpu.CompilerParams(vmem_limit_bytes=32 * 1024 * 1024),
        name="row_squares",
        cost_estimate=pl.CostEstimate(flops=10**9, bytes_accessed=4 * 10**6, transcendentals=0),
    )(*parts)


def head_call(bias, rates, gain, keys, values, query, grad):
    vm = pltpu.VMEM
    bf, f32 = jnp.bfloat16, jnp.float32
    width = query.shape[1]
    rows = pl.BlockSpec((FT, BLK), lambda i: (0, i))
    return pl.pallas_call(
        head_kernel,
        grid=(width // BLK,),
        in_specs=[
            pl.BlockSpec((4 * SLOTS, FT), lambda i: (0, 0)),
            pl.BlockSpec((8, FT), lambda i: (0, 0)),
            pl.BlockSpec((BLK, 1), lambda i: (i, 0)),
        ]
        + [rows] * (2 * SLOTS + 2),
        out_specs=[rows] * (2 + 2 * SLOTS),
        out_shape=[jax.ShapeDtypeStruct((FT, width), bf), jax.ShapeDtypeStruct((FT, width), f32)]
        + [jax.ShapeDtypeStruct((FT, width), bf)] * (2 * SLOTS),
        scratch_shapes=[
            vm((KEYS, BLK), bf),
            vm((BLK, KEYS), bf),
            vm((KEYS, BLK), bf),
            vm((KEYS, FT), f32),
        ],
        compiler_params=pltpu.CompilerParams(vmem_limit_bytes=56 * 1024 * 1024),
        name="head_attention",
        cost_estimate=pl.CostEstimate(flops=9 * 10**9, bytes_accessed=12 * 10**6, transcendentals=12 * 10**6),
    )(bias, rates, gain, *keys, *values, query, grad)


epsilon = 1e-06


def shifted(value, steps):
    count = lax.axis_size("tm")
    return lax.ppermute(value, "tm", [(s, s + steps) for s in range(max(0, -steps), min(count, count - steps))])


def turned(value, steps):
    count = lax.axis_size("head")
    return lax.ppermute(value, "head", [(s, (s + steps) % count) for s in range(count)])


def ring_sum(value):
    after, before = turned(value, -1), turned(value, 1)
    pair = value + after
    return pair + before + turned(pair + before, -3) + turned(pair, 3)


def swapped(value):
    return lax.ppermute(value, "tm", [(s, s ^ 1) for s in range(lax.axis_size("tm"))])


def outward(value, steps):
    count = lax.axis_size("tm")
    pairs = [(s, s + steps) if s % 2 else (s, s - steps) for s in range(count)]
    return lax.ppermute(value, "tm", [(a, b) for a, b in pairs if 0 <= b < count])


def band(value, odd):
    ahead, behind = shifted(value, -2), shifted(value, 2)
    beside = swapped(value)
    outer = outward(jnp.where(odd, behind, ahead), 1)
    return [value, ahead, behind, beside, swapped(ahead), swapped(behind), outer]


def returned(terms):
    f32 = jnp.float32
    outer = outward(terms[6], 3)
    ahead = (terms[1].astype(f32) + swapped(terms[4]).astype(f32)).astype(jnp.bfloat16)
    behind = (terms[2].astype(f32) + swapped(terms[5]).astype(f32)).astype(jnp.bfloat16)
    beside = swapped(terms[3])
    return [terms[0], beside, outer, shifted(ahead, 2), shifted(behind, -2)]


def summed(parts):
    total = parts[0].astype(jnp.float32)
    for part in parts[1:]:
        total = total + part.astype(jnp.float32)
    return total


def local(queries, key_rows, value_rows, query_gain, key_gain, block_mask, out_grad):
    frame = lax.axis_index("tm")
    frame_count = lax.axis_size("tm")
    odd = frame % 2 == 1
    full_width = queries.shape[1] * lax.axis_size("head")
    keys = band(key_rows, odd)
    values = band(value_rows, odd)

    offsets = jnp.where(odd, jnp.array([0, 2, -2, -1, 1, -3, 3]), jnp.array([0, 2, -2, 1, 3, -1, -3]))
    mask_rows = lax.dynamic_index_in_dim(block_mask, frame, 0, keepdims=False)
    is_valid = (frame + offsets >= 0) & (frame + offsets < frame_count)
    live = jnp.where(is_valid[:, None, None], mask_rows[offsets + 3], 0)
    bias = jnp.where(jnp.swapaxes(live, 1, 2) > 0, 0.0, NEG).reshape(SLOTS * live.shape[2], live.shape[1])
    bias = jnp.repeat(bias, BLK, axis=1)

    query_float = queries.astype(jnp.float32)
    key_float = key_rows.astype(jnp.float32)
    rates = lax.rsqrt(ring_sum(square_call(keys + [queries])) / full_width + epsilon)
    query_rate = rates[SLOTS][:, None]
    key_rate = rates[0][:, None]
    query_scaled = (query_float * query_rate * query_gain * (SCALE * LOG2E)).astype(jnp.bfloat16)

    out = head_call(bias, rates, key_gain[:, None], keys, values, query_scaled, out_grad)
    attended, grad_qnorm = out[:2]
    key_parts = returned(out[2:2 + SLOTS])
    value_parts = returned(out[2 + SLOTS:])
    grad_knorm = summed(key_parts)
    value_sum = summed(value_parts)
    dots = jnp.stack(
        [
            jnp.sum(query_float * query_gain * grad_qnorm, axis=1),
            jnp.sum(key_float * key_gain * grad_knorm, axis=1),
        ]
    )
    query_dot, key_dot = ring_sum(dots)
    query_grad = (
        query_rate * query_gain * grad_qnorm
        - query_float * query_rate**3 * query_dot[:, None] / full_width
    )
    key_grad = (
        key_rate * key_gain * grad_knorm - key_float * key_rate**3 * key_dot[:, None] / full_width
    )
    return (
        attended,
        query_grad.astype(jnp.bfloat16),
        key_grad.astype(jnp.bfloat16),
        value_sum.astype(jnp.bfloat16),
    )


def solution(mesh):
    return jax.shard_map(
        local,
        mesh=mesh,
        in_specs=(
            P("tm", "head"),
            P("tm", "head"),
            P("tm", "head"),
            P("head"),
            P("head"),
            P(),
            P("tm", "head"),
        ),
        out_specs=(P("tm", "head"), P("tm", "head"), P("tm", "head"), P("tm", "head")),
        check_vma=False,
    )
```

time: 279 us -> 141 us (0.51)
  local copies, waits for them, and re-layouts: 62.7 us -> 5.99 us
  matrix products: 52.7 us -> 0 us
  blocking collectives: 34.1 us -> 0 us
  Pallas kernels: 0 us -> 25.1 us
  waiting for transfers between devices: 62.9 us -> 41.9 us
  starting transfers between devices: 46.7 us -> 58.1 us
  other arithmetic: 15.3 us -> 7.59 us
    dot_general x18 -> x0, matrix products: 52.7 us -> none  [the longest x3 17.2 us: one_head(): jnp.einsum('qk,qd->kd', weights_low, grad_part, preferred_element_type=jn...]
    psum x2 -> x0, blocking collectives: 34.1 us -> none  [the longest x1 20 us: local(): lax.psum((jnp.sum(query_float * query_float, axis=1), jnp.sum(key_float *...]
    pallas_call x0 -> x2, Pallas kernels: none -> 25.1 us  [the longest x1 23.3 us: head_call(): pl.pallas_call(head_kernel, grid=(width // BLK,), in_specs=[pl.BlockSpec(...]
    reshape x6 -> x2, local copies, waits for them, and re-layouts: 24.4 us -> 0.14 us  [local(): jnp.where(jnp.swapaxes(live, 1, 2) > 0, 0.0, NEG)]
    ppermute x12 -> x32, waiting for transfers between devices: 62.9 us -> 41.9 us  [the longest x8 17.7 us: shifted(): lax.ppermute(value, 'tm', [(s, s + steps) for s in range(max(0, -steps),...]
    ppermute x12 -> x32, starting transfers between devices: 46.7 us -> 58.1 us  [the longest x8 31 us: shifted(): lax.ppermute(value, 'tm', [(s, s + steps) for s in range(max(0, -steps),...]
    while x30 -> x0, local copies, waits for them, and re-layouts: 8.07 us -> none
    broadcast_in_dim x5 -> x2, local copies, waits for them, and re-layouts: 8.45 us -> 0.88 us  [the longest x1 0.78 us: local(): key_gain[:, None]]
  transfers between devices with their start and end apart: 12 -> 32, of which waited for: 8 -> 10; matrix products, arithmetic and copies ran while one was open for 3% -> 6% of each run, Pallas kernels for 0% -> 1%
where the time goes in v1:
time: 141 us; the launch traced here: 140 us
  starting transfers between devices  58.1 us (41%)
  waiting for transfers between devices  41.9 us (30%)
  Pallas kernels  25.1 us (18%)
  other arithmetic  7.59 us (5%)
  local copies, waits for them, and re-layouts  5.99 us (4%)
    ppermute x8, starting transfers between devices, shifted(): lax.ppermute(value, 'tm', [(s, s + steps) for s in range(max(0, -steps),...  31 us
    pallas_call x1, Pallas kernels, head_call(): pl.pallas_call(head_kernel, grid=(width // BLK,), in_specs=[pl.BlockSpec(...  23.3 us
    ppermute x8, waiting for transfers between devices, shifted(): lax.ppermute(value, 'tm', [(s, s + steps) for s in range(max(0, -steps),...  17.7 us
    ppermute x8, starting transfers between devices, turned(): lax.ppermute(value, 'head', [(s, (s + steps) % count) for s in range(coun...  16 us
    ppermute x4, waiting for transfers between devices, outward(): lax.ppermute(value, 'tm', [(a, b) for a, b in pairs if 0 <= b < count])  15 us
    ppermute x8, waiting for transfers between devices, turned(): lax.ppermute(value, 'head', [(s, (s + steps) % count) for s in range(coun...  9.19 us
    ppermute x4, starting transfers between devices, outward(): lax.ppermute(value, 'tm', [(a, b) for a, b in pairs if 0 <= b < count])  8.21 us
    unnamed x56, local copies, waits for them, and re-layouts  4.02 us
  transfers between devices with their start and end apart: 32, of which 10 were waited for; matrix products, arithmetic and copies ran while one was open for 6% of the time, Pallas kernels for 1%

profile of v1, /device:TPU:8, one launch (start us, length us, event | category | flops | bytes accessed | tf_op | source)
XLA Modules:
  0.0 139.9 jit_solution(12181890963723970860)
XLA Ops:
  0.6 4.7 %collective-permute-start = (bf16[512,384]{1,0:T(8,128)(2,1)}, bf16[512,384]{1,0:T(8,128)(2,1)S(1)}, u32[]{:S(2)}, u32[]{:S(2)}) collective-permute-start(bf16[512,384]{1,0:T(8,128)(2,1)} %refs_0_.3), channel_id=1, source_target_pairs={{16,0},{24,8},{32,16},{40,24},{48,32},{56,40},{64,48},{72,56},{80,... | collective-permute-start | bytes 1179656 | tf_op jit(solution)/shard_map/ppermute | solution.py:135
  5.3 1.9 %collective-permute-start.1 = (bf16[512,384]{1,0:T(8,128)(2,1)}, bf16[512,384]{1,0:T(8,128)(2,1)S(1)}, u32[]{:S(2)}, u32[]{:S(2)}) collective-permute-start(bf16[512,384]{1,0:T(8,128)(2,1)} %refs_0_.3), channel_id=1, source_target_pairs={{0,16},{8,24},{16,32},{24,40},{32,48},{40,56},{48,64},{56,72},{64,... | collective-permute-start | bytes 1179656 | tf_op jit(solution)/shard_map/ppermute | solution.py:135
  7.4 6.0 %collective-permute-start.10 = (bf16[512,384]{1,0:T(8,128)(2,1)}, bf16[512,384]{1,0:T(8,128)(2,1)}, u32[]{:S(2)}, u32[]{:S(2)}) collective-permute-start(bf16[512,384]{1,0:T(8,128)(2,1)} %refs_7_.3), channel_id=1, source_target_pairs={{16,0},{24,8},{32,16},{40,24},{48,32},{56,40},{64,48},{72,56},{80,... | collective-permute-start | bytes 1179656 | tf_op jit(solution)/shard_map/ppermute | solution.py:135
  13.5 0.6 copy-done.19
  14.1 0.8 collective-permute-done.refs_1_
  14.9 5.2 %collective-permute-done.1.refs_2_ = bf16[512,384]{1,0:T(8,128)(2,1)S(1)} collective-permute-done((bf16[512,384]{1,0:T(8,128)(2,1)}, bf16[512,384]{1,0:T(8,128)(2,1)S(1)}, u32[]{:S(2)}, u32[]{:S(2)}) %collective-permute-start.1) | collective-permute-done | bytes 393248 | tf_op jit(solution)/shard_map/ppermute | solution.py:135
  20.1 0.8 broadcast_select_fusion.1
  21.0 1.9 %collective-permute-start.5 = (bf16[512,384]{1,0:T(8,128)(2,1)}, bf16[512,384]{1,0:T(8,128)(2,1)S(1)}, u32[]{:S(2)}, u32[]{:S(2)}) collective-permute-start(bf16[512,384]{1,0:T(8,128)(2,1)} %broadcast_select_fusion.1), channel_id=1, source_target_pairs={{8,16},{16,8},{24,32},{32,24},{40,48},{48,40},{56,64},{64,56},{72,... | collective-permute-start | bytes 1179656 | tf_op jit(solution)/shard_map/ppermute | solution.py:156
  23.0 0.5 collective-permute-start.4
  23.9 0.6 gather_fusion
  24.5 2.2 %collective-permute-start.11 = (bf16[512,384]{1,0:T(8,128)(2,1)}, bf16[512,384]{1,0:T(8,128)(2,1)}, u32[]{:S(2)}, u32[]{:S(2)}) collective-permute-start(bf16[512,384]{1,0:T(8,128)(2,1)} %refs_7_.3), channel_id=1, source_target_pairs={{0,16},{8,24},{16,32},{24,40},{32,48},{40,56},{48,64},{56,72},{64,... | collective-permute-start | bytes 1179656 | tf_op jit(solution)/shard_map/ppermute | solution.py:135
  26.7 5.8 %collective-permute-done.5.refs_6_ = bf16[512,384]{1,0:T(8,128)(2,1)S(1)} collective-permute-done((bf16[512,384]{1,0:T(8,128)(2,1)}, bf16[512,384]{1,0:T(8,128)(2,1)S(1)}, u32[]{:S(2)}, u32[]{:S(2)}) %collective-permute-start.5) | collective-permute-done | bytes 393248 | tf_op jit(solution)/shard_map/ppermute | solution.py:156
  32.5 1.8 %row_squares.1 = f32[8,512]{1,0:T(8,128)S(1)} custom-call(bf16[512,384]{1,0:T(8,128)(2,1)S(1)} %copy-done.2, bf16[512,384]{1,0:T(8,128)(2,1)S(1)} %collective-permute-done.refs_1_, bf16[512,384]{1,0:T(8,128)(2,1)S(1)} %collective-permute-done.1.refs_2_, bf16[512,384]{1,0:T(8,128)(2,1)S(1)} %collective-permute-done.2.refs_3_, ...), custom_call_target="tpu_custom_call" | custom-call | flops 1000000000 | bytes 4000000 | tf_op jit(solution)/shard_map/row_squares/pallas_call | solution.py:92
  34.3 5.9 %collective-permute-start.6 = (f32[8,512]{1,0:T(8,128)S(1)}, f32[8,512]{1,0:T(8,128)S(1)}, u32[]{:S(2)}, u32[]{:S(2)}) collective-permute-start(f32[8,512]{1,0:T(8,128)S(1)} %row_squares.1), channel_id=1, source_target_pairs={{0,7},{1,0},{2,1},{3,2},{4,3},{5,4},{6,5},{7,6},{8,15},{9,8},{10,9... | collective-permute-start | bytes 49160 | tf_op jit(solution)/shard_map/ppermute | solution.py:140
  40.6 0.6 copy.24
  41.3 0.8 broadcast_in_dim.42.gain_ref
  42.1 3.1 %collective-permute-done.7 = f32[8,512]{1,0:T(8,128)S(1)} collective-permute-done((f32[8,512]{1,0:T(8,128)S(1)}, f32[8,512]{1,0:T(8,128)S(1)}, u32[]{:S(2)}, u32[]{:S(2)}) %collective-permute-start.7) | collective-permute-done | bytes 16416 | tf_op jit(solution)/shard_map/ppermute | solution.py:140
  45.2 0.7 collective-permute-start.8
  45.9 3.1 %collective-permute-start.9 = (f32[8,512]{1,0:T(8,128)S(1)}, f32[8,512]{1,0:T(8,128)S(1)}, u32[]{:S(2)}, u32[]{:S(2)}) collective-permute-start(f32[8,512]{1,0:T(8,128)S(1)} %get-tuple-element.39), channel_id=1, source_target_pairs={{0,3},{1,4},{2,5},{3,6},{4,7},{5,0},{6,1},{7,2},{8,11},{9,12},{10,... | collective-permute-start | bytes 49160 | tf_op jit(solution)/shard_map/ppermute | solution.py:140
  49.1 1.1 broadcast_select_fusion
  50.1 1.9 %collective-permute-start.15 = (bf16[512,384]{1,0:T(8,128)(2,1)S(1)}, bf16[512,384]{1,0:T(8,128)(2,1)S(1)}, u32[]{:S(2)}, u32[]{:S(2)}) collective-permute-start(bf16[512,384]{1,0:T(8,128)(2,1)S(1)} %broadcast_select_fusion), channel_id=1, source_target_pairs={{8,16},{16,8},{24,32},{32,24},{40,48},{48,40},{56,64},{64,56},{72,... | collective-permute-start | bytes 1179656 | tf_op jit(solution)/shard_map/ppermute | solution.py:156
  52.1 0.5 collective-permute-start.14
  52.7 0.7 copy-done.18
  53.4 0.9 fusion.8.refs_14_
  54.3 7.0 %collective-permute-done.15.refs_13_ = bf16[512,384]{1,0:T(8,128)(2,1)S(1)} collective-permute-done((bf16[512,384]{1,0:T(8,128)(2,1)S(1)}, bf16[512,384]{1,0:T(8,128)(2,1)S(1)}, u32[]{:S(2)}, u32[]{:S(2)}) %collective-permute-start.15) | collective-permute-done | bytes 393248 | tf_op jit(solution)/shard_map/ppermute | solution.py:156
  61.3 0.7 copy-done.24
  62.3 23.3 %head_attention.1 = (bf16[512,384]{1,0:T(8,128)(2,1)}, f32[512,384]{1,0:T(8,128)}, bf16[512,384]{1,0:T(8,128)(2,1)}, bf16[512,384]{1,0:T(8,128)(2,1)}, bf16[512,...) custom-call(f32[28,512]{1,0:T(8,128)} %bitcast.14, ...), custom_call_target="tpu_custom_call" | custom-call | flops 8999999488 | bytes 12000000 | tf_op jit(solution)/shard_map/head_attention/pallas_call | solution.py:106
  85.8 0.5 collective-permute-start.28
  86.8 1.9 %collective-permute-start.17 = (bf16[512,384]{1,0:T(8,128)(2,1)}, bf16[512,384]{1,0:T(8,128)(2,1)S(1)}, u32[]{:S(2)}, u32[]{:S(2)}) collective-permute-start(bf16[512,384]{1,0:T(8,128)(2,1)} %get-tuple-element.24), channel_id=1, source_target_pairs={{8,32},{24,48},{32,8},{40,64},{48,24},{56,80},{64,40},{72,96},{80,... | collective-permute-start | bytes 1179656 | tf_op jit(solution)/shard_map/ppermute | solution.py:156
  88.7 1.1 add_convert_fusion.4
  89.9 2.9 %collective-permute-start.19 = (bf16[512,384]{1,0:T(8,128)(2,1)S(1)}, bf16[512,384]{1,0:T(8,128)(2,1)S(1)}, u32[]{:S(2)}, u32[]{:S(2)}) collective-permute-start(bf16[512,384]{1,0:T(8,128)(2,1)S(1)} %add_convert_fusion.4), channel_id=1, source_target_pairs={{0,16},{8,24},{16,32},{24,40},{32,48},{40,56},{48,64},{56,72},{64,... | collective-permute-start | bytes 1179656 | tf_op jit(solution)/shard_map/ppermute | solution.py:135
  92.9 5.2 %collective-permute-start.21 = (bf16[512,384]{1,0:T(8,128)(2,1)S(1)}, bf16[512,384]{1,0:T(8,128)(2,1)S(1)}, u32[]{:S(2)}, u32[]{:S(2)}) collective-permute-start(bf16[512,384]{1,0:T(8,128)(2,1)S(1)} %add_convert_fusion.3), channel_id=1, source_target_pairs={{16,0},{24,8},{32,16},{40,24},{48,32},{56,40},{64,48},{72,56},{80,... | collective-permute-start | bytes 1179656 | tf_op jit(solution)/shard_map/ppermute | solution.py:135
  98.3 0.8 copy-done.23
  99.4 0.5 collective-permute-start.26
  99.8 2.2 %collective-permute-done.17 = bf16[512,384]{1,0:T(8,128)(2,1)S(1)} collective-permute-done((bf16[512,384]{1,0:T(8,128)(2,1)}, bf16[512,384]{1,0:T(8,128)(2,1)S(1)}, u32[]{:S(2)}, u32[]{:S(2)}) %collective-permute-start.17) | collective-permute-done | bytes 393248 | tf_op jit(solution)/shard_map/ppermute | solution.py:156
  102.1 2.5 %collective-permute-start.27 = (bf16[512,384]{1,0:T(8,128)(2,1)S(1)}, bf16[512,384]{1,0:T(8,128)(2,1)S(1)}, u32[]{:S(2)}, u32[]{:S(2)}) collective-permute-start(bf16[512,384]{1,0:T(8,128)(2,1)S(1)} %copy-done.21), channel_id=1, source_target_pairs={{8,32},{24,48},{32,8},{40,64},{48,24},{56,80},{64,40},{72,96},{80,... | collective-permute-start | bytes 1179656 | tf_op jit(solution)/shard_map/ppermute | solution.py:156
  104.6 11.7 %collective-permute-done.19 = bf16[512,384]{1,0:T(8,128)(2,1)S(1)} collective-permute-done((bf16[512,384]{1,0:T(8,128)(2,1)S(1)}, bf16[512,384]{1,0:T(8,128)(2,1)S(1)}, u32[]{:S(2)}, u32[]{:S(2)}) %collective-permute-start.19) | collective-permute-done | bytes 393248 | tf_op jit(solution)/shard_map/ppermute | solution.py:135
  116.2 1.9 %collective-permute-start.29 = (bf16[512,384]{1,0:T(8,128)(2,1)S(1)}, bf16[512,384]{1,0:T(8,128)(2,1)S(1)}, u32[]{:S(2)}, u32[]{:S(2)}) collective-permute-start(bf16[512,384]{1,0:T(8,128)(2,1)S(1)} %add_convert_fusion.2), channel_id=1, source_target_pairs={{0,16},{8,24},{16,32},{24,40},{32,48},{40,56},{48,64},{56,72},{64,... | collective-permute-start | bytes 1179656 | tf_op jit(solution)/shard_map/ppermute | solution.py:135
  118.2 0.4 fusion.1
  118.6 1.7 %collective-permute-start.22 = (f32[2,512]{1,0:T(2,128)S(1)}, f32[2,512]{1,0:T(2,128)S(1)}, u32[]{:S(2)}, u32[]{:S(2)}) collective-permute-start(f32[2,512]{1,0:T(2,128)S(1)} %pad_maximum_fusion), channel_id=1, source_target_pairs={{0,7},{1,0},{2,1},{3,2},{4,3},{5,4},{6,5},{7,6},{8,15},{9,8},{10,9... | collective-permute-start | bytes 12296 | tf_op jit(solution)/shard_map/ppermute | solution.py:140
  120.4 6.2 %collective-permute-start.31 = (bf16[512,384]{1,0:T(8,128)(2,1)S(1)}, bf16[512,384]{1,0:T(8,128)(2,1)S(1)}, u32[]{:S(2)}, u32[]{:S(2)}) collective-permute-start(bf16[512,384]{1,0:T(8,128)(2,1)S(1)} %add_convert_fusion.1), channel_id=1, source_target_pairs={{16,0},{24,8},{32,16},{40,24},{48,32},{56,40},{64,48},{72,56},{80,... | collective-permute-start | bytes 1179656 | tf_op jit(solution)/shard_map/ppermute | solution.py:135
  126.6 0.7 collective-permute-start.23
  127.3 4.2 %collective-permute-done.23 = f32[2,512]{1,0:T(2,128)S(1)} collective-permute-done((f32[2,512]{1,0:T(2,128)S(1)}, f32[2,512]{1,0:T(2,128)S(1)}, u32[]{:S(2)}, u32[]{:S(2)}) %collective-permute-start.23) | collective-permute-done | bytes 4128 | tf_op jit(solution)/shard_map/ppermute | solution.py:140
  131.6 3.8 %collective-permute-start.25 = (f32[2,512]{1,0:T(2,128)S(1)}, f32[2,512]{1,0:T(2,128)S(1)}, u32[]{:S(2)}, u32[]{:S(2)}) collective-permute-start(f32[2,512]{1,0:T(2,128)S(1)} %get-tuple-element.37), channel_id=1, source_target_pairs={{0,3},{1,4},{2,5},{3,6},{4,7},{5,0},{6,1},{7,2},{8,11},{9,12},{10,... | collective-permute-start | bytes 12296 | tf_op jit(solution)/shard_map/ppermute | solution.py:140
  135.4 1.0 add_convert_fusion
  136.4 0.6 collective-permute-done.24
  137.0 1.3 collective-permute-done.25
  138.3 1.6 %fusion.5 = (bf16[512,384]{1,0:T(8,128)(2,1)}, bf16[512,384]{1,0:T(8,128)(2,1)}) fusion(bf16[512,384]{1,0:T(8,128)(2,1)S(1)} %copy-done.3, f32[512]{0:T(512)S(1)} %bitcast.25, f32[512]{0:T(512)S(1)} %multiply_multiply_fusion, f32[512]{0:T(512)S(1)} %bitcast.24, f32[384]{0:T(512)S(1)} %copy-done.17, bf16[512,384]{1,0:T(8,128)(2,1)S(1)} %collective-permute-done.21, ...), kind=kLoop, calls=%fused_computation.11 | loop fusion | flops 4915200 | bytes 4340736 | tf_op jit(solution)/shard_map/convert_element_type | solution.py:227
  (105 shorter events, 2.9 us)
Async XLA Ops:
  0.6 22.9 %copy-start = (s32[32,7,4,4]{0,3,2,1:T(4,128)S(1)}, s32[32,7,4,4]{0,3,2,1:T(4,128)}, u32[]{:S(2)}) copy-start(s32[32,7,4,4]{0,3,2,1:T(4,128)} %param.14) | copy-start | bytes 43012
  0.6 14.2 %collective-permute-start = (bf16[512,384]{1,0:T(8,128)(2,1)}, bf16[512,384]{1,0:T(8,128)(2,1)S(1)}, u32[]{:S(2)}, u32[]{:S(2)}) collective-permute-start(bf16[512,384]{1,0:T(8,128)(2,1)} %refs_0_.3), channel_id=1, source_target_pairs={{16,0},{24,8},{32,16},{40,24},{48,32},{56,40},{64,48},{72,56},{80,... | collective-permute-start | bytes 1179656 | tf_op jit(solution)/shard_map/ppermute | solution.py:135
  5.3 14.8 %collective-permute-start.1 = (bf16[512,384]{1,0:T(8,128)(2,1)}, bf16[512,384]{1,0:T(8,128)(2,1)S(1)}, u32[]{:S(2)}, u32[]{:S(2)}) collective-permute-start(bf16[512,384]{1,0:T(8,128)(2,1)} %refs_0_.3), channel_id=1, source_target_pairs={{0,16},{8,24},{16,32},{24,40},{32,48},{40,56},{48,64},{56,72},{64,... | collective-permute-start | bytes 1179656 | tf_op jit(solution)/shard_map/ppermute | solution.py:135
  7.3 17.2 %collective-permute-start.2 = (bf16[512,384]{1,0:T(8,128)(2,1)}, bf16[512,384]{1,0:T(8,128)(2,1)S(1)}, u32[]{:S(2)}, u32[]{:S(2)}) collective-permute-start(bf16[512,384]{1,0:T(8,128)(2,1)} %refs_0_.3), channel_id=1, source_target_pairs={{0,8},{8,0},{16,24},{24,16},{32,40},{40,32},{48,56},{56,48},{64,72... | collective-permute-start | bytes 1179656 | tf_op jit(solution)/shard_map/ppermute | solution.py:150
  7.4 41.7 %collective-permute-start.10 = (bf16[512,384]{1,0:T(8,128)(2,1)}, bf16[512,384]{1,0:T(8,128)(2,1)}, u32[]{:S(2)}, u32[]{:S(2)}) collective-permute-start(bf16[512,384]{1,0:T(8,128)(2,1)} %refs_7_.3), channel_id=1, source_target_pairs={{16,0},{24,8},{32,16},{40,24},{48,32},{56,40},{64,48},{72,56},{80,... | collective-permute-start | bytes 1179656 | tf_op jit(solution)/shard_map/ppermute | solution.py:135
  14.1 18.4 %copy-start.1 = (bf16[512,384]{1,0:T(8,128)(2,1)S(1)}, bf16[512,384]{1,0:T(8,128)(2,1)}, u32[]{:S(2)}) copy-start(bf16[512,384]{1,0:T(8,128)(2,1)} %refs_7_.2) | copy-start | bytes 1179652
  14.1 18.4 %copy-start.2 = (bf16[512,384]{1,0:T(8,128)(2,1)S(1)}, bf16[512,384]{1,0:T(8,128)(2,1)}, u32[]{:S(2)}) copy-start(bf16[512,384]{1,0:T(8,128)(2,1)} %refs_0_.3) | copy-start | bytes 1179652
  14.9 17.6 %copy-start.4 = (bf16[512,384]{1,0:T(8,128)(2,1)}, bf16[512,384]{1,0:T(8,128)(2,1)S(1)}, u32[]{:S(2)}) copy-start(bf16[512,384]{1,0:T(8,128)(2,1)S(1)} %collective-permute-done.refs_1_) | copy-start | bytes 1179652
  20.1 12.3 %copy-start.5 = (bf16[512,384]{1,0:T(8,128)(2,1)}, bf16[512,384]{1,0:T(8,128)(2,1)S(1)}, u32[]{:S(2)}) copy-start(bf16[512,384]{1,0:T(8,128)(2,1)S(1)} %collective-permute-done.1.refs_2_) | copy-start | bytes 1179652
  21.0 11.4 %collective-permute-start.5 = (bf16[512,384]{1,0:T(8,128)(2,1)}, bf16[512,384]{1,0:T(8,128)(2,1)S(1)}, u32[]{:S(2)}, u32[]{:S(2)}) collective-permute-start(bf16[512,384]{1,0:T(8,128)(2,1)} %broadcast_select_fusion.1), channel_id=1, source_target_pairs={{8,16},{16,8},{24,32},{32,24},{40,48},{48,40},{56,64},{64,56},{72,... | collective-permute-start | bytes 1179656 | tf_op jit(solution)/shard_map/ppermute | solution.py:156
  22.9 9.5 %collective-permute-start.3 = (bf16[512,384]{1,0:T(8,128)(2,1)S(1)}, bf16[512,384]{1,0:T(8,128)(2,1)S(1)}, u32[]{:S(2)}, u32[]{:S(2)}) collective-permute-start(bf16[512,384]{1,0:T(8,128)(2,1)S(1)} %collective-permute-done.refs_1_), channel_id=1, source_target_pairs={{0,8},{8,0},{16,24},{24,16},{32,40},{40,32},{48,56},{56,48},{64,72... | collective-permute-start | bytes 1179656 | tf_op jit(solution)/shard_map/ppermute | solution.py:150
  23.0 9.5 %collective-permute-start.4 = (bf16[512,384]{1,0:T(8,128)(2,1)S(1)}, bf16[512,384]{1,0:T(8,128)(2,1)S(1)}, u32[]{:S(2)}, u32[]{:S(2)}) collective-permute-start(bf16[512,384]{1,0:T(8,128)(2,1)S(1)} %collective-permute-done.1.refs_2_), channel_id=1, source_target_pairs={{0,8},{8,0},{16,24},{24,16},{32,40},{40,32},{48,56},{56,48},{64,72... | collective-permute-start | bytes 1179656 | tf_op jit(solution)/shard_map/ppermute | solution.py:150
  24.5 9.8 %copy-start.6 = (bf16[512,384]{1,0:T(8,128)(2,1)}, bf16[512,384]{1,0:T(8,128)(2,1)S(1)}, u32[]{:S(2)}) copy-start(bf16[512,384]{1,0:T(8,128)(2,1)S(1)} %collective-permute-done.2.refs_3_) | copy-start | bytes 1179652
  24.5 24.6 %collective-permute-start.11 = (bf16[512,384]{1,0:T(8,128)(2,1)}, bf16[512,384]{1,0:T(8,128)(2,1)}, u32[]{:S(2)}, u32[]{:S(2)}) collective-permute-start(bf16[512,384]{1,0:T(8,128)(2,1)} %refs_7_.3), channel_id=1, source_target_pairs={{0,16},{8,24},{16,32},{24,40},{32,48},{40,56},{48,64},{56,72},{64,... | collective-permute-start | bytes 1179656 | tf_op jit(solution)/shard_map/ppermute | solution.py:135
  32.4 1.9 %copy-start.7 = (bf16[512,384]{1,0:T(8,128)(2,1)}, bf16[512,384]{1,0:T(8,128)(2,1)S(1)}, u32[]{:S(2)}) copy-start(bf16[512,384]{1,0:T(8,128)(2,1)S(1)} %collective-permute-done.5.refs_6_) | copy-start | bytes 1179652
  32.4 21.9 %collective-permute-start.12 = (bf16[512,384]{1,0:T(8,128)(2,1)}, bf16[512,384]{1,0:T(8,128)(2,1)}, u32[]{:S(2)}, u32[]{:S(2)}) collective-permute-start(bf16[512,384]{1,0:T(8,128)(2,1)} %refs_7_.3), channel_id=1, source_target_pairs={{0,8},{8,0},{16,24},{24,16},{32,40},{40,32},{48,56},{56,48},{64,72... | collective-permute-start | bytes 1179656 | tf_op jit(solution)/shard_map/ppermute | solution.py:150
  32.4 1.9 %copy-start.8 = (bf16[512,384]{1,0:T(8,128)(2,1)}, bf16[512,384]{1,0:T(8,128)(2,1)S(1)}, u32[]{:S(2)}) copy-start(bf16[512,384]{1,0:T(8,128)(2,1)S(1)} %collective-permute-done.3.refs_4_) | copy-start | bytes 1179652
  32.5 1.8 %copy-start.9 = (bf16[512,384]{1,0:T(8,128)(2,1)}, bf16[512,384]{1,0:T(8,128)(2,1)S(1)}, u32[]{:S(2)}) copy-start(bf16[512,384]{1,0:T(8,128)(2,1)S(1)} %collective-permute-done.4.refs_5_) | copy-start | bytes 1179652
  34.3 7.8 %collective-permute-start.6 = (f32[8,512]{1,0:T(8,128)S(1)}, f32[8,512]{1,0:T(8,128)S(1)}, u32[]{:S(2)}, u32[]{:S(2)}) collective-permute-start(f32[8,512]{1,0:T(8,128)S(1)} %row_squares.1), channel_id=1, source_target_pairs={{0,7},{1,0},{2,1},{3,2},{4,3},{5,4},{6,5},{7,6},{8,15},{9,8},{10,9... | collective-permute-start | bytes 49160 | tf_op jit(solution)/shard_map/ppermute | solution.py:140
  40.3 4.9 %collective-permute-start.7 = (f32[8,512]{1,0:T(8,128)S(1)}, f32[8,512]{1,0:T(8,128)S(1)}, u32[]{:S(2)}, u32[]{:S(2)}) collective-permute-start(f32[8,512]{1,0:T(8,128)S(1)} %row_squares.1), channel_id=1, source_target_pairs={{0,1},{1,2},{2,3},{3,4},{4,5},{5,6},{6,7},{7,0},{8,9},{9,10},{10,1... | collective-permute-start | bytes 49160 | tf_op jit(solution)/shard_map/ppermute | solution.py:140
  45.2 6.9 %collective-permute-start.8 = (f32[8,512]{1,0:T(8,128)S(1)}, f32[8,512]{1,0:T(8,128)S(1)}, u32[]{:S(2)}, u32[]{:S(2)}) collective-permute-start(f32[8,512]{1,0:T(8,128)S(1)} %get-tuple-element.38), channel_id=1, source_target_pairs={{0,5},{1,6},{2,7},{3,0},{4,1},{5,2},{6,3},{7,4},{8,13},{9,14},{10,... | collective-permute-start | bytes 49160 | tf_op jit(solution)/shard_map/ppermute | solution.py:140
  45.9 6.7 %collective-permute-start.9 = (f32[8,512]{1,0:T(8,128)S(1)}, f32[8,512]{1,0:T(8,128)S(1)}, u32[]{:S(2)}, u32[]{:S(2)}) collective-permute-start(f32[8,512]{1,0:T(8,128)S(1)} %get-tuple-element.39), channel_id=1, source_target_pairs={{0,3},{1,4},{2,5},{3,6},{4,7},{5,0},{6,1},{7,2},{8,11},{9,12},{10,... | collective-permute-start | bytes 49160 | tf_op jit(solution)/shard_map/ppermute | solution.py:140
  50.1 11.2 %collective-permute-start.15 = (bf16[512,384]{1,0:T(8,128)(2,1)S(1)}, bf16[512,384]{1,0:T(8,128)(2,1)S(1)}, u32[]{:S(2)}, u32[]{:S(2)}) collective-permute-start(bf16[512,384]{1,0:T(8,128)(2,1)S(1)} %broadcast_select_fusion), channel_id=1, source_target_pairs={{8,16},{16,8},{24,32},{32,24},{40,48},{48,40},{56,64},{64,56},{72,... | collective-permute-start | bytes 1179656 | tf_op jit(solution)/shard_map/ppermute | solution.py:156
  52.0 9.3 %collective-permute-start.13 = (bf16[512,384]{1,0:T(8,128)(2,1)}, bf16[512,384]{1,0:T(8,128)(2,1)S(1)}, u32[]{:S(2)}, u32[]{:S(2)}) collective-permute-start(bf16[512,384]{1,0:T(8,128)(2,1)} %collective-permute-done.10.refs_8_), channel_id=1, source_target_pairs={{0,8},{8,0},{16,24},{24,16},{32,40},{40,32},{48,56},{56,48},{64,72... | collective-permute-start | bytes 1179656 | tf_op jit(solution)/shard_map/ppermute | solution.py:150
  52.1 9.2 %collective-permute-start.14 = (bf16[512,384]{1,0:T(8,128)(2,1)}, bf16[512,384]{1,0:T(8,128)(2,1)S(1)}, u32[]{:S(2)}, u32[]{:S(2)}) collective-permute-start(bf16[512,384]{1,0:T(8,128)(2,1)} %collective-permute-done.11.refs_9_), channel_id=1, source_target_pairs={{0,8},{8,0},{16,24},{24,16},{32,40},{40,32},{48,56},{56,48},{64,72... | collective-permute-start | bytes 1179656 | tf_op jit(solution)/shard_map/ppermute | solution.py:150
  85.7 3.0 %collective-permute-start.18 = (bf16[512,384]{1,0:T(8,128)(2,1)}, bf16[512,384]{1,0:T(8,128)(2,1)S(1)}, u32[]{:S(2)}, u32[]{:S(2)}) collective-permute-start(bf16[512,384]{1,0:T(8,128)(2,1)} %get-tuple-element.26), channel_id=1, source_target_pairs={{0,8},{8,0},{16,24},{24,16},{32,40},{40,32},{48,56},{56,48},{64,72... | collective-permute-start | bytes 1179656 | tf_op jit(solution)/shard_map/ppermute | solution.py:150
  85.8 12.6 %collective-permute-start.28 = (bf16[512,384]{1,0:T(8,128)(2,1)}, bf16[512,384]{1,0:T(8,128)(2,1)S(1)}, u32[]{:S(2)}, u32[]{:S(2)}) collective-permute-start(bf16[512,384]{1,0:T(8,128)(2,1)} %get-tuple-element.33), channel_id=1, source_target_pairs={{0,8},{8,0},{16,24},{24,16},{32,40},{40,32},{48,56},{56,48},{64,72... | collective-permute-start | bytes 1179656 | tf_op jit(solution)/shard_map/ppermute | solution.py:150
  86.2 6.5 %collective-permute-start.20 = (bf16[512,384]{1,0:T(8,128)(2,1)}, bf16[512,384]{1,0:T(8,128)(2,1)S(1)}, u32[]{:S(2)}, u32[]{:S(2)}) collective-permute-start(bf16[512,384]{1,0:T(8,128)(2,1)} %get-tuple-element.28), channel_id=1, source_target_pairs={{0,8},{8,0},{16,24},{24,16},{32,40},{40,32},{48,56},{56,48},{64,72... | collective-permute-start | bytes 1179656 | tf_op jit(solution)/shard_map/ppermute | solution.py:150
  86.3 13.0 %collective-permute-start.16 = (bf16[512,384]{1,0:T(8,128)(2,1)}, bf16[512,384]{1,0:T(8,128)(2,1)S(1)}, u32[]{:S(2)}, u32[]{:S(2)}) collective-permute-start(bf16[512,384]{1,0:T(8,128)(2,1)} %get-tuple-element.23), channel_id=1, source_target_pairs={{0,8},{8,0},{16,24},{24,16},{32,40},{40,32},{48,56},{56,48},{64,72... | collective-permute-start | bytes 1179656 | tf_op jit(solution)/shard_map/ppermute | solution.py:150
  86.8 15.3 %collective-permute-start.17 = (bf16[512,384]{1,0:T(8,128)(2,1)}, bf16[512,384]{1,0:T(8,128)(2,1)S(1)}, u32[]{:S(2)}, u32[]{:S(2)}) collective-permute-start(bf16[512,384]{1,0:T(8,128)(2,1)} %get-tuple-element.24), channel_id=1, source_target_pairs={{8,32},{24,48},{32,8},{40,64},{48,24},{56,80},{64,40},{72,96},{80,... | collective-permute-start | bytes 1179656 | tf_op jit(solution)/shard_map/ppermute | solution.py:156
  88.7 4.1 %copy-start.15 = (bf16[512,384]{1,0:T(8,128)(2,1)S(1)}, bf16[512,384]{1,0:T(8,128)(2,1)}, u32[]{:S(2)}) copy-start(bf16[512,384]{1,0:T(8,128)(2,1)} %get-tuple-element.27) | copy-start | bytes 1179652
  89.9 8.2 %copy-start.10 = (f32[512,384]{1,0:T(8,128)S(1)}, f32[512,384]{1,0:T(8,128)}, u32[]{:S(2)}) copy-start(f32[512,384]{1,0:T(8,128)} %get-tuple-element.21) | copy-start | bytes 2359300
  89.9 26.4 %collective-permute-start.19 = (bf16[512,384]{1,0:T(8,128)(2,1)S(1)}, bf16[512,384]{1,0:T(8,128)(2,1)S(1)}, u32[]{:S(2)}, u32[]{:S(2)}) collective-permute-start(bf16[512,384]{1,0:T(8,128)(2,1)S(1)} %add_convert_fusion.4), channel_id=1, source_target_pairs={{0,16},{8,24},{16,32},{24,40},{32,48},{40,56},{48,64},{56,72},{64,... | collective-permute-start | bytes 1179656 | tf_op jit(solution)/shard_map/ppermute | solution.py:135
  92.9 25.3 %collective-permute-start.21 = (bf16[512,384]{1,0:T(8,128)(2,1)S(1)}, bf16[512,384]{1,0:T(8,128)(2,1)S(1)}, u32[]{:S(2)}, u32[]{:S(2)}) collective-permute-start(bf16[512,384]{1,0:T(8,128)(2,1)S(1)} %add_convert_fusion.3), channel_id=1, source_target_pairs={{16,0},{24,8},{32,16},{40,24},{48,32},{56,40},{64,48},{72,56},{80,... | collective-permute-start | bytes 1179656 | tf_op jit(solution)/shard_map/ppermute | solution.py:135
  99.1 21.2 %collective-permute-start.30 = (bf16[512,384]{1,0:T(8,128)(2,1)S(1)}, bf16[512,384]{1,0:T(8,128)(2,1)S(1)}, u32[]{:S(2)}, u32[]{:S(2)}) collective-permute-start(bf16[512,384]{1,0:T(8,128)(2,1)S(1)} %copy-done.23), channel_id=1, source_target_pairs={{0,8},{8,0},{16,24},{24,16},{32,40},{40,32},{48,56},{56,48},{64,72... | collective-permute-start | bytes 1179656 | tf_op jit(solution)/shard_map/ppermute | solution.py:150
  99.2 2.9 %copy-start.21 = (bf16[512,384]{1,0:T(8,128)(2,1)S(1)}, bf16[512,384]{1,0:T(8,128)(2,1)}, u32[]{:S(2)}) copy-start(bf16[512,384]{1,0:T(8,128)(2,1)} %get-tuple-element.31) | copy-start | bytes 1179652
  99.2 19.0 %copy-start.3 = (bf16[512,384]{1,0:T(8,128)(2,1)S(1)}, bf16[512,384]{1,0:T(8,128)(2,1)}, u32[]{:S(2)}) copy-start(bf16[512,384]{1,0:T(8,128)(2,1)} %refs_0_.3) | copy-start | bytes 1179652
  99.2 19.0 %copy-start.11 = (bf16[512,384]{1,0:T(8,128)(2,1)S(1)}, bf16[512,384]{1,0:T(8,128)(2,1)}, u32[]{:S(2)}) copy-start(bf16[512,384]{1,0:T(8,128)(2,1)} %get-tuple-element.22) | copy-start | bytes 1179652
  99.4 32.3 %collective-permute-start.26 = (bf16[512,384]{1,0:T(8,128)(2,1)S(1)}, bf16[512,384]{1,0:T(8,128)(2,1)S(1)}, u32[]{:S(2)}, u32[]{:S(2)}) collective-permute-start(bf16[512,384]{1,0:T(8,128)(2,1)S(1)} %copy-done.22), channel_id=1, source_target_pairs={{0,8},{8,0},{16,24},{24,16},{32,40},{40,32},{48,56},{56,48},{64,72... | collective-permute-start | bytes 1179656 | tf_op jit(solution)/shard_map/ppermute | solution.py:150
  102.1 33.3 %collective-permute-start.27 = (bf16[512,384]{1,0:T(8,128)(2,1)S(1)}, bf16[512,384]{1,0:T(8,128)(2,1)S(1)}, u32[]{:S(2)}, u32[]{:S(2)}) collective-permute-start(bf16[512,384]{1,0:T(8,128)(2,1)S(1)} %copy-done.21), channel_id=1, source_target_pairs={{8,32},{24,48},{32,8},{40,64},{48,24},{56,80},{64,40},{72,96},{80,... | collective-permute-start | bytes 1179656 | tf_op jit(solution)/shard_map/ppermute | solution.py:156
  116.2 19.2 %collective-permute-start.29 = (bf16[512,384]{1,0:T(8,128)(2,1)S(1)}, bf16[512,384]{1,0:T(8,128)(2,1)S(1)}, u32[]{:S(2)}, u32[]{:S(2)}) collective-permute-start(bf16[512,384]{1,0:T(8,128)(2,1)S(1)} %add_convert_fusion.2), channel_id=1, source_target_pairs={{0,16},{8,24},{16,32},{24,40},{32,48},{40,56},{48,64},{56,72},{64,... | collective-permute-start | bytes 1179656 | tf_op jit(solution)/shard_map/ppermute | solution.py:135
  118.2 2.1 %copy-start.13 = (bf16[512,384]{1,0:T(8,128)(2,1)S(1)}, bf16[512,384]{1,0:T(8,128)(2,1)}, u32[]{:S(2)}) copy-start(bf16[512,384]{1,0:T(8,128)(2,1)} %get-tuple-element.34) | copy-start | bytes 1179652
  118.6 8.0 %collective-permute-start.22 = (f32[2,512]{1,0:T(2,128)S(1)}, f32[2,512]{1,0:T(2,128)S(1)}, u32[]{:S(2)}, u32[]{:S(2)}) collective-permute-start(f32[2,512]{1,0:T(2,128)S(1)} %pad_maximum_fusion), channel_id=1, source_target_pairs={{0,7},{1,0},{2,1},{3,2},{4,3},{5,4},{6,5},{7,6},{8,15},{9,8},{10,9... | collective-permute-start | bytes 12296 | tf_op jit(solution)/shard_map/ppermute | solution.py:140
  120.3 15.1 %copy-start.12 = (bf16[512,384]{1,0:T(8,128)(2,1)S(1)}, bf16[512,384]{1,0:T(8,128)(2,1)}, u32[]{:S(2)}) copy-start(bf16[512,384]{1,0:T(8,128)(2,1)} %get-tuple-element.29) | copy-start | bytes 1179652
  120.4 15.0 %collective-permute-start.31 = (bf16[512,384]{1,0:T(8,128)(2,1)S(1)}, bf16[512,384]{1,0:T(8,128)(2,1)S(1)}, u32[]{:S(2)}, u32[]{:S(2)}) collective-permute-start(bf16[512,384]{1,0:T(8,128)(2,1)S(1)} %add_convert_fusion.1), channel_id=1, source_target_pairs={{16,0},{24,8},{32,16},{40,24},{48,32},{56,40},{64,48},{72,56},{80,... | collective-permute-start | bytes 1179656 | tf_op jit(solution)/shard_map/ppermute | solution.py:135
  126.6 4.9 %collective-permute-start.23 = (f32[2,512]{1,0:T(2,128)S(1)}, f32[2,512]{1,0:T(2,128)S(1)}, u32[]{:S(2)}, u32[]{:S(2)}) collective-permute-start(f32[2,512]{1,0:T(2,128)S(1)} %pad_maximum_fusion), channel_id=1, source_target_pairs={{0,1},{1,2},{2,3},{3,4},{4,5},{5,6},{6,7},{7,0},{8,9},{9,10},{10,1... | collective-permute-start | bytes 12296 | tf_op jit(solution)/shard_map/ppermute | solution.py:140
  131.5 5.5 %collective-permute-start.24 = (f32[2,512]{1,0:T(2,128)S(1)}, f32[2,512]{1,0:T(2,128)S(1)}, u32[]{:S(2)}, u32[]{:S(2)}) collective-permute-start(f32[2,512]{1,0:T(2,128)S(1)} %get-tuple-element.36), channel_id=1, source_target_pairs={{0,5},{1,6},{2,7},{3,0},{4,1},{5,2},{6,3},{7,4},{8,13},{9,14},{10,... | collective-permute-start | bytes 12296 | tf_op jit(solution)/shard_map/ppermute | solution.py:140
  131.6 6.7 %collective-permute-start.25 = (f32[2,512]{1,0:T(2,128)S(1)}, f32[2,512]{1,0:T(2,128)S(1)}, u32[]{:S(2)}, u32[]{:S(2)}) collective-permute-start(f32[2,512]{1,0:T(2,128)S(1)} %get-tuple-element.37), channel_id=1, source_target_pairs={{0,3},{1,4},{2,5},{3,6},{4,7},{5,0},{6,1},{7,2},{8,11},{9,12},{10,... | collective-permute-start | bytes 12296 | tf_op jit(solution)/shard_map/ppermute | solution.py:140
  (11 other events, 10.3 us)

commit v2 on v1

--- a/solution.py
+++ b/solution.py
@@ -15,12 +15,12 @@
 KEYS = SLOTS * FT
 
 
-def head_kernel(bias_ref, rate_ref, gain_ref, *refs):
+def head_kernel(bias_ref, *refs):
     key_refs = refs[:SLOTS]
     value_refs = refs[SLOTS:2 * SLOTS]
     q_ref, g_ref, att_ref, gq_ref = refs[2 * SLOTS:2 * SLOTS + 4]
     term_refs = refs[2 * SLOTS + 4:4 * SLOTS + 4]
-    kb, kt, vb, st = refs[4 * SLOTS + 4:]
+    kb, vb, st = refs[4 * SLOTS + 4:]
     f32, bf = jnp.float32, jnp.bfloat16
     q = q_ref[...]
     g = g_ref[...]
@@ -33,8 +33,7 @@
     m8 = jnp.full((8, FT), NEG, f32)
     for s in range(SLOTS):
         cols = slice(s * FT, (s + 1) * FT)
-        normed = (key_refs[s][...].T.astype(f32) * rate_ref[s:s + 1, :] * gain_ref[...]).astype(bf)
-        kb[cols, :] = normed.T
+        kb[cols, :] = key_refs[s][...]
         vb[cols, :] = value_refs[s][...]
     for lo, hi in [(0, 2), (2, 4), (4, 6), (6, 7)]:
         cols = slice(lo * FT, hi * FT)
@@ -98,7 +97,7 @@
     )(*parts)
 
 
-def head_call(bias, rates, gain, keys, values, query, grad):
+def head_call(bias, keys, values, query, grad):
     vm = pltpu.VMEM
     bf, f32 = jnp.bfloat16, jnp.float32
     width = query.shape[1]
@@ -108,8 +107,6 @@
         grid=(width // BLK,),
         in_specs=[
             pl.BlockSpec((4 * SLOTS, FT), lambda i: (0, 0)),
-            pl.BlockSpec((8, FT), lambda i: (0, 0)),
-            pl.BlockSpec((BLK, 1), lambda i: (i, 0)),
         ]
         + [rows] * (2 * SLOTS + 2),
         out_specs=[rows] * (2 + 2 * SLOTS),
@@ -117,22 +114,22 @@
         + [jax.ShapeDtypeStruct((FT, width), bf)] * (2 * SLOTS),
         scratch_shapes=[
             vm((KEYS, BLK), bf),
-            vm((BLK, KEYS), bf),
             vm((KEYS, BLK), bf),
             vm((KEYS, FT), f32),
         ],
         compiler_params=pltpu.CompilerParams(vmem_limit_bytes=56 * 1024 * 1024),
         name="head_attention",
         cost_estimate=pl.CostEstimate(flops=9 * 10**9, bytes_accessed=12 * 10**6, transcendentals=12 * 10**6),
-    )(bias, rates, gain, *keys, *values, query, grad)
+    )(bias, *keys, *values, query, grad)
 
 
 epsilon = 1e-06
 
 
-def shifted(value, steps):
+def across(value, late):
     count = lax.axis_size("tm")
-    return lax.ppermute(value, "tm", [(s, s + steps) for s in range(max(0, -steps), min(count, count - steps))])
+    pairs = [(s, s ^ 2) if not late else (s, ((s + 2) ^ 2) - 2) for s in range(count)]
+    return lax.ppermute(value, "tm", [(a, b) for a, b in pairs if 0 <= b < count])
 
 
 def turned(value, steps):
@@ -150,26 +147,29 @@
     return lax.ppermute(value, "tm", [(s, s ^ 1) for s in range(lax.axis_size("tm"))])
 
 
-def outward(value, steps):
+def outward(value):
     count = lax.axis_size("tm")
-    pairs = [(s, s + steps) if s % 2 else (s, s - steps) for s in range(count)]
+    pairs = [(s, s + 1) if s % 2 else (s, s - 1) for s in range(count)]
     return lax.ppermute(value, "tm", [(a, b) for a, b in pairs if 0 <= b < count])
 
 
-def band(value, odd):
-    ahead, behind = shifted(value, -2), shifted(value, 2)
+def band(value, cross):
+    early, late = across(value, False), across(value, True)
     beside = swapped(value)
-    outer = outward(jnp.where(odd, behind, ahead), 1)
-    return [value, ahead, behind, beside, swapped(ahead), swapped(behind), outer]
-
-
-def returned(terms):
+    outer = outward(jnp.where(cross, early, late))
+    return [value, early, late, beside, swapped(early), swapped(late), outer]
+
+
+def paired(terms, cross):
     f32 = jnp.float32
-    outer = outward(terms[6], 3)
-    ahead = (terms[1].astype(f32) + swapped(terms[4]).astype(f32)).astype(jnp.bfloat16)
-    behind = (terms[2].astype(f32) + swapped(terms[5]).astype(f32)).astype(jnp.bfloat16)
-    beside = swapped(terms[3])
-    return [terms[0], beside, outer, shifted(ahead, 2), shifted(behind, -2)]
+    outer = outward(terms[6]).astype(f32)
+    early = terms[1].astype(f32) + swapped(terms[4]).astype(f32) + jnp.where(cross, outer, 0.0)
+    late = terms[2].astype(f32) + swapped(terms[5]).astype(f32) + jnp.where(cross, 0.0, outer)
+    return early.astype(jnp.bfloat16), late.astype(jnp.bfloat16)
+
+
+def returned(terms, early, late):
+    return [terms[0], swapped(terms[3]), across(early, False), across(late, True)]
 
 
 def summed(parts):
@@ -182,12 +182,13 @@
 def local(queries, key_rows, value_rows, query_gain, key_gain, block_mask, out_grad):
     frame = lax.axis_index("tm")
     frame_count = lax.axis_size("tm")
-    odd = frame % 2 == 1
+    core = 1 - 2 * (frame % 2)
+    chip = 2 - 4 * (frame // 2 % 2)
+    cross = core * chip > 0
     full_width = queries.shape[1] * lax.axis_size("head")
-    keys = band(key_rows, odd)
-    values = band(value_rows, odd)
-
-    offsets = jnp.where(odd, jnp.array([0, 2, -2, -1, 1, -3, 3]), jnp.array([0, 2, -2, 1, 3, -1, -3]))
+    values = band(value_rows, cross)
+
+    offsets = jnp.stack([0 * core, chip, -chip, core, core + chip, core - chip, -3 * core])
     mask_rows = lax.dynamic_index_in_dim(block_mask, frame, 0, keepdims=False)
     is_valid = (frame + offsets >= 0) & (frame + offsets < frame_count)
     live = jnp.where(is_valid[:, None, None], mask_rows[offsets + 3], 0)
@@ -196,24 +197,30 @@
 
     query_float = queries.astype(jnp.float32)
     key_float = key_rows.astype(jnp.float32)
-    rates = lax.rsqrt(ring_sum(square_call(keys + [queries])) / full_width + epsilon)
-    query_rate = rates[SLOTS][:, None]
-    key_rate = rates[0][:, None]
+    key_raw, values[3] = lax.optimization_barrier((key_rows, values[3]))
+    rates = lax.rsqrt(ring_sum(square_call([queries, key_raw])) / full_width + epsilon)
+    query_rate = rates[0][:, None]
+    key_rate = rates[1][:, None]
     query_scaled = (query_float * query_rate * query_gain * (SCALE * LOG2E)).astype(jnp.bfloat16)
-
-    out = head_call(bias, rates, key_gain[:, None], keys, values, query_scaled, out_grad)
+    keys = band((key_float * key_rate * key_gain).astype(jnp.bfloat16), cross)
+
+    out = head_call(bias, keys, values, query_scaled, out_grad)
     attended, grad_qnorm = out[:2]
-    key_parts = returned(out[2:2 + SLOTS])
-    value_parts = returned(out[2 + SLOTS:])
+    key_terms, value_terms = out[2:2 + SLOTS], out[2 + SLOTS:]
+    key_parts = returned(key_terms, *paired(key_terms, cross))
+    value_near = paired(value_terms, cross)
+    key_parts, value_near = lax.optimization_barrier((key_parts, value_near))
+    value_parts = returned(value_terms, *value_near)
     grad_knorm = summed(key_parts)
-    value_sum = summed(value_parts)
     dots = jnp.stack(
         [
             jnp.sum(query_float * query_gain * grad_qnorm, axis=1),
             jnp.sum(key_float * key_gain * grad_knorm, axis=1),
         ]
     )
-    query_dot, key_dot = ring_sum(dots)
+    dots, value_parts = lax.optimization_barrier((ring_sum(dots), value_parts))
+    query_dot, key_dot = dots
+    value_sum = summed(value_parts)
     query_grad = (
         query_rate * query_gain * grad_qnorm
         - query_float * query_rate**3 * query_dot[:, None] / full_width

time: 141 us -> 127 us (0.901)
  starting transfers between devices: 58.1 us -> 45.5 us
  waiting for transfers between devices: 41.9 us -> 43.4 us
    ppermute x8, starting transfers between devices: 31 us -> 14.3 us  [across(): lax.ppermute(value, 'tm', [(a, b) for a, b in pairs if 0 <= b < count])]
    ppermute x4, waiting for transfers between devices: 15 us -> 8.95 us  [outward(): lax.ppermute(value, 'tm', [(a, b) for a, b in pairs if 0 <= b < count])]
    ppermute x8, waiting for transfers between devices: 9.19 us -> 13 us  [turned(): lax.ppermute(value, 'head', [(s, (s + steps) % count) for s in range(coun...]
    ppermute x8, waiting for transfers between devices: 17.7 us -> 21.4 us  [across(): lax.ppermute(value, 'tm', [(a, b) for a, b in pairs if 0 <= b < count])]
    ppermute x4, starting transfers between devices: 8.21 us -> 11.6 us  [outward(): lax.ppermute(value, 'tm', [(a, b) for a, b in pairs if 0 <= b < count])]
    select_n x2, other arithmetic: 1.9 us -> 0.1 us  [band(): outer = outward(jnp.where(cross, early, late))]
    unnamed x56 -> x42, local copies, waits for them, and re-layouts: 4.02 us -> 5.01 us
  transfers between devices with their start and end apart: 32 -> 32, of which waited for: 10 -> 15; matrix products, arithmetic and copies ran while one was open for 6% -> 4% of each run, Pallas kernels for 1% -> 0%
where the time goes in v2:
time: 127 us; the launch traced here: 126 us
  starting transfers between devices  45.5 us (36%)
  waiting for transfers between devices  43.4 us (34%)
  Pallas kernels  23.7 us (19%)
  local copies, waits for them, and re-layouts  6.39 us (5%)
  other arithmetic  6.19 us (5%)
    pallas_call x1, Pallas kernels, head_call(): pl.pallas_call(head_kernel, grid=(width // BLK,), in_specs=[pl.BlockSpec(...  23.2 us
    ppermute x8, waiting for transfers between devices, across(): lax.ppermute(value, 'tm', [(a, b) for a, b in pairs if 0 <= b < count])  21.4 us
    ppermute x8, starting transfers between devices, turned(): lax.ppermute(value, 'head', [(s, (s + steps) % count) for s in range(coun...  15.9 us
    ppermute x8, starting transfers between devices, across(): lax.ppermute(value, 'tm', [(a, b) for a, b in pairs if 0 <= b < count])  14.3 us
    ppermute x8, waiting for transfers between devices, turned(): lax.ppermute(value, 'head', [(s, (s + steps) % count) for s in range(coun...  13 us
    ppermute x4, starting transfers between devices, outward(): lax.ppermute(value, 'tm', [(a, b) for a, b in pairs if 0 <= b < count])  11.6 us
    ppermute x4, waiting for transfers between devices, outward(): lax.ppermute(value, 'tm', [(a, b) for a, b in pairs if 0 <= b < count])  8.95 us
    unnamed x42, local copies, waits for them, and re-layouts  5.01 us
  transfers between devices with their start and end apart: 32, of which 15 were waited for; matrix products, arithmetic and copies ran while one was open for 4% of the time, Pallas kernels for 0%

profile of v2, /device:TPU:8, one launch (start us, length us, event | category | flops | bytes accessed | tf_op | source)
XLA Modules:
  0.0 126.2 jit_solution(6526403023591363387)
XLA Ops:
  0.7 1.6 %collective-permute-start.11 = (bf16[512,384]{1,0:T(8,128)(2,1)}, bf16[512,384]{1,0:T(8,128)(2,1)S(1)}, u32[]{:S(2)}, u32[]{:S(2)}) collective-permute-start(bf16[512,384]{1,0:T(8,128)(2,1)} %refs_7_.1), channel_id=1, source_target_pairs={{0,16},{8,24},{16,0},{24,8},{32,48},{40,56},{48,32},{56,40},{64,80... | collective-permute-start | bytes 1179656 | tf_op jit(solution)/shard_map/ppermute | solution.py:132
  2.3 3.9 %collective-permute-start.12 = (bf16[512,384]{1,0:T(8,128)(2,1)}, bf16[512,384]{1,0:T(8,128)(2,1)S(1)}, u32[]{:S(2)}, u32[]{:S(2)}) collective-permute-start(bf16[512,384]{1,0:T(8,128)(2,1)} %refs_7_.1), channel_id=1, source_target_pairs={{16,32},{24,40},{32,16},{40,24},{48,64},{56,72},{64,48},{72,56},{8... | collective-permute-start | bytes 1179656 | tf_op jit(solution)/shard_map/ppermute | solution.py:132
  6.4 1.0 copy-done.1
  7.4 1.0 copy-done.3
  8.4 0.5 row_squares.1
  8.9 5.9 %collective-permute-start.1 = (f32[2,512]{1,0:T(2,128)S(1)}, f32[2,512]{1,0:T(2,128)S(1)}, u32[]{:S(2)}, u32[]{:S(2)}) collective-permute-start(f32[2,512]{1,0:T(2,128)S(1)} %row_squares.1), channel_id=1, source_target_pairs={{0,7},{1,0},{2,1},{3,2},{4,3},{5,4},{6,5},{7,6},{8,15},{9,8},{10,9... | collective-permute-start | bytes 12296 | tf_op jit(solution)/shard_map/ppermute | solution.py:137
  14.9 1.2 collective-permute-done.1
  16.1 3.5 %collective-permute-done.2 = f32[2,512]{1,0:T(2,128)S(1)} collective-permute-done((f32[2,512]{1,0:T(2,128)S(1)}, f32[2,512]{1,0:T(2,128)S(1)}, u32[]{:S(2)}, u32[]{:S(2)}) %collective-permute-start.2) | collective-permute-done | bytes 4128 | tf_op jit(solution)/shard_map/ppermute | solution.py:137
  19.6 0.7 collective-permute-start.3
  20.3 3.1 %collective-permute-start.4 = (f32[2,512]{1,0:T(2,128)S(1)}, f32[2,512]{1,0:T(2,128)S(1)}, u32[]{:S(2)}, u32[]{:S(2)}) collective-permute-start(f32[2,512]{1,0:T(2,128)S(1)} %get-tuple-element.65), channel_id=1, source_target_pairs={{0,3},{1,4},{2,5},{3,6},{4,7},{5,0},{6,1},{7,2},{8,11},{9,12},{10,... | collective-permute-start | bytes 12296 | tf_op jit(solution)/shard_map/ppermute | solution.py:137
  23.7 0.6 gather_fusion
  24.4 0.6 collective-permute-done.3
  25.0 1.9 %collective-permute-done.4 = f32[2,512]{1,0:T(2,128)S(1)} collective-permute-done((f32[2,512]{1,0:T(2,128)S(1)}, f32[2,512]{1,0:T(2,128)S(1)}, u32[]{:S(2)}, u32[]{:S(2)}) %collective-permute-start.4) | collective-permute-done | bytes 4128 | tf_op jit(solution)/shard_map/ppermute | solution.py:137
  27.0 0.7 copy-done.16
  27.8 0.8 collective-permute-start.5
  28.6 3.4 %collective-permute-start.6 = (bf16[512,384]{1,0:T(8,128)(2,1)S(1)}, bf16[512,384]{1,0:T(8,128)(2,1)S(1)}, u32[]{:S(2)}, u32[]{:S(2)}) collective-permute-start(bf16[512,384]{1,0:T(8,128)(2,1)S(1)} %fusion.9.refs_0_), channel_id=1, source_target_pairs={{16,32},{24,40},{32,16},{40,24},{48,64},{56,72},{64,48},{72,56},{8... | collective-permute-start | bytes 1179656 | tf_op jit(solution)/shard_map/ppermute | solution.py:132
  32.1 1.9 %collective-permute-start.15 = (bf16[512,384]{1,0:T(8,128)(2,1)S(1)}, bf16[512,384]{1,0:T(8,128)(2,1)S(1)}, u32[]{:S(2)}, u32[]{:S(2)}) collective-permute-start(bf16[512,384]{1,0:T(8,128)(2,1)S(1)} %broadcast_select_fusion), channel_id=1, source_target_pairs={{8,16},{16,8},{24,32},{32,24},{40,48},{48,40},{56,64},{64,56},{72,... | collective-permute-start | bytes 1179656 | tf_op jit(solution)/shard_map/ppermute | solution.py:153
  34.0 1.7 %collective-permute-start.13 = (bf16[512,384]{1,0:T(8,128)(2,1)S(1)}, bf16[512,384]{1,0:T(8,128)(2,1)S(1)}, u32[]{:S(2)}, u32[]{:S(2)}) collective-permute-start(bf16[512,384]{1,0:T(8,128)(2,1)S(1)} %collective-permute-done.11.refs_8_), channel_id=1, source_target_pairs={{0,8},{8,0},{16,24},{24,16},{32,40},{40,32},{48,56},{56,48},{64,72... | collective-permute-start | bytes 1179656 | tf_op jit(solution)/shard_map/ppermute | solution.py:147
  35.8 0.4 collective-permute-done.5.refs_1_
  36.4 5.7 %collective-permute-done.6.refs_2_ = bf16[512,384]{1,0:T(8,128)(2,1)S(1)} collective-permute-done((bf16[512,384]{1,0:T(8,128)(2,1)S(1)}, bf16[512,384]{1,0:T(8,128)(2,1)S(1)}, u32[]{:S(2)}, u32[]{:S(2)}) %collective-permute-start.6) | collective-permute-done | bytes 393248 | tf_op jit(solution)/shard_map/ppermute | solution.py:132
  42.2 2.1 %collective-permute-start.10 = (bf16[512,384]{1,0:T(8,128)(2,1)S(1)}, bf16[512,384]{1,0:T(8,128)(2,1)}, u32[]{:S(2)}, u32[]{:S(2)}) collective-permute-start(bf16[512,384]{1,0:T(8,128)(2,1)S(1)} %broadcast_select_fusion.1), channel_id=1, source_target_pairs={{8,16},{16,8},{24,32},{32,24},{40,48},{48,40},{56,64},{64,56},{72,... | collective-permute-start | bytes 1179656 | tf_op jit(solution)/shard_map/ppermute | solution.py:153
  44.3 0.6 collective-permute-done.15.refs_13_
  44.9 0.7 collective-permute-start.9
  46.1 0.6 copy.21
  46.7 0.7 copy-done.15
  47.4 1.0 fusion.18.refs_14_
  48.3 5.3 %collective-permute-done.10.refs_6_ = bf16[512,384]{1,0:T(8,128)(2,1)} collective-permute-done((bf16[512,384]{1,0:T(8,128)(2,1)S(1)}, bf16[512,384]{1,0:T(8,128)(2,1)}, u32[]{:S(2)}, u32[]{:S(2)}) %collective-permute-start.10) | collective-permute-done | bytes 393248 | tf_op jit(solution)/shard_map/ppermute | solution.py:153
  53.6 23.2 %head_attention.1 = (bf16[512,384]{1,0:T(8,128)(2,1)}, f32[512,384]{1,0:T(8,128)}, bf16[512,384]{1,0:T(8,128)(2,1)}, bf16[512,384]{1,0:T(8,128)(2,1)}, bf16[512,...) custom-call(f32[28,512]{1,0:T(8,128)} %bitcast.28, ...), custom_call_target="tpu_custom_call" | custom-call | flops 8999999488 | bytes 12000000 | tf_op jit(solution)/shard_map/head_attention/pallas_call | solution.py:105
  76.9 1.9 %collective-permute-start.18 = (bf16[512,384]{1,0:T(8,128)(2,1)}, bf16[512,384]{1,0:T(8,128)(2,1)S(1)}, u32[]{:S(2)}, u32[]{:S(2)}) collective-permute-start(bf16[512,384]{1,0:T(8,128)(2,1)} %get-tuple-element.41), channel_id=1, source_target_pairs={{8,16},{16,8},{24,32},{32,24},{40,48},{48,40},{56,64},{64,56},{72,... | collective-permute-start | bytes 1179656 | tf_op jit(solution)/shard_map/ppermute | solution.py:153
  78.9 0.6 collective-permute-start.20
  79.5 5.7 %collective-permute-start.23 = (bf16[512,384]{1,0:T(8,128)(2,1)}, bf16[512,384]{1,0:T(8,128)(2,1)S(1)}, u32[]{:S(2)}, u32[]{:S(2)}) collective-permute-start(bf16[512,384]{1,0:T(8,128)(2,1)} %get-tuple-element.46), channel_id=1, source_target_pairs={{8,16},{16,8},{24,32},{32,24},{40,48},{48,40},{56,64},{64,56},{72,... | collective-permute-start | bytes 1179656 | tf_op jit(solution)/shard_map/ppermute | solution.py:153
  85.3 3.0 %collective-permute-done.18 = bf16[512,384]{1,0:T(8,128)(2,1)S(1)} collective-permute-done((bf16[512,384]{1,0:T(8,128)(2,1)}, bf16[512,384]{1,0:T(8,128)(2,1)S(1)}, u32[]{:S(2)}, u32[]{:S(2)}) %collective-permute-start.18) | collective-permute-done | bytes 393248 | tf_op jit(solution)/shard_map/ppermute | solution.py:153
  88.4 1.5 %fusion.3 = (bf16[512,384]{1,0:T(8,128)(2,1)S(1)}, bf16[512,384]{1,0:T(8,128)(2,1)S(1)}) fusion(bf16[512,384]{1,0:T(8,128)(2,1)S(1)} %collective-permute-done.18, bf16[512,384]{1,0:T(8,128)(2,1)S(1)} %collective-permute-done.20, bf16[512,384]{1,0:T(8,128)(2,1)} %get-tuple-element.42, pred[]{:T(512)S(6)} %gt.9, ...), kind=kLoop, calls=%fused_computation.14 | loop fusion | flops 2555904 | bytes 2752513 | tf_op jit(solution)/shard_map/convert_element_type | solution.py:168
  90.0 2.3 %collective-permute-start.21 = (bf16[512,384]{1,0:T(8,128)(2,1)S(1)}, bf16[512,384]{1,0:T(8,128)(2,1)S(1)}, u32[]{:S(2)}, u32[]{:S(2)}) collective-permute-start(bf16[512,384]{1,0:T(8,128)(2,1)S(1)} %get-tuple-element.68), channel_id=1, source_target_pairs={{16,32},{24,40},{32,16},{40,24},{48,64},{56,72},{64,48},{72,56},{8... | collective-permute-start | bytes 1179656 | tf_op jit(solution)/shard_map/ppermute | solution.py:132
  92.6 0.8 copy-done.13
  93.8 7.7 %collective-permute-done.19 = bf16[512,384]{1,0:T(8,128)(2,1)S(1)} collective-permute-done((bf16[512,384]{1,0:T(8,128)(2,1)S(1)}, bf16[512,384]{1,0:T(8,128)(2,1)S(1)}, u32[]{:S(2)}, u32[]{:S(2)}) %collective-permute-start.19) | collective-permute-done | bytes 393248 | tf_op jit(solution)/shard_map/ppermute | solution.py:132
  101.5 4.0 %collective-permute-done.21 = bf16[512,384]{1,0:T(8,128)(2,1)S(1)} collective-permute-done((bf16[512,384]{1,0:T(8,128)(2,1)S(1)}, bf16[512,384]{1,0:T(8,128)(2,1)S(1)}, u32[]{:S(2)}, u32[]{:S(2)}) %collective-permute-start.21) | collective-permute-done | bytes 393248 | tf_op jit(solution)/shard_map/ppermute | solution.py:132
  105.5 0.4 fusion.11
  106.2 2.0 %collective-permute-start.26 = (f32[2,512]{1,0:T(2,128)S(1)}, f32[2,512]{1,0:T(2,128)S(1)}, u32[]{:S(2)}, u32[]{:S(2)}) collective-permute-start(f32[2,512]{1,0:T(2,128)S(1)} %pad_maximum_fusion), channel_id=1, source_target_pairs={{0,1},{1,2},{2,3},{3,4},{4,5},{5,6},{6,7},{7,0},{8,9},{9,10},{10,1... | collective-permute-start | bytes 12296 | tf_op jit(solution)/shard_map/ppermute | solution.py:137
  108.3 2.2 %collective-permute-start.31 = (bf16[512,384]{1,0:T(8,128)(2,1)S(1)}, bf16[512,384]{1,0:T(8,128)(2,1)S(1)}, u32[]{:S(2)}, u32[]{:S(2)}) collective-permute-start(bf16[512,384]{1,0:T(8,128)(2,1)S(1)} %get-tuple-element.56), channel_id=1, source_target_pairs={{16,32},{24,40},{32,16},{40,24},{48,64},{56,72},{64,48},{72,56},{8... | collective-permute-start | bytes 1179656 | tf_op jit(solution)/shard_map/ppermute | solution.py:132
  110.6 0.6 collective-permute-done.26
  111.1 2.5 %collective-permute-start.27 = (f32[2,512]{1,0:T(2,128)S(1)}, f32[2,512]{1,0:T(2,128)S(1)}, u32[]{:S(2)}, u32[]{:S(2)}) collective-permute-start(f32[2,512]{1,0:T(2,128)S(1)} %get-tuple-element.62), channel_id=1, source_target_pairs={{0,5},{1,6},{2,7},{3,0},{4,1},{5,2},{6,3},{7,4},{8,13},{9,14},{10,... | collective-permute-start | bytes 12296 | tf_op jit(solution)/shard_map/ppermute | solution.py:137
  113.6 1.4 %collective-permute-start.28 = (f32[2,512]{1,0:T(2,128)S(1)}, f32[2,512]{1,0:T(2,128)S(1)}, u32[]{:S(2)}, u32[]{:S(2)}) collective-permute-start(f32[2,512]{1,0:T(2,128)S(1)} %get-tuple-element.63), channel_id=1, source_target_pairs={{0,3},{1,4},{2,5},{3,6},{4,7},{5,0},{6,1},{7,2},{8,11},{9,12},{10,... | collective-permute-start | bytes 12296 | tf_op jit(solution)/shard_map/ppermute | solution.py:137
  115.0 1.6 %collective-permute-done.27 = f32[2,512]{1,0:T(2,128)S(1)} collective-permute-done((f32[2,512]{1,0:T(2,128)S(1)}, f32[2,512]{1,0:T(2,128)S(1)}, u32[]{:S(2)}, u32[]{:S(2)}) %collective-permute-start.27) | collective-permute-done | bytes 4128 | tf_op jit(solution)/shard_map/ppermute | solution.py:137
  116.6 3.6 %collective-permute-done.28 = f32[2,512]{1,0:T(2,128)S(1)} collective-permute-done((f32[2,512]{1,0:T(2,128)S(1)}, f32[2,512]{1,0:T(2,128)S(1)}, u32[]{:S(2)}, u32[]{:S(2)}) %collective-permute-start.28) | collective-permute-done | bytes 4128 | tf_op jit(solution)/shard_map/ppermute | solution.py:137
  120.2 3.5 %collective-permute-done.31 = bf16[512,384]{1,0:T(8,128)(2,1)S(1)} collective-permute-done((bf16[512,384]{1,0:T(8,128)(2,1)S(1)}, bf16[512,384]{1,0:T(8,128)(2,1)S(1)}, u32[]{:S(2)}, u32[]{:S(2)}) %collective-permute-start.31) | collective-permute-done | bytes 393248 | tf_op jit(solution)/shard_map/ppermute | solution.py:132
  123.8 0.9 add_convert_fusion
  124.7 1.5 %fusion.15 = (bf16[512,384]{1,0:T(8,128)(2,1)}, bf16[512,384]{1,0:T(8,128)(2,1)}) fusion(bf16[512,384]{1,0:T(8,128)(2,1)S(1)} %copy-done.4, f32[512]{0:T(512)S(1)} %bitcast.40, f32[512]{0:T(512)S(1)} %multiply_multiply_fusion, f32[384]{0:T(512)S(1)} %copy-done.16, f32[512]{0:T(512)S(1)} %bitcast.35, bf16[512,384]{1,0:T(8,128)(2,1)S(1)} %collective-permute-done.21, ...), kind=kLoop, calls=%fused_computation.26 | loop fusion | flops 4521984 | bytes 3947520 | tf_op jit(solution)/shard_map/convert_element_type | solution.py:234
  (91 shorter events, 3.3 us)
Async XLA Ops:
  0.6 14.2 %copy-start = (s32[32,7,4,4]{0,3,2,1:T(4,128)S(1)}, s32[32,7,4,4]{0,3,2,1:T(4,128)}, u32[]{:S(2)}) copy-start(s32[32,7,4,4]{0,3,2,1:T(4,128)} %param.12) | copy-start | bytes 43012
  0.6 5.7 %collective-permute-start = (bf16[512,384]{1,0:T(8,128)(2,1)}, bf16[512,384]{1,0:T(8,128)(2,1)}, u32[]{:S(2)}, u32[]{:S(2)}) collective-permute-start(bf16[512,384]{1,0:T(8,128)(2,1)} %refs_7_.1), channel_id=1, source_target_pairs={{0,8},{8,0},{16,24},{24,16},{32,40},{40,32},{48,56},{56,48},{64,72... | collective-permute-start | bytes 1179656 | tf_op jit(solution)/shard_map/ppermute | solution.py:147
  0.7 31.2 %collective-permute-start.11 = (bf16[512,384]{1,0:T(8,128)(2,1)}, bf16[512,384]{1,0:T(8,128)(2,1)S(1)}, u32[]{:S(2)}, u32[]{:S(2)}) collective-permute-start(bf16[512,384]{1,0:T(8,128)(2,1)} %refs_7_.1), channel_id=1, source_target_pairs={{0,16},{8,24},{16,0},{24,8},{32,48},{40,56},{48,32},{56,40},{64,80... | collective-permute-start | bytes 1179656 | tf_op jit(solution)/shard_map/ppermute | solution.py:132
  2.3 29.7 %collective-permute-start.12 = (bf16[512,384]{1,0:T(8,128)(2,1)}, bf16[512,384]{1,0:T(8,128)(2,1)S(1)}, u32[]{:S(2)}, u32[]{:S(2)}) collective-permute-start(bf16[512,384]{1,0:T(8,128)(2,1)} %refs_7_.1), channel_id=1, source_target_pairs={{16,32},{24,40},{32,16},{40,24},{48,64},{56,72},{64,48},{72,56},{8... | collective-permute-start | bytes 1179656 | tf_op jit(solution)/shard_map/ppermute | solution.py:132
  6.4 1.0 copy-start.1
  7.4 1.0 copy-start.3
  8.4 18.6 %copy-start.4 = (bf16[512,384]{1,0:T(8,128)(2,1)S(1)}, bf16[512,384]{1,0:T(8,128)(2,1)}, u32[]{:S(2)}) copy-start(bf16[512,384]{1,0:T(8,128)(2,1)} %refs_1_) | copy-start | bytes 1179652
  8.9 7.2 %collective-permute-start.1 = (f32[2,512]{1,0:T(2,128)S(1)}, f32[2,512]{1,0:T(2,128)S(1)}, u32[]{:S(2)}, u32[]{:S(2)}) collective-permute-start(f32[2,512]{1,0:T(2,128)S(1)} %row_squares.1), channel_id=1, source_target_pairs={{0,7},{1,0},{2,1},{3,2},{4,3},{5,4},{6,5},{7,6},{8,15},{9,8},{10,9... | collective-permute-start | bytes 12296 | tf_op jit(solution)/shard_map/ppermute | solution.py:137
  14.8 4.8 %collective-permute-start.2 = (f32[2,512]{1,0:T(2,128)S(1)}, f32[2,512]{1,0:T(2,128)S(1)}, u32[]{:S(2)}, u32[]{:S(2)}) collective-permute-start(f32[2,512]{1,0:T(2,128)S(1)} %row_squares.1), channel_id=1, source_target_pairs={{0,1},{1,2},{2,3},{3,4},{4,5},{5,6},{6,7},{7,0},{8,9},{9,10},{10,1... | collective-permute-start | bytes 12296 | tf_op jit(solution)/shard_map/ppermute | solution.py:137
  19.6 5.4 %collective-permute-start.3 = (f32[2,512]{1,0:T(2,128)S(1)}, f32[2,512]{1,0:T(2,128)S(1)}, u32[]{:S(2)}, u32[]{:S(2)}) collective-permute-start(f32[2,512]{1,0:T(2,128)S(1)} %get-tuple-element.64), channel_id=1, source_target_pairs={{0,5},{1,6},{2,7},{3,0},{4,1},{5,2},{6,3},{7,4},{8,13},{9,14},{10,... | collective-permute-start | bytes 12296 | tf_op jit(solution)/shard_map/ppermute | solution.py:137
  20.3 6.6 %collective-permute-start.4 = (f32[2,512]{1,0:T(2,128)S(1)}, f32[2,512]{1,0:T(2,128)S(1)}, u32[]{:S(2)}, u32[]{:S(2)}) collective-permute-start(f32[2,512]{1,0:T(2,128)S(1)} %get-tuple-element.65), channel_id=1, source_target_pairs={{0,3},{1,4},{2,5},{3,6},{4,7},{5,0},{6,1},{7,2},{8,11},{9,12},{10,... | collective-permute-start | bytes 12296 | tf_op jit(solution)/shard_map/ppermute | solution.py:137
  27.8 8.4 %copy-start.7 = (bf16[512,384]{1,0:T(8,128)(2,1)}, bf16[512,384]{1,0:T(8,128)(2,1)S(1)}, u32[]{:S(2)}) copy-start(bf16[512,384]{1,0:T(8,128)(2,1)S(1)} %fusion.9.refs_0_) | copy-start | bytes 1179652
  27.8 8.4 %collective-permute-start.5 = (bf16[512,384]{1,0:T(8,128)(2,1)S(1)}, bf16[512,384]{1,0:T(8,128)(2,1)S(1)}, u32[]{:S(2)}, u32[]{:S(2)}) collective-permute-start(bf16[512,384]{1,0:T(8,128)(2,1)S(1)} %fusion.9.refs_0_), channel_id=1, source_target_pairs={{0,16},{8,24},{16,0},{24,8},{32,48},{40,56},{48,32},{56,40},{64,80... | collective-permute-start | bytes 1179656 | tf_op jit(solution)/shard_map/ppermute | solution.py:132
  28.6 13.5 %collective-permute-start.6 = (bf16[512,384]{1,0:T(8,128)(2,1)S(1)}, bf16[512,384]{1,0:T(8,128)(2,1)S(1)}, u32[]{:S(2)}, u32[]{:S(2)}) collective-permute-start(bf16[512,384]{1,0:T(8,128)(2,1)S(1)} %fusion.9.refs_0_), channel_id=1, source_target_pairs={{16,32},{24,40},{32,16},{40,24},{48,64},{56,72},{64,48},{72,56},{8... | collective-permute-start | bytes 1179656 | tf_op jit(solution)/shard_map/ppermute | solution.py:132
  32.0 2.0 %copy-start.8 = (bf16[512,384]{1,0:T(8,128)(2,1)}, bf16[512,384]{1,0:T(8,128)(2,1)S(1)}, u32[]{:S(2)}) copy-start(bf16[512,384]{1,0:T(8,128)(2,1)S(1)} %collective-permute-done.11.refs_8_) | copy-start | bytes 1179652
  32.0 3.7 %copy-start.9 = (bf16[512,384]{1,0:T(8,128)(2,1)}, bf16[512,384]{1,0:T(8,128)(2,1)S(1)}, u32[]{:S(2)}) copy-start(bf16[512,384]{1,0:T(8,128)(2,1)S(1)} %collective-permute-done.12.refs_9_) | copy-start | bytes 1179652
  32.1 12.8 %collective-permute-start.15 = (bf16[512,384]{1,0:T(8,128)(2,1)S(1)}, bf16[512,384]{1,0:T(8,128)(2,1)S(1)}, u32[]{:S(2)}, u32[]{:S(2)}) collective-permute-start(bf16[512,384]{1,0:T(8,128)(2,1)S(1)} %broadcast_select_fusion), channel_id=1, source_target_pairs={{8,16},{16,8},{24,32},{32,24},{40,48},{48,40},{56,64},{64,56},{72,... | collective-permute-start | bytes 1179656 | tf_op jit(solution)/shard_map/ppermute | solution.py:153
  34.0 10.8 %collective-permute-start.13 = (bf16[512,384]{1,0:T(8,128)(2,1)S(1)}, bf16[512,384]{1,0:T(8,128)(2,1)S(1)}, u32[]{:S(2)}, u32[]{:S(2)}) collective-permute-start(bf16[512,384]{1,0:T(8,128)(2,1)S(1)} %collective-permute-done.11.refs_8_), channel_id=1, source_target_pairs={{0,8},{8,0},{16,24},{24,16},{32,40},{40,32},{48,56},{56,48},{64,72... | collective-permute-start | bytes 1179656 | tf_op jit(solution)/shard_map/ppermute | solution.py:147
  35.7 12.6 %collective-permute-start.14 = (bf16[512,384]{1,0:T(8,128)(2,1)S(1)}, bf16[512,384]{1,0:T(8,128)(2,1)}, u32[]{:S(2)}, u32[]{:S(2)}) collective-permute-start(bf16[512,384]{1,0:T(8,128)(2,1)S(1)} %collective-permute-done.12.refs_9_), channel_id=1, source_target_pairs={{0,8},{8,0},{16,24},{24,16},{32,40},{40,32},{48,56},{56,48},{64,72... | collective-permute-start | bytes 1179656 | tf_op jit(solution)/shard_map/ppermute | solution.py:147
  36.2 8.6 %copy-start.10 = (bf16[512,384]{1,0:T(8,128)(2,1)}, bf16[512,384]{1,0:T(8,128)(2,1)S(1)}, u32[]{:S(2)}) copy-start(bf16[512,384]{1,0:T(8,128)(2,1)S(1)} %collective-permute-done.5.refs_1_) | copy-start | bytes 1179652
  36.2 12.1 %collective-permute-start.7 = (bf16[512,384]{1,0:T(8,128)(2,1)S(1)}, bf16[512,384]{1,0:T(8,128)(2,1)}, u32[]{:S(2)}, u32[]{:S(2)}) collective-permute-start(bf16[512,384]{1,0:T(8,128)(2,1)S(1)} %fusion.9.refs_0_), channel_id=1, source_target_pairs={{0,8},{8,0},{16,24},{24,16},{32,40},{40,32},{48,56},{56,48},{64,72... | collective-permute-start | bytes 1179656 | tf_op jit(solution)/shard_map/ppermute | solution.py:147
  42.1 2.7 %copy-start.11 = (bf16[512,384]{1,0:T(8,128)(2,1)}, bf16[512,384]{1,0:T(8,128)(2,1)S(1)}, u32[]{:S(2)}) copy-start(bf16[512,384]{1,0:T(8,128)(2,1)S(1)} %collective-permute-done.6.refs_2_) | copy-start | bytes 1179652
  42.2 4.5 %copy-start.2 = (bf16[512,384]{1,0:T(8,128)(2,1)S(1)}, bf16[512,384]{1,0:T(8,128)(2,1)}, u32[]{:S(2)}) copy-start(bf16[512,384]{1,0:T(8,128)(2,1)} %refs_0_.1) | copy-start | bytes 1179652
  42.2 11.4 %collective-permute-start.10 = (bf16[512,384]{1,0:T(8,128)(2,1)S(1)}, bf16[512,384]{1,0:T(8,128)(2,1)}, u32[]{:S(2)}, u32[]{:S(2)}) collective-permute-start(bf16[512,384]{1,0:T(8,128)(2,1)S(1)} %broadcast_select_fusion.1), channel_id=1, source_target_pairs={{8,16},{16,8},{24,32},{32,24},{40,48},{48,40},{56,64},{64,56},{72,... | collective-permute-start | bytes 1179656 | tf_op jit(solution)/shard_map/ppermute | solution.py:153
  44.9 8.8 %collective-permute-start.8 = (bf16[512,384]{1,0:T(8,128)(2,1)S(1)}, bf16[512,384]{1,0:T(8,128)(2,1)}, u32[]{:S(2)}, u32[]{:S(2)}) collective-permute-start(bf16[512,384]{1,0:T(8,128)(2,1)S(1)} %collective-permute-done.5.refs_1_), channel_id=1, source_target_pairs={{0,8},{8,0},{16,24},{24,16},{32,40},{40,32},{48,56},{56,48},{64,72... | collective-permute-start | bytes 1179656 | tf_op jit(solution)/shard_map/ppermute | solution.py:147
  44.9 8.8 %collective-permute-start.9 = (bf16[512,384]{1,0:T(8,128)(2,1)S(1)}, bf16[512,384]{1,0:T(8,128)(2,1)}, u32[]{:S(2)}, u32[]{:S(2)}) collective-permute-start(bf16[512,384]{1,0:T(8,128)(2,1)S(1)} %collective-permute-done.6.refs_2_), channel_id=1, source_target_pairs={{0,8},{8,0},{16,24},{24,16},{32,40},{40,32},{48,56},{56,48},{64,72... | collective-permute-start | bytes 1179656 | tf_op jit(solution)/shard_map/ppermute | solution.py:147
  76.8 8.4 %collective-permute-start.17 = (bf16[512,384]{1,0:T(8,128)(2,1)}, bf16[512,384]{1,0:T(8,128)(2,1)S(1)}, u32[]{:S(2)}, u32[]{:S(2)}) collective-permute-start(bf16[512,384]{1,0:T(8,128)(2,1)} %get-tuple-element.40), channel_id=1, source_target_pairs={{0,8},{8,0},{16,24},{24,16},{32,40},{40,32},{48,56},{56,48},{64,72... | collective-permute-start | bytes 1179656 | tf_op jit(solution)/shard_map/ppermute | solution.py:147
  76.9 11.4 %collective-permute-start.18 = (bf16[512,384]{1,0:T(8,128)(2,1)}, bf16[512,384]{1,0:T(8,128)(2,1)S(1)}, u32[]{:S(2)}, u32[]{:S(2)}) collective-permute-start(bf16[512,384]{1,0:T(8,128)(2,1)} %get-tuple-element.41), channel_id=1, source_target_pairs={{8,16},{16,8},{24,32},{32,24},{40,48},{48,40},{56,64},{64,56},{72,... | collective-permute-start | bytes 1179656 | tf_op jit(solution)/shard_map/ppermute | solution.py:153
  78.9 9.5 %collective-permute-start.20 = (bf16[512,384]{1,0:T(8,128)(2,1)}, bf16[512,384]{1,0:T(8,128)(2,1)S(1)}, u32[]{:S(2)}, u32[]{:S(2)}) collective-permute-start(bf16[512,384]{1,0:T(8,128)(2,1)} %get-tuple-element.43), channel_id=1, source_target_pairs={{0,8},{8,0},{16,24},{24,16},{32,40},{40,32},{48,56},{56,48},{64,72... | collective-permute-start | bytes 1179656 | tf_op jit(solution)/shard_map/ppermute | solution.py:147
  79.4 10.6 %collective-permute-start.22 = (bf16[512,384]{1,0:T(8,128)(2,1)}, bf16[512,384]{1,0:T(8,128)(2,1)S(1)}, u32[]{:S(2)}, u32[]{:S(2)}) collective-permute-start(bf16[512,384]{1,0:T(8,128)(2,1)} %get-tuple-element.45), channel_id=1, source_target_pairs={{0,8},{8,0},{16,24},{24,16},{32,40},{40,32},{48,56},{56,48},{64,72... | collective-permute-start | bytes 1179656 | tf_op jit(solution)/shard_map/ppermute | solution.py:147
  79.5 13.0 %collective-permute-start.23 = (bf16[512,384]{1,0:T(8,128)(2,1)}, bf16[512,384]{1,0:T(8,128)(2,1)S(1)}, u32[]{:S(2)}, u32[]{:S(2)}) collective-permute-start(bf16[512,384]{1,0:T(8,128)(2,1)} %get-tuple-element.46), channel_id=1, source_target_pairs={{8,16},{16,8},{24,32},{32,24},{40,48},{48,40},{56,64},{64,56},{72,... | collective-permute-start | bytes 1179656 | tf_op jit(solution)/shard_map/ppermute | solution.py:153
  85.2 7.3 %collective-permute-start.24 = (bf16[512,384]{1,0:T(8,128)(2,1)}, bf16[512,384]{1,0:T(8,128)(2,1)S(1)}, u32[]{:S(2)}, u32[]{:S(2)}) collective-permute-start(bf16[512,384]{1,0:T(8,128)(2,1)} %get-tuple-element.48), channel_id=1, source_target_pairs={{0,8},{8,0},{16,24},{24,16},{32,40},{40,32},{48,56},{56,48},{64,72... | collective-permute-start | bytes 1179656 | tf_op jit(solution)/shard_map/ppermute | solution.py:147
  88.3 5.4 %collective-permute-start.16 = (bf16[512,384]{1,0:T(8,128)(2,1)}, bf16[512,384]{1,0:T(8,128)(2,1)S(1)}, u32[]{:S(2)}, u32[]{:S(2)}) collective-permute-start(bf16[512,384]{1,0:T(8,128)(2,1)} %get-tuple-element.38), channel_id=1, source_target_pairs={{0,8},{8,0},{16,24},{24,16},{32,40},{40,32},{48,56},{56,48},{64,72... | collective-permute-start | bytes 1179656 | tf_op jit(solution)/shard_map/ppermute | solution.py:147
  88.4 4.0 %copy-start.5 = (f32[512,384]{1,0:T(8,128)S(1)}, f32[512,384]{1,0:T(8,128)}, u32[]{:S(2)}) copy-start(f32[512,384]{1,0:T(8,128)} %get-tuple-element.36) | copy-start | bytes 2359300
  89.9 11.6 %collective-permute-start.19 = (bf16[512,384]{1,0:T(8,128)(2,1)S(1)}, bf16[512,384]{1,0:T(8,128)(2,1)S(1)}, u32[]{:S(2)}, u32[]{:S(2)}) collective-permute-start(bf16[512,384]{1,0:T(8,128)(2,1)S(1)} %get-tuple-element.69), channel_id=1, source_target_pairs={{0,16},{8,24},{16,0},{24,8},{32,48},{40,56},{48,32},{56,40},{64,80... | collective-permute-start | bytes 1179656 | tf_op jit(solution)/shard_map/ppermute | solution.py:132
  90.0 15.5 %collective-permute-start.21 = (bf16[512,384]{1,0:T(8,128)(2,1)S(1)}, bf16[512,384]{1,0:T(8,128)(2,1)S(1)}, u32[]{:S(2)}, u32[]{:S(2)}) collective-permute-start(bf16[512,384]{1,0:T(8,128)(2,1)S(1)} %get-tuple-element.68), channel_id=1, source_target_pairs={{16,32},{24,40},{32,16},{40,24},{48,64},{56,72},{64,48},{72,56},{8... | collective-permute-start | bytes 1179656 | tf_op jit(solution)/shard_map/ppermute | solution.py:132
  92.3 1.0 copy-start.13
  92.3 1.1 copy-start.14
  93.4 12.1 %copy-start.6 = (bf16[512,384]{1,0:T(8,128)(2,1)S(1)}, bf16[512,384]{1,0:T(8,128)(2,1)}, u32[]{:S(2)}) copy-start(bf16[512,384]{1,0:T(8,128)(2,1)} %get-tuple-element.49) | copy-start | bytes 1179652
  105.5 2.7 %copy-start.17 = (bf16[512,384]{1,0:T(8,128)(2,1)S(1)}, bf16[512,384]{1,0:T(8,128)(2,1)}, u32[]{:S(2)}) copy-start(bf16[512,384]{1,0:T(8,128)(2,1)} %get-tuple-element.54) | copy-start | bytes 1179652
  105.5 18.3 %copy-start.12 = (bf16[512,384]{1,0:T(8,128)(2,1)S(1)}, bf16[512,384]{1,0:T(8,128)(2,1)}, u32[]{:S(2)}) copy-start(bf16[512,384]{1,0:T(8,128)(2,1)} %get-tuple-element.58) | copy-start | bytes 1179652
  105.9 4.6 %collective-permute-start.25 = (f32[2,512]{1,0:T(2,128)S(1)}, f32[2,512]{1,0:T(2,128)S(1)}, u32[]{:S(2)}, u32[]{:S(2)}) collective-permute-start(f32[2,512]{1,0:T(2,128)S(1)} %pad_maximum_fusion), channel_id=1, source_target_pairs={{0,7},{1,0},{2,1},{3,2},{4,3},{5,4},{6,5},{7,6},{8,15},{9,8},{10,9... | collective-permute-start | bytes 12296 | tf_op jit(solution)/shard_map/ppermute | solution.py:137
  106.2 4.9 %collective-permute-start.26 = (f32[2,512]{1,0:T(2,128)S(1)}, f32[2,512]{1,0:T(2,128)S(1)}, u32[]{:S(2)}, u32[]{:S(2)}) collective-permute-start(f32[2,512]{1,0:T(2,128)S(1)} %pad_maximum_fusion), channel_id=1, source_target_pairs={{0,1},{1,2},{2,3},{3,4},{4,5},{5,6},{6,7},{7,0},{8,9},{9,10},{10,1... | collective-permute-start | bytes 12296 | tf_op jit(solution)/shard_map/ppermute | solution.py:137
  108.2 12.0 %collective-permute-start.29 = (bf16[512,384]{1,0:T(8,128)(2,1)S(1)}, bf16[512,384]{1,0:T(8,128)(2,1)S(1)}, u32[]{:S(2)}, u32[]{:S(2)}) collective-permute-start(bf16[512,384]{1,0:T(8,128)(2,1)S(1)} %copy-done.17), channel_id=1, source_target_pairs={{0,8},{8,0},{16,24},{24,16},{32,40},{40,32},{48,56},{56,48},{64,72... | collective-permute-start | bytes 1179656 | tf_op jit(solution)/shard_map/ppermute | solution.py:147
  108.2 12.0 %collective-permute-start.30 = (bf16[512,384]{1,0:T(8,128)(2,1)S(1)}, bf16[512,384]{1,0:T(8,128)(2,1)S(1)}, u32[]{:S(2)}, u32[]{:S(2)}) collective-permute-start(bf16[512,384]{1,0:T(8,128)(2,1)S(1)} %get-tuple-element.55), channel_id=1, source_target_pairs={{0,16},{8,24},{16,0},{24,8},{32,48},{40,56},{48,32},{56,40},{64,80... | collective-permute-start | bytes 1179656 | tf_op jit(solution)/shard_map/ppermute | solution.py:132
  108.3 15.5 %collective-permute-start.31 = (bf16[512,384]{1,0:T(8,128)(2,1)S(1)}, bf16[512,384]{1,0:T(8,128)(2,1)S(1)}, u32[]{:S(2)}, u32[]{:S(2)}) collective-permute-start(bf16[512,384]{1,0:T(8,128)(2,1)S(1)} %get-tuple-element.56), channel_id=1, source_target_pairs={{16,32},{24,40},{32,16},{40,24},{48,64},{56,72},{64,48},{72,56},{8... | collective-permute-start | bytes 1179656 | tf_op jit(solution)/shard_map/ppermute | solution.py:132
  111.1 5.5 %collective-permute-start.27 = (f32[2,512]{1,0:T(2,128)S(1)}, f32[2,512]{1,0:T(2,128)S(1)}, u32[]{:S(2)}, u32[]{:S(2)}) collective-permute-start(f32[2,512]{1,0:T(2,128)S(1)} %get-tuple-element.62), channel_id=1, source_target_pairs={{0,5},{1,6},{2,7},{3,0},{4,1},{5,2},{6,3},{7,4},{8,13},{9,14},{10,... | collective-permute-start | bytes 12296 | tf_op jit(solution)/shard_map/ppermute | solution.py:137
  113.6 6.6 %collective-permute-start.28 = (f32[2,512]{1,0:T(2,128)S(1)}, f32[2,512]{1,0:T(2,128)S(1)}, u32[]{:S(2)}, u32[]{:S(2)}) collective-permute-start(f32[2,512]{1,0:T(2,128)S(1)} %get-tuple-element.63), channel_id=1, source_target_pairs={{0,3},{1,4},{2,5},{3,6},{4,7},{5,0},{6,1},{7,2},{8,11},{9,12},{10,... | collective-permute-start | bytes 12296 | tf_op jit(solution)/shard_map/ppermute | solution.py:137
  (4 other events, 3.0 us)

commit v3 on v2

--- a/solution.py
+++ b/solution.py
@@ -132,15 +132,11 @@
     return lax.ppermute(value, "tm", [(a, b) for a, b in pairs if 0 <= b < count])
 
 
-def turned(value, steps):
-    count = lax.axis_size("head")
-    return lax.ppermute(value, "head", [(s, (s + steps) % count) for s in range(count)])
-
-
 def ring_sum(value):
-    after, before = turned(value, -1), turned(value, 1)
-    pair = value + after
-    return pair + before + turned(pair + before, -3) + turned(pair, 3)
+    rounds = ((1, 0, 3, 2, 5, 4, 7, 6), (7, 2, 1, 4, 3, 6, 5, 0), (3, 6, 5, 0, 7, 2, 1, 4))
+    for partners in rounds:
+        value = value + lax.ppermute(value, "head", list(enumerate(partners)))
+    return value
 
 
 def swapped(value):

time: 127 us -> 130 us (1.024)
  waiting for transfers between devices: 43.4 us -> 45.8 us
    ppermute x8, waiting for transfers between devices: 21.4 us -> 24.7 us  [across(): lax.ppermute(value, 'tm', [(a, b) for a, b in pairs if 0 <= b < count])]
    ppermute x8 -> x6, waiting for transfers between devices: 13 us -> 12.1 us  [ring_sum(): value = value + lax.ppermute(value, 'head', list(enumerate(partners)))]
    ppermute x8 -> x6, starting transfers between devices: 15.9 us -> 16 us  [ring_sum(): value = value + lax.ppermute(value, 'head', list(enumerate(partners)))]
  transfers between devices with their start and end apart: 32 -> 30, of which waited for: 15 -> 14; matrix products, arithmetic and copies ran while one was open for 4% -> 4% of each run, Pallas kernels for 0% -> 0%
where the time goes in v3:
time: 130 us; the launch traced here: 129 us
  starting transfers between devices  45.9 us (35%)
  waiting for transfers between devices  45.8 us (35%)
  Pallas kernels  23.7 us (18%)
  local copies, waits for them, and re-layouts  6.39 us (5%)
  other arithmetic  6.22 us (5%)
    ppermute x8, waiting for transfers between devices, across(): lax.ppermute(value, 'tm', [(a, b) for a, b in pairs if 0 <= b < count])  24.7 us
    pallas_call x1, Pallas kernels, head_call(): pl.pallas_call(head_kernel, grid=(width // BLK,), in_specs=[pl.BlockSpec(...  23.1 us
    ppermute x6, starting transfers between devices, ring_sum(): value = value + lax.ppermute(value, 'head', list(enumerate(partners)))  16 us
    ppermute x8, starting transfers between devices, across(): lax.ppermute(value, 'tm', [(a, b) for a, b in pairs if 0 <= b < count])  14.3 us
    ppermute x6, waiting for transfers between devices, ring_sum(): value = value + lax.ppermute(value, 'head', list(enumerate(partners)))  12.1 us
    ppermute x4, starting transfers between devices, outward(): lax.ppermute(value, 'tm', [(a, b) for a, b in pairs if 0 <= b < count])  11.6 us
    ppermute x4, waiting for transfers between devices, outward(): lax.ppermute(value, 'tm', [(a, b) for a, b in pairs if 0 <= b < count])  8.92 us
    unnamed x42, local copies, waits for them, and re-layouts  5.02 us
  transfers between devices with their start and end apart: 30, of which 14 were waited for; matrix products, arithmetic and copies ran while one was open for 4% of the time, Pallas kernels for 0%

profile of v3, /device:TPU:8, one launch (start us, length us, event | category | flops | bytes accessed | tf_op | source)
XLA Modules:
  0.0 129.1 jit_solution(13775443385608351170)
XLA Ops:
  0.7 1.6 %collective-permute-start.10 = (bf16[512,384]{1,0:T(8,128)(2,1)}, bf16[512,384]{1,0:T(8,128)(2,1)S(1)}, u32[]{:S(2)}, u32[]{:S(2)}) collective-permute-start(bf16[512,384]{1,0:T(8,128)(2,1)} %refs_7_.1), channel_id=1, source_target_pairs={{0,16},{8,24},{16,0},{24,8},{32,48},{40,56},{48,32},{56,40},{64,80... | collective-permute-start | bytes 1179656 | tf_op jit(solution)/shard_map/ppermute | solution.py:132
  2.3 3.9 %collective-permute-start.11 = (bf16[512,384]{1,0:T(8,128)(2,1)}, bf16[512,384]{1,0:T(8,128)(2,1)S(1)}, u32[]{:S(2)}, u32[]{:S(2)}) collective-permute-start(bf16[512,384]{1,0:T(8,128)(2,1)} %refs_7_.1), channel_id=1, source_target_pairs={{16,32},{24,40},{32,16},{40,24},{48,64},{56,72},{64,48},{72,56},{8... | collective-permute-start | bytes 1179656 | tf_op jit(solution)/shard_map/ppermute | solution.py:132
  6.4 1.0 copy-done.1
  7.4 1.0 copy-done.3
  8.4 0.5 row_squares.1
  8.9 1.9 %collective-permute-start.1 = (f32[2,512]{1,0:T(2,128)S(1)}, f32[2,512]{1,0:T(2,128)S(1)}, u32[]{:S(2)}, u32[]{:S(2)}) collective-permute-start(f32[2,512]{1,0:T(2,128)S(1)} %row_squares.1), channel_id=1, source_target_pairs={{0,1},{1,0},{2,3},{3,2},{4,5},{5,4},{6,7},{7,6},{8,9},{9,8},{10,11... | collective-permute-start | bytes 12296 | tf_op jit(solution)/shard_map/ppermute | solution.py:138
  10.8 1.7 %collective-permute-done.1 = f32[2,512]{1,0:T(2,128)S(1)} collective-permute-done((f32[2,512]{1,0:T(2,128)S(1)}, f32[2,512]{1,0:T(2,128)S(1)}, u32[]{:S(2)}, u32[]{:S(2)}) %collective-permute-start.1) | collective-permute-done | bytes 4128 | tf_op jit(solution)/shard_map/ppermute | solution.py:138
  12.5 5.9 %collective-permute-start.2 = (f32[2,512]{1,0:T(2,128)S(1)}, f32[2,512]{1,0:T(2,128)S(1)}, u32[]{:S(2)}, u32[]{:S(2)}) collective-permute-start(f32[2,512]{1,0:T(2,128)S(1)} %add.126), channel_id=1, source_target_pairs={{0,7},{1,2},{2,1},{3,4},{4,3},{5,6},{6,5},{7,0},{8,15},{9,10},{10,... | collective-permute-start | bytes 12296 | tf_op jit(solution)/shard_map/ppermute | solution.py:138
  18.5 1.5 %collective-permute-done.2 = f32[2,512]{1,0:T(2,128)S(1)} collective-permute-done((f32[2,512]{1,0:T(2,128)S(1)}, f32[2,512]{1,0:T(2,128)S(1)}, u32[]{:S(2)}, u32[]{:S(2)}) %collective-permute-start.2) | collective-permute-done | bytes 4128 | tf_op jit(solution)/shard_map/ppermute | solution.py:138
  20.0 2.0 %collective-permute-start.3 = (f32[2,512]{1,0:T(2,128)S(1)}, f32[2,512]{1,0:T(2,128)S(1)}, u32[]{:S(2)}, u32[]{:S(2)}) collective-permute-start(f32[2,512]{1,0:T(2,128)S(1)} %add.127), channel_id=1, source_target_pairs={{0,3},{1,6},{2,5},{3,0},{4,7},{5,2},{6,1},{7,4},{8,11},{9,14},{10,... | collective-permute-start | bytes 12296 | tf_op jit(solution)/shard_map/ppermute | solution.py:138
  22.3 0.6 gather_fusion
  22.9 2.5 %collective-permute-done.3 = f32[2,512]{1,0:T(2,128)S(1)} collective-permute-done((f32[2,512]{1,0:T(2,128)S(1)}, f32[2,512]{1,0:T(2,128)S(1)}, u32[]{:S(2)}, u32[]{:S(2)}) %collective-permute-start.3) | collective-permute-done | bytes 4128 | tf_op jit(solution)/shard_map/ppermute | solution.py:138
  25.4 0.7 copy-done.16
  26.3 0.8 collective-permute-start.4
  27.1 3.4 %collective-permute-start.5 = (bf16[512,384]{1,0:T(8,128)(2,1)S(1)}, bf16[512,384]{1,0:T(8,128)(2,1)S(1)}, u32[]{:S(2)}, u32[]{:S(2)}) collective-permute-start(bf16[512,384]{1,0:T(8,128)(2,1)S(1)} %fusion.9.refs_0_), channel_id=1, source_target_pairs={{16,32},{24,40},{32,16},{40,24},{48,64},{56,72},{64,48},{72,56},{8... | collective-permute-start | bytes 1179656 | tf_op jit(solution)/shard_map/ppermute | solution.py:132
  30.5 1.9 %collective-permute-start.14 = (bf16[512,384]{1,0:T(8,128)(2,1)S(1)}, bf16[512,384]{1,0:T(8,128)(2,1)S(1)}, u32[]{:S(2)}, u32[]{:S(2)}) collective-permute-start(bf16[512,384]{1,0:T(8,128)(2,1)S(1)} %broadcast_select_fusion), channel_id=1, source_target_pairs={{8,16},{16,8},{24,32},{32,24},{40,48},{48,40},{56,64},{64,56},{72,... | collective-permute-start | bytes 1179656 | tf_op jit(solution)/shard_map/ppermute | solution.py:149
  32.5 1.7 %collective-permute-start.12 = (bf16[512,384]{1,0:T(8,128)(2,1)S(1)}, bf16[512,384]{1,0:T(8,128)(2,1)S(1)}, u32[]{:S(2)}, u32[]{:S(2)}) collective-permute-start(bf16[512,384]{1,0:T(8,128)(2,1)S(1)} %collective-permute-done.10.refs_8_), channel_id=1, source_target_pairs={{0,8},{8,0},{16,24},{24,16},{32,40},{40,32},{48,56},{56,48},{64,72... | collective-permute-start | bytes 1179656 | tf_op jit(solution)/shard_map/ppermute | solution.py:143
  34.4 0.5 collective-permute-start.6
  34.9 5.2 %collective-permute-done.5.refs_2_ = bf16[512,384]{1,0:T(8,128)(2,1)S(1)} collective-permute-done((bf16[512,384]{1,0:T(8,128)(2,1)S(1)}, bf16[512,384]{1,0:T(8,128)(2,1)S(1)}, u32[]{:S(2)}, u32[]{:S(2)}) %collective-permute-start.5) | collective-permute-done | bytes 393248 | tf_op jit(solution)/shard_map/ppermute | solution.py:132
  40.1 2.1 %collective-permute-start.9 = (bf16[512,384]{1,0:T(8,128)(2,1)S(1)}, bf16[512,384]{1,0:T(8,128)(2,1)}, u32[]{:S(2)}, u32[]{:S(2)}) collective-permute-start(bf16[512,384]{1,0:T(8,128)(2,1)S(1)} %broadcast_select_fusion.1), channel_id=1, source_target_pairs={{8,16},{16,8},{24,32},{32,24},{40,48},{48,40},{56,64},{64,56},{72,... | collective-permute-start | bytes 1179656 | tf_op jit(solution)/shard_map/ppermute | solution.py:149
  42.2 0.9 collective-permute-done.14.refs_13_
  43.1 0.7 collective-permute-start.8
  44.3 0.6 copy.21
  44.9 0.7 copy-done.15
  45.6 1.0 fusion.18.refs_14_
  46.6 5.0 %collective-permute-done.9.refs_6_ = bf16[512,384]{1,0:T(8,128)(2,1)} collective-permute-done((bf16[512,384]{1,0:T(8,128)(2,1)S(1)}, bf16[512,384]{1,0:T(8,128)(2,1)}, u32[]{:S(2)}, u32[]{:S(2)}) %collective-permute-start.9) | collective-permute-done | bytes 393248 | tf_op jit(solution)/shard_map/ppermute | solution.py:149
  51.6 23.1 %head_attention.1 = (bf16[512,384]{1,0:T(8,128)(2,1)}, f32[512,384]{1,0:T(8,128)}, bf16[512,384]{1,0:T(8,128)(2,1)}, bf16[512,384]{1,0:T(8,128)(2,1)}, bf16[512,...) custom-call(f32[28,512]{1,0:T(8,128)} %bitcast.28, ...), custom_call_target="tpu_custom_call" | custom-call | flops 8999999488 | bytes 12000000 | tf_op jit(solution)/shard_map/head_attention/pallas_call | solution.py:105
  74.8 1.9 %collective-permute-start.17 = (bf16[512,384]{1,0:T(8,128)(2,1)}, bf16[512,384]{1,0:T(8,128)(2,1)S(1)}, u32[]{:S(2)}, u32[]{:S(2)}) collective-permute-start(bf16[512,384]{1,0:T(8,128)(2,1)} %get-tuple-element.41), channel_id=1, source_target_pairs={{8,16},{16,8},{24,32},{32,24},{40,48},{48,40},{56,64},{64,56},{72,... | collective-permute-start | bytes 1179656 | tf_op jit(solution)/shard_map/ppermute | solution.py:149
  76.8 0.6 collective-permute-start.19
  77.4 5.7 %collective-permute-start.22 = (bf16[512,384]{1,0:T(8,128)(2,1)}, bf16[512,384]{1,0:T(8,128)(2,1)S(1)}, u32[]{:S(2)}, u32[]{:S(2)}) collective-permute-start(bf16[512,384]{1,0:T(8,128)(2,1)} %get-tuple-element.46), channel_id=1, source_target_pairs={{8,16},{16,8},{24,32},{32,24},{40,48},{48,40},{56,64},{64,56},{72,... | collective-permute-start | bytes 1179656 | tf_op jit(solution)/shard_map/ppermute | solution.py:149
  83.2 3.0 %collective-permute-done.17 = bf16[512,384]{1,0:T(8,128)(2,1)S(1)} collective-permute-done((bf16[512,384]{1,0:T(8,128)(2,1)}, bf16[512,384]{1,0:T(8,128)(2,1)S(1)}, u32[]{:S(2)}, u32[]{:S(2)}) %collective-permute-start.17) | collective-permute-done | bytes 393248 | tf_op jit(solution)/shard_map/ppermute | solution.py:149
  86.3 1.5 %fusion.3 = (bf16[512,384]{1,0:T(8,128)(2,1)S(1)}, bf16[512,384]{1,0:T(8,128)(2,1)S(1)}) fusion(bf16[512,384]{1,0:T(8,128)(2,1)S(1)} %collective-permute-done.17, bf16[512,384]{1,0:T(8,128)(2,1)S(1)} %collective-permute-done.19, bf16[512,384]{1,0:T(8,128)(2,1)} %get-tuple-element.42, pred[]{:T(512)S(6)} %gt.9, ...), kind=kLoop, calls=%fused_computation.14 | loop fusion | flops 2555904 | bytes 2752513 | tf_op jit(solution)/shard_map/convert_element_type | solution.py:164
  87.9 2.3 %collective-permute-start.20 = (bf16[512,384]{1,0:T(8,128)(2,1)S(1)}, bf16[512,384]{1,0:T(8,128)(2,1)S(1)}, u32[]{:S(2)}, u32[]{:S(2)}) collective-permute-start(bf16[512,384]{1,0:T(8,128)(2,1)S(1)} %get-tuple-element.64), channel_id=1, source_target_pairs={{16,32},{24,40},{32,16},{40,24},{48,64},{56,72},{64,48},{72,56},{8... | collective-permute-start | bytes 1179656 | tf_op jit(solution)/shard_map/ppermute | solution.py:132
  90.5 0.8 copy-done.13
  91.4 0.3 fusion.7
  91.7 7.7 %collective-permute-done.18 = bf16[512,384]{1,0:T(8,128)(2,1)S(1)} collective-permute-done((bf16[512,384]{1,0:T(8,128)(2,1)S(1)}, bf16[512,384]{1,0:T(8,128)(2,1)S(1)}, u32[]{:S(2)}, u32[]{:S(2)}) %collective-permute-start.18) | collective-permute-done | bytes 393248 | tf_op jit(solution)/shard_map/ppermute | solution.py:132
  99.4 4.0 %collective-permute-done.20 = bf16[512,384]{1,0:T(8,128)(2,1)S(1)} collective-permute-done((bf16[512,384]{1,0:T(8,128)(2,1)S(1)}, bf16[512,384]{1,0:T(8,128)(2,1)S(1)}, u32[]{:S(2)}, u32[]{:S(2)}) %collective-permute-start.20) | collective-permute-done | bytes 393248 | tf_op jit(solution)/shard_map/ppermute | solution.py:132
  103.4 0.4 fusion.11
  103.8 0.9 collective-permute-start.24
  104.7 3.0 %collective-permute-done.24 = f32[2,512]{1,0:T(2,128)S(1)} collective-permute-done((f32[2,512]{1,0:T(2,128)S(1)}, f32[2,512]{1,0:T(2,128)S(1)}, u32[]{:S(2)}, u32[]{:S(2)}) %collective-permute-start.24) | collective-permute-done | bytes 4128 | tf_op jit(solution)/shard_map/ppermute | solution.py:138
  107.7 3.3 %collective-permute-start.25 = (f32[2,512]{1,0:T(2,128)S(1)}, f32[2,512]{1,0:T(2,128)S(1)}, u32[]{:S(2)}, u32[]{:S(2)}) collective-permute-start(f32[2,512]{1,0:T(2,128)S(1)} %fusion.26), channel_id=1, source_target_pairs={{0,7},{1,2},{2,1},{3,4},{4,3},{5,6},{6,5},{7,0},{8,15},{9,10},{10,... | collective-permute-start | bytes 12296 | tf_op jit(solution)/shard_map/ppermute | solution.py:138
  111.2 2.2 %collective-permute-start.29 = (bf16[512,384]{1,0:T(8,128)(2,1)S(1)}, bf16[512,384]{1,0:T(8,128)(2,1)S(1)}, u32[]{:S(2)}, u32[]{:S(2)}) collective-permute-start(bf16[512,384]{1,0:T(8,128)(2,1)S(1)} %get-tuple-element.56), channel_id=1, source_target_pairs={{16,32},{24,40},{32,16},{40,24},{48,64},{56,72},{64,48},{72,56},{8... | collective-permute-start | bytes 1179656 | tf_op jit(solution)/shard_map/ppermute | solution.py:132
  113.4 2.0 %collective-permute-start.26 = (f32[2,512]{1,0:T(2,128)S(1)}, f32[2,512]{1,0:T(2,128)S(1)}, u32[]{:S(2)}, u32[]{:S(2)}) collective-permute-start(f32[2,512]{1,0:T(2,128)S(1)} %fusion.29), channel_id=1, source_target_pairs={{0,3},{1,6},{2,5},{3,0},{4,7},{5,2},{6,1},{7,4},{8,11},{9,14},{10,... | collective-permute-start | bytes 12296 | tf_op jit(solution)/shard_map/ppermute | solution.py:138
  115.4 3.5 %collective-permute-done.26 = f32[2,512]{1,0:T(2,128)S(1)} collective-permute-done((f32[2,512]{1,0:T(2,128)S(1)}, f32[2,512]{1,0:T(2,128)S(1)}, u32[]{:S(2)}, u32[]{:S(2)}) %collective-permute-start.26) | collective-permute-done | bytes 4128 | tf_op jit(solution)/shard_map/ppermute | solution.py:138
  118.9 3.7 %collective-permute-done.28 = bf16[512,384]{1,0:T(8,128)(2,1)S(1)} collective-permute-done((bf16[512,384]{1,0:T(8,128)(2,1)S(1)}, bf16[512,384]{1,0:T(8,128)(2,1)S(1)}, u32[]{:S(2)}, u32[]{:S(2)}) %collective-permute-start.28) | collective-permute-done | bytes 393248 | tf_op jit(solution)/shard_map/ppermute | solution.py:132
  122.6 4.0 %collective-permute-done.29 = bf16[512,384]{1,0:T(8,128)(2,1)S(1)} collective-permute-done((bf16[512,384]{1,0:T(8,128)(2,1)S(1)}, bf16[512,384]{1,0:T(8,128)(2,1)S(1)}, u32[]{:S(2)}, u32[]{:S(2)}) %collective-permute-start.29) | collective-permute-done | bytes 393248 | tf_op jit(solution)/shard_map/ppermute | solution.py:132
  126.6 0.9 add_convert_fusion
  127.6 1.5 %fusion.15 = (bf16[512,384]{1,0:T(8,128)(2,1)}, bf16[512,384]{1,0:T(8,128)(2,1)}) fusion(bf16[512,384]{1,0:T(8,128)(2,1)S(1)} %copy-done.4, f32[512]{0:T(512)S(1)} %bitcast.42, f32[512]{0:T(512)S(1)} %multiply_multiply_fusion, f32[384]{0:T(512)S(1)} %copy-done.16, f32[512]{0:T(512)S(1)} %bitcast.35, bf16[512,384]{1,0:T(8,128)(2,1)S(1)} %collective-permute-done.20, ...), kind=kLoop, calls=%fused_computation.26 | loop fusion | flops 4521984 | bytes 3947520 | tf_op jit(solution)/shard_map/convert_element_type | solution.py:230
  (89 shorter events, 2.5 us)
Async XLA Ops:
  0.6 17.8 %copy-start = (s32[32,7,4,4]{0,3,2,1:T(4,128)S(1)}, s32[32,7,4,4]{0,3,2,1:T(4,128)}, u32[]{:S(2)}) copy-start(s32[32,7,4,4]{0,3,2,1:T(4,128)} %param.12) | copy-start | bytes 43012
  0.6 5.7 %collective-permute-start = (bf16[512,384]{1,0:T(8,128)(2,1)}, bf16[512,384]{1,0:T(8,128)(2,1)}, u32[]{:S(2)}, u32[]{:S(2)}) collective-permute-start(bf16[512,384]{1,0:T(8,128)(2,1)} %refs_7_.1), channel_id=1, source_target_pairs={{0,8},{8,0},{16,24},{24,16},{32,40},{40,32},{48,56},{56,48},{64,72... | collective-permute-start | bytes 1179656 | tf_op jit(solution)/shard_map/ppermute | solution.py:143
  0.7 29.7 %collective-permute-start.10 = (bf16[512,384]{1,0:T(8,128)(2,1)}, bf16[512,384]{1,0:T(8,128)(2,1)S(1)}, u32[]{:S(2)}, u32[]{:S(2)}) collective-permute-start(bf16[512,384]{1,0:T(8,128)(2,1)} %refs_7_.1), channel_id=1, source_target_pairs={{0,16},{8,24},{16,0},{24,8},{32,48},{40,56},{48,32},{56,40},{64,80... | collective-permute-start | bytes 1179656 | tf_op jit(solution)/shard_map/ppermute | solution.py:132
  2.3 28.1 %collective-permute-start.11 = (bf16[512,384]{1,0:T(8,128)(2,1)}, bf16[512,384]{1,0:T(8,128)(2,1)S(1)}, u32[]{:S(2)}, u32[]{:S(2)}) collective-permute-start(bf16[512,384]{1,0:T(8,128)(2,1)} %refs_7_.1), channel_id=1, source_target_pairs={{16,32},{24,40},{32,16},{40,24},{48,64},{56,72},{64,48},{72,56},{8... | collective-permute-start | bytes 1179656 | tf_op jit(solution)/shard_map/ppermute | solution.py:132
  6.4 1.0 copy-start.1
  7.4 1.0 copy-start.3
  8.4 17.1 %copy-start.4 = (bf16[512,384]{1,0:T(8,128)(2,1)S(1)}, bf16[512,384]{1,0:T(8,128)(2,1)}, u32[]{:S(2)}) copy-start(bf16[512,384]{1,0:T(8,128)(2,1)} %refs_1_) | copy-start | bytes 1179652
  8.9 3.6 %collective-permute-start.1 = (f32[2,512]{1,0:T(2,128)S(1)}, f32[2,512]{1,0:T(2,128)S(1)}, u32[]{:S(2)}, u32[]{:S(2)}) collective-permute-start(f32[2,512]{1,0:T(2,128)S(1)} %row_squares.1), channel_id=1, source_target_pairs={{0,1},{1,0},{2,3},{3,2},{4,5},{5,4},{6,7},{7,6},{8,9},{9,8},{10,11... | collective-permute-start | bytes 12296 | tf_op jit(solution)/shard_map/ppermute | solution.py:138
  12.5 7.4 %collective-permute-start.2 = (f32[2,512]{1,0:T(2,128)S(1)}, f32[2,512]{1,0:T(2,128)S(1)}, u32[]{:S(2)}, u32[]{:S(2)}) collective-permute-start(f32[2,512]{1,0:T(2,128)S(1)} %add.126), channel_id=1, source_target_pairs={{0,7},{1,2},{2,1},{3,4},{4,3},{5,6},{6,5},{7,0},{8,15},{9,10},{10,... | collective-permute-start | bytes 12296 | tf_op jit(solution)/shard_map/ppermute | solution.py:138
  20.0 5.4 %collective-permute-start.3 = (f32[2,512]{1,0:T(2,128)S(1)}, f32[2,512]{1,0:T(2,128)S(1)}, u32[]{:S(2)}, u32[]{:S(2)}) collective-permute-start(f32[2,512]{1,0:T(2,128)S(1)} %add.127), channel_id=1, source_target_pairs={{0,3},{1,6},{2,5},{3,0},{4,7},{5,2},{6,1},{7,4},{8,11},{9,14},{10,... | collective-permute-start | bytes 12296 | tf_op jit(solution)/shard_map/ppermute | solution.py:138
  26.3 8.1 %copy-start.7 = (bf16[512,384]{1,0:T(8,128)(2,1)}, bf16[512,384]{1,0:T(8,128)(2,1)S(1)}, u32[]{:S(2)}) copy-start(bf16[512,384]{1,0:T(8,128)(2,1)S(1)} %fusion.9.refs_0_) | copy-start | bytes 1179652
  26.3 8.1 %collective-permute-start.4 = (bf16[512,384]{1,0:T(8,128)(2,1)S(1)}, bf16[512,384]{1,0:T(8,128)(2,1)S(1)}, u32[]{:S(2)}, u32[]{:S(2)}) collective-permute-start(bf16[512,384]{1,0:T(8,128)(2,1)S(1)} %fusion.9.refs_0_), channel_id=1, source_target_pairs={{0,16},{8,24},{16,0},{24,8},{32,48},{40,56},{48,32},{56,40},{64,80... | collective-permute-start | bytes 1179656 | tf_op jit(solution)/shard_map/ppermute | solution.py:132
  27.1 13.0 %collective-permute-start.5 = (bf16[512,384]{1,0:T(8,128)(2,1)S(1)}, bf16[512,384]{1,0:T(8,128)(2,1)S(1)}, u32[]{:S(2)}, u32[]{:S(2)}) collective-permute-start(bf16[512,384]{1,0:T(8,128)(2,1)S(1)} %fusion.9.refs_0_), channel_id=1, source_target_pairs={{16,32},{24,40},{32,16},{40,24},{48,64},{56,72},{64,48},{72,56},{8... | collective-permute-start | bytes 1179656 | tf_op jit(solution)/shard_map/ppermute | solution.py:132
  30.5 2.0 %copy-start.8 = (bf16[512,384]{1,0:T(8,128)(2,1)}, bf16[512,384]{1,0:T(8,128)(2,1)S(1)}, u32[]{:S(2)}) copy-start(bf16[512,384]{1,0:T(8,128)(2,1)S(1)} %collective-permute-done.10.refs_8_) | copy-start | bytes 1179652
  30.5 3.7 %copy-start.9 = (bf16[512,384]{1,0:T(8,128)(2,1)}, bf16[512,384]{1,0:T(8,128)(2,1)S(1)}, u32[]{:S(2)}) copy-start(bf16[512,384]{1,0:T(8,128)(2,1)S(1)} %collective-permute-done.11.refs_9_) | copy-start | bytes 1179652
  30.5 12.5 %collective-permute-start.14 = (bf16[512,384]{1,0:T(8,128)(2,1)S(1)}, bf16[512,384]{1,0:T(8,128)(2,1)S(1)}, u32[]{:S(2)}, u32[]{:S(2)}) collective-permute-start(bf16[512,384]{1,0:T(8,128)(2,1)S(1)} %broadcast_select_fusion), channel_id=1, source_target_pairs={{8,16},{16,8},{24,32},{32,24},{40,48},{48,40},{56,64},{64,56},{72,... | collective-permute-start | bytes 1179656 | tf_op jit(solution)/shard_map/ppermute | solution.py:149
  32.5 10.6 %collective-permute-start.12 = (bf16[512,384]{1,0:T(8,128)(2,1)S(1)}, bf16[512,384]{1,0:T(8,128)(2,1)S(1)}, u32[]{:S(2)}, u32[]{:S(2)}) collective-permute-start(bf16[512,384]{1,0:T(8,128)(2,1)S(1)} %collective-permute-done.10.refs_8_), channel_id=1, source_target_pairs={{0,8},{8,0},{16,24},{24,16},{32,40},{40,32},{48,56},{56,48},{64,72... | collective-permute-start | bytes 1179656 | tf_op jit(solution)/shard_map/ppermute | solution.py:143
  34.2 12.4 %collective-permute-start.13 = (bf16[512,384]{1,0:T(8,128)(2,1)S(1)}, bf16[512,384]{1,0:T(8,128)(2,1)}, u32[]{:S(2)}, u32[]{:S(2)}) collective-permute-start(bf16[512,384]{1,0:T(8,128)(2,1)S(1)} %collective-permute-done.11.refs_9_), channel_id=1, source_target_pairs={{0,8},{8,0},{16,24},{24,16},{32,40},{40,32},{48,56},{56,48},{64,72... | collective-permute-start | bytes 1179656 | tf_op jit(solution)/shard_map/ppermute | solution.py:143
  34.4 8.7 %copy-start.10 = (bf16[512,384]{1,0:T(8,128)(2,1)}, bf16[512,384]{1,0:T(8,128)(2,1)S(1)}, u32[]{:S(2)}) copy-start(bf16[512,384]{1,0:T(8,128)(2,1)S(1)} %collective-permute-done.4.refs_1_) | copy-start | bytes 1179652
  34.4 12.2 %collective-permute-start.6 = (bf16[512,384]{1,0:T(8,128)(2,1)S(1)}, bf16[512,384]{1,0:T(8,128)(2,1)}, u32[]{:S(2)}, u32[]{:S(2)}) collective-permute-start(bf16[512,384]{1,0:T(8,128)(2,1)S(1)} %fusion.9.refs_0_), channel_id=1, source_target_pairs={{0,8},{8,0},{16,24},{24,16},{32,40},{40,32},{48,56},{56,48},{64,72... | collective-permute-start | bytes 1179656 | tf_op jit(solution)/shard_map/ppermute | solution.py:143
  40.1 3.0 %copy-start.11 = (bf16[512,384]{1,0:T(8,128)(2,1)}, bf16[512,384]{1,0:T(8,128)(2,1)S(1)}, u32[]{:S(2)}) copy-start(bf16[512,384]{1,0:T(8,128)(2,1)S(1)} %collective-permute-done.5.refs_2_) | copy-start | bytes 1179652
  40.1 4.8 %copy-start.2 = (bf16[512,384]{1,0:T(8,128)(2,1)S(1)}, bf16[512,384]{1,0:T(8,128)(2,1)}, u32[]{:S(2)}) copy-start(bf16[512,384]{1,0:T(8,128)(2,1)} %refs_0_.1) | copy-start | bytes 1179652
  40.1 11.4 %collective-permute-start.9 = (bf16[512,384]{1,0:T(8,128)(2,1)S(1)}, bf16[512,384]{1,0:T(8,128)(2,1)}, u32[]{:S(2)}, u32[]{:S(2)}) collective-permute-start(bf16[512,384]{1,0:T(8,128)(2,1)S(1)} %broadcast_select_fusion.1), channel_id=1, source_target_pairs={{8,16},{16,8},{24,32},{32,24},{40,48},{48,40},{56,64},{64,56},{72,... | collective-permute-start | bytes 1179656 | tf_op jit(solution)/shard_map/ppermute | solution.py:149
  43.1 0.8 copy-start.18
  43.1 8.5 %collective-permute-start.7 = (bf16[512,384]{1,0:T(8,128)(2,1)S(1)}, bf16[512,384]{1,0:T(8,128)(2,1)}, u32[]{:S(2)}, u32[]{:S(2)}) collective-permute-start(bf16[512,384]{1,0:T(8,128)(2,1)S(1)} %collective-permute-done.4.refs_1_), channel_id=1, source_target_pairs={{0,8},{8,0},{16,24},{24,16},{32,40},{40,32},{48,56},{56,48},{64,72... | collective-permute-start | bytes 1179656 | tf_op jit(solution)/shard_map/ppermute | solution.py:143
  43.1 0.9 copy-start.19
  43.1 8.5 %collective-permute-start.8 = (bf16[512,384]{1,0:T(8,128)(2,1)S(1)}, bf16[512,384]{1,0:T(8,128)(2,1)}, u32[]{:S(2)}, u32[]{:S(2)}) collective-permute-start(bf16[512,384]{1,0:T(8,128)(2,1)S(1)} %collective-permute-done.5.refs_2_), channel_id=1, source_target_pairs={{0,8},{8,0},{16,24},{24,16},{32,40},{40,32},{48,56},{56,48},{64,72... | collective-permute-start | bytes 1179656 | tf_op jit(solution)/shard_map/ppermute | solution.py:143
  74.7 8.4 %collective-permute-start.16 = (bf16[512,384]{1,0:T(8,128)(2,1)}, bf16[512,384]{1,0:T(8,128)(2,1)S(1)}, u32[]{:S(2)}, u32[]{:S(2)}) collective-permute-start(bf16[512,384]{1,0:T(8,128)(2,1)} %get-tuple-element.40), channel_id=1, source_target_pairs={{0,8},{8,0},{16,24},{24,16},{32,40},{40,32},{48,56},{56,48},{64,72... | collective-permute-start | bytes 1179656 | tf_op jit(solution)/shard_map/ppermute | solution.py:143
  74.8 11.4 %collective-permute-start.17 = (bf16[512,384]{1,0:T(8,128)(2,1)}, bf16[512,384]{1,0:T(8,128)(2,1)S(1)}, u32[]{:S(2)}, u32[]{:S(2)}) collective-permute-start(bf16[512,384]{1,0:T(8,128)(2,1)} %get-tuple-element.41), channel_id=1, source_target_pairs={{8,16},{16,8},{24,32},{32,24},{40,48},{48,40},{56,64},{64,56},{72,... | collective-permute-start | bytes 1179656 | tf_op jit(solution)/shard_map/ppermute | solution.py:149
  76.8 9.5 %collective-permute-start.19 = (bf16[512,384]{1,0:T(8,128)(2,1)}, bf16[512,384]{1,0:T(8,128)(2,1)S(1)}, u32[]{:S(2)}, u32[]{:S(2)}) collective-permute-start(bf16[512,384]{1,0:T(8,128)(2,1)} %get-tuple-element.43), channel_id=1, source_target_pairs={{0,8},{8,0},{16,24},{24,16},{32,40},{40,32},{48,56},{56,48},{64,72... | collective-permute-start | bytes 1179656 | tf_op jit(solution)/shard_map/ppermute | solution.py:143
  77.3 10.6 %collective-permute-start.21 = (bf16[512,384]{1,0:T(8,128)(2,1)}, bf16[512,384]{1,0:T(8,128)(2,1)S(1)}, u32[]{:S(2)}, u32[]{:S(2)}) collective-permute-start(bf16[512,384]{1,0:T(8,128)(2,1)} %get-tuple-element.45), channel_id=1, source_target_pairs={{0,8},{8,0},{16,24},{24,16},{32,40},{40,32},{48,56},{56,48},{64,72... | collective-permute-start | bytes 1179656 | tf_op jit(solution)/shard_map/ppermute | solution.py:143
  77.4 13.0 %collective-permute-start.22 = (bf16[512,384]{1,0:T(8,128)(2,1)}, bf16[512,384]{1,0:T(8,128)(2,1)S(1)}, u32[]{:S(2)}, u32[]{:S(2)}) collective-permute-start(bf16[512,384]{1,0:T(8,128)(2,1)} %get-tuple-element.46), channel_id=1, source_target_pairs={{8,16},{16,8},{24,32},{32,24},{40,48},{48,40},{56,64},{64,56},{72,... | collective-permute-start | bytes 1179656 | tf_op jit(solution)/shard_map/ppermute | solution.py:149
  83.1 7.3 %collective-permute-start.23 = (bf16[512,384]{1,0:T(8,128)(2,1)}, bf16[512,384]{1,0:T(8,128)(2,1)S(1)}, u32[]{:S(2)}, u32[]{:S(2)}) collective-permute-start(bf16[512,384]{1,0:T(8,128)(2,1)} %get-tuple-element.48), channel_id=1, source_target_pairs={{0,8},{8,0},{16,24},{24,16},{32,40},{40,32},{48,56},{56,48},{64,72... | collective-permute-start | bytes 1179656 | tf_op jit(solution)/shard_map/ppermute | solution.py:143
  86.3 5.4 %collective-permute-start.15 = (bf16[512,384]{1,0:T(8,128)(2,1)}, bf16[512,384]{1,0:T(8,128)(2,1)S(1)}, u32[]{:S(2)}, u32[]{:S(2)}) collective-permute-start(bf16[512,384]{1,0:T(8,128)(2,1)} %get-tuple-element.38), channel_id=1, source_target_pairs={{0,8},{8,0},{16,24},{24,16},{32,40},{40,32},{48,56},{56,48},{64,72... | collective-permute-start | bytes 1179656 | tf_op jit(solution)/shard_map/ppermute | solution.py:143
  86.3 4.0 %copy-start.5 = (f32[512,384]{1,0:T(8,128)S(1)}, f32[512,384]{1,0:T(8,128)}, u32[]{:S(2)}) copy-start(f32[512,384]{1,0:T(8,128)} %get-tuple-element.36) | copy-start | bytes 2359300
  87.8 11.6 %collective-permute-start.18 = (bf16[512,384]{1,0:T(8,128)(2,1)S(1)}, bf16[512,384]{1,0:T(8,128)(2,1)S(1)}, u32[]{:S(2)}, u32[]{:S(2)}) collective-permute-start(bf16[512,384]{1,0:T(8,128)(2,1)S(1)} %get-tuple-element.65), channel_id=1, source_target_pairs={{0,16},{8,24},{16,0},{24,8},{32,48},{40,56},{48,32},{56,40},{64,80... | collective-permute-start | bytes 1179656 | tf_op jit(solution)/shard_map/ppermute | solution.py:132
  87.9 15.5 %collective-permute-start.20 = (bf16[512,384]{1,0:T(8,128)(2,1)S(1)}, bf16[512,384]{1,0:T(8,128)(2,1)S(1)}, u32[]{:S(2)}, u32[]{:S(2)}) collective-permute-start(bf16[512,384]{1,0:T(8,128)(2,1)S(1)} %get-tuple-element.64), channel_id=1, source_target_pairs={{16,32},{24,40},{32,16},{40,24},{48,64},{56,72},{64,48},{72,56},{8... | collective-permute-start | bytes 1179656 | tf_op jit(solution)/shard_map/ppermute | solution.py:132
  90.2 1.0 copy-start.13
  90.2 1.1 copy-start.14
  91.4 12.1 %copy-start.6 = (bf16[512,384]{1,0:T(8,128)(2,1)S(1)}, bf16[512,384]{1,0:T(8,128)(2,1)}, u32[]{:S(2)}) copy-start(bf16[512,384]{1,0:T(8,128)(2,1)} %get-tuple-element.49) | copy-start | bytes 1179652
  103.4 7.6 %copy-start.17 = (bf16[512,384]{1,0:T(8,128)(2,1)S(1)}, bf16[512,384]{1,0:T(8,128)(2,1)}, u32[]{:S(2)}) copy-start(bf16[512,384]{1,0:T(8,128)(2,1)} %get-tuple-element.54) | copy-start | bytes 1179652
  103.4 23.2 %copy-start.12 = (bf16[512,384]{1,0:T(8,128)(2,1)S(1)}, bf16[512,384]{1,0:T(8,128)(2,1)}, u32[]{:S(2)}) copy-start(bf16[512,384]{1,0:T(8,128)(2,1)} %get-tuple-element.58) | copy-start | bytes 1179652
  103.8 3.9 %collective-permute-start.24 = (f32[2,512]{1,0:T(2,128)S(1)}, f32[2,512]{1,0:T(2,128)S(1)}, u32[]{:S(2)}, u32[]{:S(2)}) collective-permute-start(f32[2,512]{1,0:T(2,128)S(1)} %pad_maximum_fusion), channel_id=1, source_target_pairs={{0,1},{1,0},{2,3},{3,2},{4,5},{5,4},{6,7},{7,6},{8,9},{9,8},{10,11... | collective-permute-start | bytes 12296 | tf_op jit(solution)/shard_map/ppermute | solution.py:138
  107.7 5.6 %collective-permute-start.25 = (f32[2,512]{1,0:T(2,128)S(1)}, f32[2,512]{1,0:T(2,128)S(1)}, u32[]{:S(2)}, u32[]{:S(2)}) collective-permute-start(f32[2,512]{1,0:T(2,128)S(1)} %fusion.26), channel_id=1, source_target_pairs={{0,7},{1,2},{2,1},{3,4},{4,3},{5,6},{6,5},{7,0},{8,15},{9,10},{10,... | collective-permute-start | bytes 12296 | tf_op jit(solution)/shard_map/ppermute | solution.py:138
  111.1 7.8 %collective-permute-start.27 = (bf16[512,384]{1,0:T(8,128)(2,1)S(1)}, bf16[512,384]{1,0:T(8,128)(2,1)S(1)}, u32[]{:S(2)}, u32[]{:S(2)}) collective-permute-start(bf16[512,384]{1,0:T(8,128)(2,1)S(1)} %copy-done.17), channel_id=1, source_target_pairs={{0,8},{8,0},{16,24},{24,16},{32,40},{40,32},{48,56},{56,48},{64,72... | collective-permute-start | bytes 1179656 | tf_op jit(solution)/shard_map/ppermute | solution.py:143
  111.1 11.5 %collective-permute-start.28 = (bf16[512,384]{1,0:T(8,128)(2,1)S(1)}, bf16[512,384]{1,0:T(8,128)(2,1)S(1)}, u32[]{:S(2)}, u32[]{:S(2)}) collective-permute-start(bf16[512,384]{1,0:T(8,128)(2,1)S(1)} %get-tuple-element.55), channel_id=1, source_target_pairs={{0,16},{8,24},{16,0},{24,8},{32,48},{40,56},{48,32},{56,40},{64,80... | collective-permute-start | bytes 1179656 | tf_op jit(solution)/shard_map/ppermute | solution.py:132
  111.2 15.5 %collective-permute-start.29 = (bf16[512,384]{1,0:T(8,128)(2,1)S(1)}, bf16[512,384]{1,0:T(8,128)(2,1)S(1)}, u32[]{:S(2)}, u32[]{:S(2)}) collective-permute-start(bf16[512,384]{1,0:T(8,128)(2,1)S(1)} %get-tuple-element.56), channel_id=1, source_target_pairs={{16,32},{24,40},{32,16},{40,24},{48,64},{56,72},{64,48},{72,56},{8... | collective-permute-start | bytes 1179656 | tf_op jit(solution)/shard_map/ppermute | solution.py:132
  113.4 5.5 %collective-permute-start.26 = (f32[2,512]{1,0:T(2,128)S(1)}, f32[2,512]{1,0:T(2,128)S(1)}, u32[]{:S(2)}, u32[]{:S(2)}) collective-permute-start(f32[2,512]{1,0:T(2,128)S(1)} %fusion.29), channel_id=1, source_target_pairs={{0,3},{1,6},{2,5},{3,0},{4,7},{5,2},{6,1},{7,4},{8,11},{9,14},{10,... | collective-permute-start | bytes 12296 | tf_op jit(solution)/shard_map/ppermute | solution.py:138
  (2 other events, 1.4 us)

commit v4 on v2

--- a/solution.py
+++ b/solution.py
@@ -143,6 +143,13 @@
     return pair + before + turned(pair + before, -3) + turned(pair, 3)
 
 
+def pair_sum(value):
+    rounds = ((1, 0, 3, 2, 5, 4, 7, 6), (7, 2, 1, 4, 3, 6, 5, 0), (3, 6, 5, 0, 7, 2, 1, 4))
+    for partners in rounds:
+        value = value + lax.ppermute(value, "head", list(enumerate(partners)))
+    return value
+
+
 def swapped(value):
     return lax.ppermute(value, "tm", [(s, s ^ 1) for s in range(lax.axis_size("tm"))])
 
@@ -198,7 +205,7 @@
     query_float = queries.astype(jnp.float32)
     key_float = key_rows.astype(jnp.float32)
     key_raw, values[3] = lax.optimization_barrier((key_rows, values[3]))
-    rates = lax.rsqrt(ring_sum(square_call([queries, key_raw])) / full_width + epsilon)
+    rates = lax.rsqrt(pair_sum(square_call([queries, key_raw])) / full_width + epsilon)
     query_rate = rates[0][:, None]
     key_rate = rates[1][:, None]
     query_scaled = (query_float * query_rate * query_gain * (SCALE * LOG2E)).astype(jnp.bfloat16)

time: 127 us -> 126 us (level)
  waiting for transfers between devices: 43.4 us -> 40.8 us
  starting transfers between devices: 45.5 us -> 47.2 us
    ppermute x0 -> x3, starting transfers between devices: none -> 9.8 us  [pair_sum(): value = value + lax.ppermute(value, 'head', list(enumerate(partners)))]
    ppermute x8 -> x4, starting transfers between devices: 15.9 us -> 7.44 us  [turned(): lax.ppermute(value, 'head', [(s, (s + steps) % count) for s in range(coun...]
    ppermute x8 -> x4, waiting for transfers between devices: 13 us -> 5.84 us  [turned(): lax.ppermute(value, 'head', [(s, (s + steps) % count) for s in range(coun...]
    ppermute x0 -> x3, waiting for transfers between devices: none -> 5.63 us  [pair_sum(): value = value + lax.ppermute(value, 'head', list(enumerate(partners)))]
  transfers between devices with their start and end apart: 32 -> 31, of which waited for: 15 -> 14; matrix products, arithmetic and copies ran while one was open for 4% -> 4% of each run, Pallas kernels for 0% -> 0%
where the time goes in v4:
time: 126 us; the launch traced here: 125 us
  starting transfers between devices  47.2 us (37%)
  waiting for transfers between devices  40.8 us (32%)
  Pallas kernels  23.7 us (19%)
  local copies, waits for them, and re-layouts  6.4 us (5%)
  other arithmetic  6.2 us (5%)
    pallas_call x1, Pallas kernels, head_call(): pl.pallas_call(head_kernel, grid=(width // BLK,), in_specs=[pl.BlockSpec(...  23.1 us
    ppermute x8, waiting for transfers between devices, across(): lax.ppermute(value, 'tm', [(a, b) for a, b in pairs if 0 <= b < count])  20.4 us
    ppermute x8, starting transfers between devices, across(): lax.ppermute(value, 'tm', [(a, b) for a, b in pairs if 0 <= b < count])  14.3 us
    ppermute x4, starting transfers between devices, outward(): lax.ppermute(value, 'tm', [(a, b) for a, b in pairs if 0 <= b < count])  11.6 us
    ppermute x3, starting transfers between devices, pair_sum(): value = value + lax.ppermute(value, 'head', list(enumerate(partners)))  9.8 us
    ppermute x4, waiting for transfers between devices, outward(): lax.ppermute(value, 'tm', [(a, b) for a, b in pairs if 0 <= b < count])  8.93 us
    ppermute x4, starting transfers between devices, turned(): lax.ppermute(value, 'head', [(s, (s + steps) % count) for s in range(coun...  7.44 us
    ppermute x4, waiting for transfers between devices, turned(): lax.ppermute(value, 'head', [(s, (s + steps) % count) for s in range(coun...  5.84 us
  transfers between devices with their start and end apart: 31, of which 14 were waited for; matrix products, arithmetic and copies ran while one was open for 4% of the time, Pallas kernels for 0%

profile of v4, /device:TPU:8, one launch (start us, length us, event | category | flops | bytes accessed | tf_op | source)
XLA Modules:
  0.0 125.4 jit_solution(7976488017068935614)
XLA Ops:
  0.7 1.6 %collective-permute-start.10 = (bf16[512,384]{1,0:T(8,128)(2,1)}, bf16[512,384]{1,0:T(8,128)(2,1)S(1)}, u32[]{:S(2)}, u32[]{:S(2)}) collective-permute-start(bf16[512,384]{1,0:T(8,128)(2,1)} %refs_7_.1), channel_id=1, source_target_pairs={{0,16},{8,24},{16,0},{24,8},{32,48},{40,56},{48,32},{56,40},{64,80... | collective-permute-start | bytes 1179656 | tf_op jit(solution)/shard_map/ppermute | solution.py:132
  2.3 3.9 %collective-permute-start.11 = (bf16[512,384]{1,0:T(8,128)(2,1)}, bf16[512,384]{1,0:T(8,128)(2,1)S(1)}, u32[]{:S(2)}, u32[]{:S(2)}) collective-permute-start(bf16[512,384]{1,0:T(8,128)(2,1)} %refs_7_.1), channel_id=1, source_target_pairs={{16,32},{24,40},{32,16},{40,24},{48,64},{56,72},{64,48},{72,56},{8... | collective-permute-start | bytes 1179656 | tf_op jit(solution)/shard_map/ppermute | solution.py:132
  6.4 1.0 copy-done.1
  7.4 1.0 copy-done.3
  8.4 0.5 row_squares.1
  8.9 1.9 %collective-permute-start.1 = (f32[2,512]{1,0:T(2,128)S(1)}, f32[2,512]{1,0:T(2,128)S(1)}, u32[]{:S(2)}, u32[]{:S(2)}) collective-permute-start(f32[2,512]{1,0:T(2,128)S(1)} %row_squares.1), channel_id=1, source_target_pairs={{0,1},{1,0},{2,3},{3,2},{4,5},{5,4},{6,7},{7,6},{8,9},{9,8},{10,11... | collective-permute-start | bytes 12296 | tf_op jit(solution)/shard_map/ppermute | solution.py:149
  10.8 1.7 %collective-permute-done.1 = f32[2,512]{1,0:T(2,128)S(1)} collective-permute-done((f32[2,512]{1,0:T(2,128)S(1)}, f32[2,512]{1,0:T(2,128)S(1)}, u32[]{:S(2)}, u32[]{:S(2)}) %collective-permute-start.1) | collective-permute-done | bytes 4128 | tf_op jit(solution)/shard_map/ppermute | solution.py:149
  12.5 5.9 %collective-permute-start.2 = (f32[2,512]{1,0:T(2,128)S(1)}, f32[2,512]{1,0:T(2,128)S(1)}, u32[]{:S(2)}, u32[]{:S(2)}) collective-permute-start(f32[2,512]{1,0:T(2,128)S(1)} %add.130), channel_id=1, source_target_pairs={{0,7},{1,2},{2,1},{3,4},{4,3},{5,6},{6,5},{7,0},{8,15},{9,10},{10,... | collective-permute-start | bytes 12296 | tf_op jit(solution)/shard_map/ppermute | solution.py:149
  18.5 1.5 %collective-permute-done.2 = f32[2,512]{1,0:T(2,128)S(1)} collective-permute-done((f32[2,512]{1,0:T(2,128)S(1)}, f32[2,512]{1,0:T(2,128)S(1)}, u32[]{:S(2)}, u32[]{:S(2)}) %collective-permute-start.2) | collective-permute-done | bytes 4128 | tf_op jit(solution)/shard_map/ppermute | solution.py:149
  20.0 2.0 %collective-permute-start.3 = (f32[2,512]{1,0:T(2,128)S(1)}, f32[2,512]{1,0:T(2,128)S(1)}, u32[]{:S(2)}, u32[]{:S(2)}) collective-permute-start(f32[2,512]{1,0:T(2,128)S(1)} %add.131), channel_id=1, source_target_pairs={{0,3},{1,6},{2,5},{3,0},{4,7},{5,2},{6,1},{7,4},{8,11},{9,14},{10,... | collective-permute-start | bytes 12296 | tf_op jit(solution)/shard_map/ppermute | solution.py:149
  22.3 0.6 gather_fusion
  22.9 2.5 %collective-permute-done.3 = f32[2,512]{1,0:T(2,128)S(1)} collective-permute-done((f32[2,512]{1,0:T(2,128)S(1)}, f32[2,512]{1,0:T(2,128)S(1)}, u32[]{:S(2)}, u32[]{:S(2)}) %collective-permute-start.3) | collective-permute-done | bytes 4128 | tf_op jit(solution)/shard_map/ppermute | solution.py:149
  25.4 0.7 copy-done.16
  26.3 0.8 collective-permute-start.4
  27.1 3.4 %collective-permute-start.5 = (bf16[512,384]{1,0:T(8,128)(2,1)S(1)}, bf16[512,384]{1,0:T(8,128)(2,1)S(1)}, u32[]{:S(2)}, u32[]{:S(2)}) collective-permute-start(bf16[512,384]{1,0:T(8,128)(2,1)S(1)} %fusion.9.refs_0_), channel_id=1, source_target_pairs={{16,32},{24,40},{32,16},{40,24},{48,64},{56,72},{64,48},{72,56},{8... | collective-permute-start | bytes 1179656 | tf_op jit(solution)/shard_map/ppermute | solution.py:132
  30.5 1.9 %collective-permute-start.14 = (bf16[512,384]{1,0:T(8,128)(2,1)S(1)}, bf16[512,384]{1,0:T(8,128)(2,1)S(1)}, u32[]{:S(2)}, u32[]{:S(2)}) collective-permute-start(bf16[512,384]{1,0:T(8,128)(2,1)S(1)} %broadcast_select_fusion), channel_id=1, source_target_pairs={{8,16},{16,8},{24,32},{32,24},{40,48},{48,40},{56,64},{64,56},{72,... | collective-permute-start | bytes 1179656 | tf_op jit(solution)/shard_map/ppermute | solution.py:160
  32.5 1.7 %collective-permute-start.12 = (bf16[512,384]{1,0:T(8,128)(2,1)S(1)}, bf16[512,384]{1,0:T(8,128)(2,1)S(1)}, u32[]{:S(2)}, u32[]{:S(2)}) collective-permute-start(bf16[512,384]{1,0:T(8,128)(2,1)S(1)} %collective-permute-done.10.refs_8_), channel_id=1, source_target_pairs={{0,8},{8,0},{16,24},{24,16},{32,40},{40,32},{48,56},{56,48},{64,72... | collective-permute-start | bytes 1179656 | tf_op jit(solution)/shard_map/ppermute | solution.py:154
  34.4 0.5 collective-permute-start.6
  34.9 5.2 %collective-permute-done.5.refs_2_ = bf16[512,384]{1,0:T(8,128)(2,1)S(1)} collective-permute-done((bf16[512,384]{1,0:T(8,128)(2,1)S(1)}, bf16[512,384]{1,0:T(8,128)(2,1)S(1)}, u32[]{:S(2)}, u32[]{:S(2)}) %collective-permute-start.5) | collective-permute-done | bytes 393248 | tf_op jit(solution)/shard_map/ppermute | solution.py:132
  40.1 2.1 %collective-permute-start.9 = (bf16[512,384]{1,0:T(8,128)(2,1)S(1)}, bf16[512,384]{1,0:T(8,128)(2,1)}, u32[]{:S(2)}, u32[]{:S(2)}) collective-permute-start(bf16[512,384]{1,0:T(8,128)(2,1)S(1)} %broadcast_select_fusion.1), channel_id=1, source_target_pairs={{8,16},{16,8},{24,32},{32,24},{40,48},{48,40},{56,64},{64,56},{72,... | collective-permute-start | bytes 1179656 | tf_op jit(solution)/shard_map/ppermute | solution.py:160
  42.2 0.9 collective-permute-done.14.refs_13_
  43.1 0.7 collective-permute-start.8
  44.3 0.6 copy.21
  44.9 0.7 copy-done.15
  45.6 1.0 fusion.18.refs_14_
  46.6 5.0 %collective-permute-done.9.refs_6_ = bf16[512,384]{1,0:T(8,128)(2,1)} collective-permute-done((bf16[512,384]{1,0:T(8,128)(2,1)S(1)}, bf16[512,384]{1,0:T(8,128)(2,1)}, u32[]{:S(2)}, u32[]{:S(2)}) %collective-permute-start.9) | collective-permute-done | bytes 393248 | tf_op jit(solution)/shard_map/ppermute | solution.py:160
  51.6 23.1 %head_attention.1 = (bf16[512,384]{1,0:T(8,128)(2,1)}, f32[512,384]{1,0:T(8,128)}, bf16[512,384]{1,0:T(8,128)(2,1)}, bf16[512,384]{1,0:T(8,128)(2,1)}, bf16[512,...) custom-call(f32[28,512]{1,0:T(8,128)} %bitcast.28, ...), custom_call_target="tpu_custom_call" | custom-call | flops 8999999488 | bytes 12000000 | tf_op jit(solution)/shard_map/head_attention/pallas_call | solution.py:105
  74.8 1.9 %collective-permute-start.17 = (bf16[512,384]{1,0:T(8,128)(2,1)}, bf16[512,384]{1,0:T(8,128)(2,1)S(1)}, u32[]{:S(2)}, u32[]{:S(2)}) collective-permute-start(bf16[512,384]{1,0:T(8,128)(2,1)} %get-tuple-element.41), channel_id=1, source_target_pairs={{8,16},{16,8},{24,32},{32,24},{40,48},{48,40},{56,64},{64,56},{72,... | collective-permute-start | bytes 1179656 | tf_op jit(solution)/shard_map/ppermute | solution.py:160
  76.8 0.6 collective-permute-start.19
  77.4 5.7 %collective-permute-start.22 = (bf16[512,384]{1,0:T(8,128)(2,1)}, bf16[512,384]{1,0:T(8,128)(2,1)S(1)}, u32[]{:S(2)}, u32[]{:S(2)}) collective-permute-start(bf16[512,384]{1,0:T(8,128)(2,1)} %get-tuple-element.46), channel_id=1, source_target_pairs={{8,16},{16,8},{24,32},{32,24},{40,48},{48,40},{56,64},{64,56},{72,... | collective-permute-start | bytes 1179656 | tf_op jit(solution)/shard_map/ppermute | solution.py:160
  83.2 3.0 %collective-permute-done.17 = bf16[512,384]{1,0:T(8,128)(2,1)S(1)} collective-permute-done((bf16[512,384]{1,0:T(8,128)(2,1)}, bf16[512,384]{1,0:T(8,128)(2,1)S(1)}, u32[]{:S(2)}, u32[]{:S(2)}) %collective-permute-start.17) | collective-permute-done | bytes 393248 | tf_op jit(solution)/shard_map/ppermute | solution.py:160
  86.2 1.5 %fusion.3 = (bf16[512,384]{1,0:T(8,128)(2,1)S(1)}, bf16[512,384]{1,0:T(8,128)(2,1)S(1)}) fusion(bf16[512,384]{1,0:T(8,128)(2,1)S(1)} %collective-permute-done.17, bf16[512,384]{1,0:T(8,128)(2,1)S(1)} %collective-permute-done.19, bf16[512,384]{1,0:T(8,128)(2,1)} %get-tuple-element.42, pred[]{:T(512)S(6)} %gt.9, ...), kind=kLoop, calls=%fused_computation.14 | loop fusion | flops 2555904 | bytes 2752513 | tf_op jit(solution)/shard_map/convert_element_type | solution.py:175
  87.9 2.3 %collective-permute-start.20 = (bf16[512,384]{1,0:T(8,128)(2,1)S(1)}, bf16[512,384]{1,0:T(8,128)(2,1)S(1)}, u32[]{:S(2)}, u32[]{:S(2)}) collective-permute-start(bf16[512,384]{1,0:T(8,128)(2,1)S(1)} %get-tuple-element.66), channel_id=1, source_target_pairs={{16,32},{24,40},{32,16},{40,24},{48,64},{56,72},{64,48},{72,56},{8... | collective-permute-start | bytes 1179656 | tf_op jit(solution)/shard_map/ppermute | solution.py:132
  90.5 0.8 copy-done.13
  91.3 0.3 fusion.7
  91.7 7.7 %collective-permute-done.18 = bf16[512,384]{1,0:T(8,128)(2,1)S(1)} collective-permute-done((bf16[512,384]{1,0:T(8,128)(2,1)S(1)}, bf16[512,384]{1,0:T(8,128)(2,1)S(1)}, u32[]{:S(2)}, u32[]{:S(2)}) %collective-permute-start.18) | collective-permute-done | bytes 393248 | tf_op jit(solution)/shard_map/ppermute | solution.py:132
  99.4 4.0 %collective-permute-done.20 = bf16[512,384]{1,0:T(8,128)(2,1)S(1)} collective-permute-done((bf16[512,384]{1,0:T(8,128)(2,1)S(1)}, bf16[512,384]{1,0:T(8,128)(2,1)S(1)}, u32[]{:S(2)}, u32[]{:S(2)}) %collective-permute-start.20) | collective-permute-done | bytes 393248 | tf_op jit(solution)/shard_map/ppermute | solution.py:132
  103.4 0.4 fusion.11
  103.8 3.5 %collective-permute-start.24 = (f32[2,512]{1,0:T(2,128)S(1)}, f32[2,512]{1,0:T(2,128)S(1)}, u32[]{:S(2)}, u32[]{:S(2)}) collective-permute-start(f32[2,512]{1,0:T(2,128)S(1)} %pad_maximum_fusion), channel_id=1, source_target_pairs={{0,7},{1,0},{2,1},{3,2},{4,3},{5,4},{6,5},{7,6},{8,15},{9,8},{10,9... | collective-permute-start | bytes 12296 | tf_op jit(solution)/shard_map/ppermute | solution.py:137
  107.5 2.2 %collective-permute-start.30 = (bf16[512,384]{1,0:T(8,128)(2,1)S(1)}, bf16[512,384]{1,0:T(8,128)(2,1)S(1)}, u32[]{:S(2)}, u32[]{:S(2)}) collective-permute-start(bf16[512,384]{1,0:T(8,128)(2,1)S(1)} %get-tuple-element.56), channel_id=1, source_target_pairs={{16,32},{24,40},{32,16},{40,24},{48,64},{56,72},{64,48},{72,56},{8... | collective-permute-start | bytes 1179656 | tf_op jit(solution)/shard_map/ppermute | solution.py:132
  109.8 2.4 %collective-permute-done.25 = f32[2,512]{1,0:T(2,128)S(1)} collective-permute-done((f32[2,512]{1,0:T(2,128)S(1)}, f32[2,512]{1,0:T(2,128)S(1)}, u32[]{:S(2)}, u32[]{:S(2)}) %collective-permute-start.25) | collective-permute-done | bytes 4128 | tf_op jit(solution)/shard_map/ppermute | solution.py:137
  112.2 0.8 collective-permute-start.26
  112.9 3.1 %collective-permute-start.27 = (f32[2,512]{1,0:T(2,128)S(1)}, f32[2,512]{1,0:T(2,128)S(1)}, u32[]{:S(2)}, u32[]{:S(2)}) collective-permute-start(f32[2,512]{1,0:T(2,128)S(1)} %get-tuple-element.63), channel_id=1, source_target_pairs={{0,3},{1,4},{2,5},{3,6},{4,7},{5,0},{6,1},{7,2},{8,11},{9,12},{10,... | collective-permute-start | bytes 12296 | tf_op jit(solution)/shard_map/ppermute | solution.py:137
  116.1 1.6 %collective-permute-done.26 = f32[2,512]{1,0:T(2,128)S(1)} collective-permute-done((f32[2,512]{1,0:T(2,128)S(1)}, f32[2,512]{1,0:T(2,128)S(1)}, u32[]{:S(2)}, u32[]{:S(2)}) %collective-permute-start.26) | collective-permute-done | bytes 4128 | tf_op jit(solution)/shard_map/ppermute | solution.py:137
  117.6 1.9 %collective-permute-done.27 = f32[2,512]{1,0:T(2,128)S(1)} collective-permute-done((f32[2,512]{1,0:T(2,128)S(1)}, f32[2,512]{1,0:T(2,128)S(1)}, u32[]{:S(2)}, u32[]{:S(2)}) %collective-permute-start.27) | collective-permute-done | bytes 4128 | tf_op jit(solution)/shard_map/ppermute | solution.py:137
  119.6 3.4 %collective-permute-done.30 = bf16[512,384]{1,0:T(8,128)(2,1)S(1)} collective-permute-done((bf16[512,384]{1,0:T(8,128)(2,1)S(1)}, bf16[512,384]{1,0:T(8,128)(2,1)S(1)}, u32[]{:S(2)}, u32[]{:S(2)}) %collective-permute-start.30) | collective-permute-done | bytes 393248 | tf_op jit(solution)/shard_map/ppermute | solution.py:132
  123.0 0.9 add_convert_fusion
  123.9 1.5 %fusion.15 = (bf16[512,384]{1,0:T(8,128)(2,1)}, bf16[512,384]{1,0:T(8,128)(2,1)}) fusion(bf16[512,384]{1,0:T(8,128)(2,1)S(1)} %copy-done.4, f32[512]{0:T(512)S(1)} %bitcast.40, f32[512]{0:T(512)S(1)} %multiply_multiply_fusion, f32[384]{0:T(512)S(1)} %copy-done.16, f32[512]{0:T(512)S(1)} %bitcast.35, bf16[512,384]{1,0:T(8,128)(2,1)S(1)} %collective-permute-done.20, ...), kind=kLoop, calls=%fused_computation.26 | loop fusion | flops 4521984 | bytes 3947520 | tf_op jit(solution)/shard_map/convert_element_type | solution.py:241
  (90 shorter events, 2.6 us)
Async XLA Ops:
  0.6 17.8 %copy-start = (s32[32,7,4,4]{0,3,2,1:T(4,128)S(1)}, s32[32,7,4,4]{0,3,2,1:T(4,128)}, u32[]{:S(2)}) copy-start(s32[32,7,4,4]{0,3,2,1:T(4,128)} %param.12) | copy-start | bytes 43012
  0.6 5.7 %collective-permute-start = (bf16[512,384]{1,0:T(8,128)(2,1)}, bf16[512,384]{1,0:T(8,128)(2,1)}, u32[]{:S(2)}, u32[]{:S(2)}) collective-permute-start(bf16[512,384]{1,0:T(8,128)(2,1)} %refs_7_.1), channel_id=1, source_target_pairs={{0,8},{8,0},{16,24},{24,16},{32,40},{40,32},{48,56},{56,48},{64,72... | collective-permute-start | bytes 1179656 | tf_op jit(solution)/shard_map/ppermute | solution.py:154
  0.7 29.7 %collective-permute-start.10 = (bf16[512,384]{1,0:T(8,128)(2,1)}, bf16[512,384]{1,0:T(8,128)(2,1)S(1)}, u32[]{:S(2)}, u32[]{:S(2)}) collective-permute-start(bf16[512,384]{1,0:T(8,128)(2,1)} %refs_7_.1), channel_id=1, source_target_pairs={{0,16},{8,24},{16,0},{24,8},{32,48},{40,56},{48,32},{56,40},{64,80... | collective-permute-start | bytes 1179656 | tf_op jit(solution)/shard_map/ppermute | solution.py:132
  2.3 28.1 %collective-permute-start.11 = (bf16[512,384]{1,0:T(8,128)(2,1)}, bf16[512,384]{1,0:T(8,128)(2,1)S(1)}, u32[]{:S(2)}, u32[]{:S(2)}) collective-permute-start(bf16[512,384]{1,0:T(8,128)(2,1)} %refs_7_.1), channel_id=1, source_target_pairs={{16,32},{24,40},{32,16},{40,24},{48,64},{56,72},{64,48},{72,56},{8... | collective-permute-start | bytes 1179656 | tf_op jit(solution)/shard_map/ppermute | solution.py:132
  6.4 1.0 copy-start.1
  7.4 1.0 copy-start.3
  8.4 17.1 %copy-start.4 = (bf16[512,384]{1,0:T(8,128)(2,1)S(1)}, bf16[512,384]{1,0:T(8,128)(2,1)}, u32[]{:S(2)}) copy-start(bf16[512,384]{1,0:T(8,128)(2,1)} %refs_1_) | copy-start | bytes 1179652
  8.9 3.6 %collective-permute-start.1 = (f32[2,512]{1,0:T(2,128)S(1)}, f32[2,512]{1,0:T(2,128)S(1)}, u32[]{:S(2)}, u32[]{:S(2)}) collective-permute-start(f32[2,512]{1,0:T(2,128)S(1)} %row_squares.1), channel_id=1, source_target_pairs={{0,1},{1,0},{2,3},{3,2},{4,5},{5,4},{6,7},{7,6},{8,9},{9,8},{10,11... | collective-permute-start | bytes 12296 | tf_op jit(solution)/shard_map/ppermute | solution.py:149
  12.5 7.4 %collective-permute-start.2 = (f32[2,512]{1,0:T(2,128)S(1)}, f32[2,512]{1,0:T(2,128)S(1)}, u32[]{:S(2)}, u32[]{:S(2)}) collective-permute-start(f32[2,512]{1,0:T(2,128)S(1)} %add.130), channel_id=1, source_target_pairs={{0,7},{1,2},{2,1},{3,4},{4,3},{5,6},{6,5},{7,0},{8,15},{9,10},{10,... | collective-permute-start | bytes 12296 | tf_op jit(solution)/shard_map/ppermute | solution.py:149
  20.0 5.4 %collective-permute-start.3 = (f32[2,512]{1,0:T(2,128)S(1)}, f32[2,512]{1,0:T(2,128)S(1)}, u32[]{:S(2)}, u32[]{:S(2)}) collective-permute-start(f32[2,512]{1,0:T(2,128)S(1)} %add.131), channel_id=1, source_target_pairs={{0,3},{1,6},{2,5},{3,0},{4,7},{5,2},{6,1},{7,4},{8,11},{9,14},{10,... | collective-permute-start | bytes 12296 | tf_op jit(solution)/shard_map/ppermute | solution.py:149
  26.3 8.1 %copy-start.7 = (bf16[512,384]{1,0:T(8,128)(2,1)}, bf16[512,384]{1,0:T(8,128)(2,1)S(1)}, u32[]{:S(2)}) copy-start(bf16[512,384]{1,0:T(8,128)(2,1)S(1)} %fusion.9.refs_0_) | copy-start | bytes 1179652
  26.3 8.1 %collective-permute-start.4 = (bf16[512,384]{1,0:T(8,128)(2,1)S(1)}, bf16[512,384]{1,0:T(8,128)(2,1)S(1)}, u32[]{:S(2)}, u32[]{:S(2)}) collective-permute-start(bf16[512,384]{1,0:T(8,128)(2,1)S(1)} %fusion.9.refs_0_), channel_id=1, source_target_pairs={{0,16},{8,24},{16,0},{24,8},{32,48},{40,56},{48,32},{56,40},{64,80... | collective-permute-start | bytes 1179656 | tf_op jit(solution)/shard_map/ppermute | solution.py:132
  27.1 13.0 %collective-permute-start.5 = (bf16[512,384]{1,0:T(8,128)(2,1)S(1)}, bf16[512,384]{1,0:T(8,128)(2,1)S(1)}, u32[]{:S(2)}, u32[]{:S(2)}) collective-permute-start(bf16[512,384]{1,0:T(8,128)(2,1)S(1)} %fusion.9.refs_0_), channel_id=1, source_target_pairs={{16,32},{24,40},{32,16},{40,24},{48,64},{56,72},{64,48},{72,56},{8... | collective-permute-start | bytes 1179656 | tf_op jit(solution)/shard_map/ppermute | solution.py:132
  30.5 2.0 %copy-start.8 = (bf16[512,384]{1,0:T(8,128)(2,1)}, bf16[512,384]{1,0:T(8,128)(2,1)S(1)}, u32[]{:S(2)}) copy-start(bf16[512,384]{1,0:T(8,128)(2,1)S(1)} %collective-permute-done.10.refs_8_) | copy-start | bytes 1179652
  30.5 3.7 %copy-start.9 = (bf16[512,384]{1,0:T(8,128)(2,1)}, bf16[512,384]{1,0:T(8,128)(2,1)S(1)}, u32[]{:S(2)}) copy-start(bf16[512,384]{1,0:T(8,128)(2,1)S(1)} %collective-permute-done.11.refs_9_) | copy-start | bytes 1179652
  30.5 12.5 %collective-permute-start.14 = (bf16[512,384]{1,0:T(8,128)(2,1)S(1)}, bf16[512,384]{1,0:T(8,128)(2,1)S(1)}, u32[]{:S(2)}, u32[]{:S(2)}) collective-permute-start(bf16[512,384]{1,0:T(8,128)(2,1)S(1)} %broadcast_select_fusion), channel_id=1, source_target_pairs={{8,16},{16,8},{24,32},{32,24},{40,48},{48,40},{56,64},{64,56},{72,... | collective-permute-start | bytes 1179656 | tf_op jit(solution)/shard_map/ppermute | solution.py:160
  32.5 10.6 %collective-permute-start.12 = (bf16[512,384]{1,0:T(8,128)(2,1)S(1)}, bf16[512,384]{1,0:T(8,128)(2,1)S(1)}, u32[]{:S(2)}, u32[]{:S(2)}) collective-permute-start(bf16[512,384]{1,0:T(8,128)(2,1)S(1)} %collective-permute-done.10.refs_8_), channel_id=1, source_target_pairs={{0,8},{8,0},{16,24},{24,16},{32,40},{40,32},{48,56},{56,48},{64,72... | collective-permute-start | bytes 1179656 | tf_op jit(solution)/shard_map/ppermute | solution.py:154
  34.2 12.4 %collective-permute-start.13 = (bf16[512,384]{1,0:T(8,128)(2,1)S(1)}, bf16[512,384]{1,0:T(8,128)(2,1)}, u32[]{:S(2)}, u32[]{:S(2)}) collective-permute-start(bf16[512,384]{1,0:T(8,128)(2,1)S(1)} %collective-permute-done.11.refs_9_), channel_id=1, source_target_pairs={{0,8},{8,0},{16,24},{24,16},{32,40},{40,32},{48,56},{56,48},{64,72... | collective-permute-start | bytes 1179656 | tf_op jit(solution)/shard_map/ppermute | solution.py:154
  34.4 8.7 %copy-start.10 = (bf16[512,384]{1,0:T(8,128)(2,1)}, bf16[512,384]{1,0:T(8,128)(2,1)S(1)}, u32[]{:S(2)}) copy-start(bf16[512,384]{1,0:T(8,128)(2,1)S(1)} %collective-permute-done.4.refs_1_) | copy-start | bytes 1179652
  34.4 12.2 %collective-permute-start.6 = (bf16[512,384]{1,0:T(8,128)(2,1)S(1)}, bf16[512,384]{1,0:T(8,128)(2,1)}, u32[]{:S(2)}, u32[]{:S(2)}) collective-permute-start(bf16[512,384]{1,0:T(8,128)(2,1)S(1)} %fusion.9.refs_0_), channel_id=1, source_target_pairs={{0,8},{8,0},{16,24},{24,16},{32,40},{40,32},{48,56},{56,48},{64,72... | collective-permute-start | bytes 1179656 | tf_op jit(solution)/shard_map/ppermute | solution.py:154
  40.1 3.0 %copy-start.11 = (bf16[512,384]{1,0:T(8,128)(2,1)}, bf16[512,384]{1,0:T(8,128)(2,1)S(1)}, u32[]{:S(2)}) copy-start(bf16[512,384]{1,0:T(8,128)(2,1)S(1)} %collective-permute-done.5.refs_2_) | copy-start | bytes 1179652
  40.1 4.8 %copy-start.2 = (bf16[512,384]{1,0:T(8,128)(2,1)S(1)}, bf16[512,384]{1,0:T(8,128)(2,1)}, u32[]{:S(2)}) copy-start(bf16[512,384]{1,0:T(8,128)(2,1)} %refs_0_.1) | copy-start | bytes 1179652
  40.1 11.4 %collective-permute-start.9 = (bf16[512,384]{1,0:T(8,128)(2,1)S(1)}, bf16[512,384]{1,0:T(8,128)(2,1)}, u32[]{:S(2)}, u32[]{:S(2)}) collective-permute-start(bf16[512,384]{1,0:T(8,128)(2,1)S(1)} %broadcast_select_fusion.1), channel_id=1, source_target_pairs={{8,16},{16,8},{24,32},{32,24},{40,48},{48,40},{56,64},{64,56},{72,... | collective-permute-start | bytes 1179656 | tf_op jit(solution)/shard_map/ppermute | solution.py:160
  43.1 8.5 %collective-permute-start.7 = (bf16[512,384]{1,0:T(8,128)(2,1)S(1)}, bf16[512,384]{1,0:T(8,128)(2,1)}, u32[]{:S(2)}, u32[]{:S(2)}) collective-permute-start(bf16[512,384]{1,0:T(8,128)(2,1)S(1)} %collective-permute-done.4.refs_1_), channel_id=1, source_target_pairs={{0,8},{8,0},{16,24},{24,16},{32,40},{40,32},{48,56},{56,48},{64,72... | collective-permute-start | bytes 1179656 | tf_op jit(solution)/shard_map/ppermute | solution.py:154
  43.1 0.9 copy-start.19
  43.1 8.5 %collective-permute-start.8 = (bf16[512,384]{1,0:T(8,128)(2,1)S(1)}, bf16[512,384]{1,0:T(8,128)(2,1)}, u32[]{:S(2)}, u32[]{:S(2)}) collective-permute-start(bf16[512,384]{1,0:T(8,128)(2,1)S(1)} %collective-permute-done.5.refs_2_), channel_id=1, source_target_pairs={{0,8},{8,0},{16,24},{24,16},{32,40},{40,32},{48,56},{56,48},{64,72... | collective-permute-start | bytes 1179656 | tf_op jit(solution)/shard_map/ppermute | solution.py:154
  74.7 8.4 %collective-permute-start.16 = (bf16[512,384]{1,0:T(8,128)(2,1)}, bf16[512,384]{1,0:T(8,128)(2,1)S(1)}, u32[]{:S(2)}, u32[]{:S(2)}) collective-permute-start(bf16[512,384]{1,0:T(8,128)(2,1)} %get-tuple-element.40), channel_id=1, source_target_pairs={{0,8},{8,0},{16,24},{24,16},{32,40},{40,32},{48,56},{56,48},{64,72... | collective-permute-start | bytes 1179656 | tf_op jit(solution)/shard_map/ppermute | solution.py:154
  74.8 11.4 %collective-permute-start.17 = (bf16[512,384]{1,0:T(8,128)(2,1)}, bf16[512,384]{1,0:T(8,128)(2,1)S(1)}, u32[]{:S(2)}, u32[]{:S(2)}) collective-permute-start(bf16[512,384]{1,0:T(8,128)(2,1)} %get-tuple-element.41), channel_id=1, source_target_pairs={{8,16},{16,8},{24,32},{32,24},{40,48},{48,40},{56,64},{64,56},{72,... | collective-permute-start | bytes 1179656 | tf_op jit(solution)/shard_map/ppermute | solution.py:160
  76.8 9.5 %collective-permute-start.19 = (bf16[512,384]{1,0:T(8,128)(2,1)}, bf16[512,384]{1,0:T(8,128)(2,1)S(1)}, u32[]{:S(2)}, u32[]{:S(2)}) collective-permute-start(bf16[512,384]{1,0:T(8,128)(2,1)} %get-tuple-element.43), channel_id=1, source_target_pairs={{0,8},{8,0},{16,24},{24,16},{32,40},{40,32},{48,56},{56,48},{64,72... | collective-permute-start | bytes 1179656 | tf_op jit(solution)/shard_map/ppermute | solution.py:154
  77.3 10.6 %collective-permute-start.21 = (bf16[512,384]{1,0:T(8,128)(2,1)}, bf16[512,384]{1,0:T(8,128)(2,1)S(1)}, u32[]{:S(2)}, u32[]{:S(2)}) collective-permute-start(bf16[512,384]{1,0:T(8,128)(2,1)} %get-tuple-element.45), channel_id=1, source_target_pairs={{0,8},{8,0},{16,24},{24,16},{32,40},{40,32},{48,56},{56,48},{64,72... | collective-permute-start | bytes 1179656 | tf_op jit(solution)/shard_map/ppermute | solution.py:154
  77.4 13.0 %collective-permute-start.22 = (bf16[512,384]{1,0:T(8,128)(2,1)}, bf16[512,384]{1,0:T(8,128)(2,1)S(1)}, u32[]{:S(2)}, u32[]{:S(2)}) collective-permute-start(bf16[512,384]{1,0:T(8,128)(2,1)} %get-tuple-element.46), channel_id=1, source_target_pairs={{8,16},{16,8},{24,32},{32,24},{40,48},{48,40},{56,64},{64,56},{72,... | collective-permute-start | bytes 1179656 | tf_op jit(solution)/shard_map/ppermute | solution.py:160
  83.1 7.3 %collective-permute-start.23 = (bf16[512,384]{1,0:T(8,128)(2,1)}, bf16[512,384]{1,0:T(8,128)(2,1)S(1)}, u32[]{:S(2)}, u32[]{:S(2)}) collective-permute-start(bf16[512,384]{1,0:T(8,128)(2,1)} %get-tuple-element.48), channel_id=1, source_target_pairs={{0,8},{8,0},{16,24},{24,16},{32,40},{40,32},{48,56},{56,48},{64,72... | collective-permute-start | bytes 1179656 | tf_op jit(solution)/shard_map/ppermute | solution.py:154
  86.2 5.4 %collective-permute-start.15 = (bf16[512,384]{1,0:T(8,128)(2,1)}, bf16[512,384]{1,0:T(8,128)(2,1)S(1)}, u32[]{:S(2)}, u32[]{:S(2)}) collective-permute-start(bf16[512,384]{1,0:T(8,128)(2,1)} %get-tuple-element.38), channel_id=1, source_target_pairs={{0,8},{8,0},{16,24},{24,16},{32,40},{40,32},{48,56},{56,48},{64,72... | collective-permute-start | bytes 1179656 | tf_op jit(solution)/shard_map/ppermute | solution.py:154
  86.2 4.0 %copy-start.5 = (f32[512,384]{1,0:T(8,128)S(1)}, f32[512,384]{1,0:T(8,128)}, u32[]{:S(2)}) copy-start(f32[512,384]{1,0:T(8,128)} %get-tuple-element.36) | copy-start | bytes 2359300
  87.8 11.6 %collective-permute-start.18 = (bf16[512,384]{1,0:T(8,128)(2,1)S(1)}, bf16[512,384]{1,0:T(8,128)(2,1)S(1)}, u32[]{:S(2)}, u32[]{:S(2)}) collective-permute-start(bf16[512,384]{1,0:T(8,128)(2,1)S(1)} %get-tuple-element.67), channel_id=1, source_target_pairs={{0,16},{8,24},{16,0},{24,8},{32,48},{40,56},{48,32},{56,40},{64,80... | collective-permute-start | bytes 1179656 | tf_op jit(solution)/shard_map/ppermute | solution.py:132
  87.9 15.5 %collective-permute-start.20 = (bf16[512,384]{1,0:T(8,128)(2,1)S(1)}, bf16[512,384]{1,0:T(8,128)(2,1)S(1)}, u32[]{:S(2)}, u32[]{:S(2)}) collective-permute-start(bf16[512,384]{1,0:T(8,128)(2,1)S(1)} %get-tuple-element.66), channel_id=1, source_target_pairs={{16,32},{24,40},{32,16},{40,24},{48,64},{56,72},{64,48},{72,56},{8... | collective-permute-start | bytes 1179656 | tf_op jit(solution)/shard_map/ppermute | solution.py:132
  90.2 1.0 copy-start.13
  90.2 1.1 copy-start.14
  91.3 12.1 %copy-start.6 = (bf16[512,384]{1,0:T(8,128)(2,1)S(1)}, bf16[512,384]{1,0:T(8,128)(2,1)}, u32[]{:S(2)}) copy-start(bf16[512,384]{1,0:T(8,128)(2,1)} %get-tuple-element.49) | copy-start | bytes 1179652
  103.4 3.9 %copy-start.17 = (bf16[512,384]{1,0:T(8,128)(2,1)S(1)}, bf16[512,384]{1,0:T(8,128)(2,1)}, u32[]{:S(2)}) copy-start(bf16[512,384]{1,0:T(8,128)(2,1)} %get-tuple-element.54) | copy-start | bytes 1179652
  103.4 19.5 %copy-start.12 = (bf16[512,384]{1,0:T(8,128)(2,1)S(1)}, bf16[512,384]{1,0:T(8,128)(2,1)}, u32[]{:S(2)}) copy-start(bf16[512,384]{1,0:T(8,128)(2,1)} %get-tuple-element.58) | copy-start | bytes 1179652
  103.8 6.0 %collective-permute-start.24 = (f32[2,512]{1,0:T(2,128)S(1)}, f32[2,512]{1,0:T(2,128)S(1)}, u32[]{:S(2)}, u32[]{:S(2)}) collective-permute-start(f32[2,512]{1,0:T(2,128)S(1)} %pad_maximum_fusion), channel_id=1, source_target_pairs={{0,7},{1,0},{2,1},{3,2},{4,3},{5,4},{6,5},{7,6},{8,15},{9,8},{10,9... | collective-permute-start | bytes 12296 | tf_op jit(solution)/shard_map/ppermute | solution.py:137
  107.3 4.8 %collective-permute-start.25 = (f32[2,512]{1,0:T(2,128)S(1)}, f32[2,512]{1,0:T(2,128)S(1)}, u32[]{:S(2)}, u32[]{:S(2)}) collective-permute-start(f32[2,512]{1,0:T(2,128)S(1)} %pad_maximum_fusion), channel_id=1, source_target_pairs={{0,1},{1,2},{2,3},{3,4},{4,5},{5,6},{6,7},{7,0},{8,9},{9,10},{10,1... | collective-permute-start | bytes 12296 | tf_op jit(solution)/shard_map/ppermute | solution.py:137
  107.3 12.2 %collective-permute-start.28 = (bf16[512,384]{1,0:T(8,128)(2,1)S(1)}, bf16[512,384]{1,0:T(8,128)(2,1)S(1)}, u32[]{:S(2)}, u32[]{:S(2)}) collective-permute-start(bf16[512,384]{1,0:T(8,128)(2,1)S(1)} %copy-done.17), channel_id=1, source_target_pairs={{0,8},{8,0},{16,24},{24,16},{32,40},{40,32},{48,56},{56,48},{64,72... | collective-permute-start | bytes 1179656 | tf_op jit(solution)/shard_map/ppermute | solution.py:154
  107.4 12.1 %collective-permute-start.29 = (bf16[512,384]{1,0:T(8,128)(2,1)S(1)}, bf16[512,384]{1,0:T(8,128)(2,1)S(1)}, u32[]{:S(2)}, u32[]{:S(2)}) collective-permute-start(bf16[512,384]{1,0:T(8,128)(2,1)S(1)} %get-tuple-element.55), channel_id=1, source_target_pairs={{0,16},{8,24},{16,0},{24,8},{32,48},{40,56},{48,32},{56,40},{64,80... | collective-permute-start | bytes 1179656 | tf_op jit(solution)/shard_map/ppermute | solution.py:132
  107.5 15.4 %collective-permute-start.30 = (bf16[512,384]{1,0:T(8,128)(2,1)S(1)}, bf16[512,384]{1,0:T(8,128)(2,1)S(1)}, u32[]{:S(2)}, u32[]{:S(2)}) collective-permute-start(bf16[512,384]{1,0:T(8,128)(2,1)S(1)} %get-tuple-element.56), channel_id=1, source_target_pairs={{16,32},{24,40},{32,16},{40,24},{48,64},{56,72},{64,48},{72,56},{8... | collective-permute-start | bytes 1179656 | tf_op jit(solution)/shard_map/ppermute | solution.py:132
  112.2 5.5 %collective-permute-start.26 = (f32[2,512]{1,0:T(2,128)S(1)}, f32[2,512]{1,0:T(2,128)S(1)}, u32[]{:S(2)}, u32[]{:S(2)}) collective-permute-start(f32[2,512]{1,0:T(2,128)S(1)} %get-tuple-element.62), channel_id=1, source_target_pairs={{0,5},{1,6},{2,7},{3,0},{4,1},{5,2},{6,3},{7,4},{8,13},{9,14},{10,... | collective-permute-start | bytes 12296 | tf_op jit(solution)/shard_map/ppermute | solution.py:137
  112.9 6.6 %collective-permute-start.27 = (f32[2,512]{1,0:T(2,128)S(1)}, f32[2,512]{1,0:T(2,128)S(1)}, u32[]{:S(2)}, u32[]{:S(2)}) collective-permute-start(f32[2,512]{1,0:T(2,128)S(1)} %get-tuple-element.63), channel_id=1, source_target_pairs={{0,3},{1,4},{2,5},{3,6},{4,7},{5,0},{6,1},{7,2},{8,11},{9,12},{10,... | collective-permute-start | bytes 12296 | tf_op jit(solution)/shard_map/ppermute | solution.py:137
  (3 other events, 2.2 us)

commit v5 on v4

--- a/solution.py
+++ b/solution.py
@@ -225,9 +225,7 @@
             jnp.sum(key_float * key_gain * grad_knorm, axis=1),
         ]
     )
-    dots, value_parts = lax.optimization_barrier((ring_sum(dots), value_parts))
-    query_dot, key_dot = dots
-    value_sum = summed(value_parts)
+    query_dot, key_dot = ring_sum(dots)
     query_grad = (
         query_rate * query_gain * grad_qnorm
         - query_float * query_rate**3 * query_dot[:, None] / full_width
@@ -235,12 +233,9 @@
     key_grad = (
         key_rate * key_gain * grad_knorm - key_float * key_rate**3 * key_dot[:, None] / full_width
     )
-    return (
-        attended,
-        query_grad.astype(jnp.bfloat16),
-        key_grad.astype(jnp.bfloat16),
-        value_sum.astype(jnp.bfloat16),
-    )
+    query_grad, key_grad = query_grad.astype(jnp.bfloat16), key_grad.astype(jnp.bfloat16)
+    query_grad, key_grad, value_parts = lax.optimization_barrier((query_grad, key_grad, value_parts))
+    return attended, query_grad, key_grad, summed(value_parts).astype(jnp.bfloat16)
 
 
 def solution(mesh):

time: 126 us -> 133 us (1.056)
  waiting for transfers between devices: 40.8 us -> 48.1 us
    ppermute x8, waiting for transfers between devices: 20.4 us -> 27.5 us  [across(): lax.ppermute(value, 'tm', [(a, b) for a, b in pairs if 0 <= b < count])]
  transfers between devices with their start and end apart: 31 -> 31, of which waited for: 14 -> 15; matrix products, arithmetic and copies ran while one was open for 4% -> 5% of each run, Pallas kernels for 0% -> 0%
where the time goes in v5:
time: 133 us
  waiting for transfers between devices  48.1 us (36%)
  starting transfers between devices  47.1 us (35%)
  Pallas kernels  23.7 us (18%)
  local copies, waits for them, and re-layouts  6.4 us (5%)
  other arithmetic  6.2 us (5%)
    ppermute x8, waiting for transfers between devices, across(): lax.ppermute(value, 'tm', [(a, b) for a, b in pairs if 0 <= b < count])  27.5 us
    pallas_call x1, Pallas kernels, head_call(): pl.pallas_call(head_kernel, grid=(width // BLK,), in_specs=[pl.BlockSpec(...  23.1 us
    ppermute x8, starting transfers between devices, across(): lax.ppermute(value, 'tm', [(a, b) for a, b in pairs if 0 <= b < count])  14.3 us
    ppermute x4, starting transfers between devices, outward(): lax.ppermute(value, 'tm', [(a, b) for a, b in pairs if 0 <= b < count])  11.6 us
    ppermute x3, starting transfers between devices, pair_sum(): value = value + lax.ppermute(value, 'head', list(enumerate(partners)))  9.8 us
    ppermute x4, waiting for transfers between devices, outward(): lax.ppermute(value, 'tm', [(a, b) for a, b in pairs if 0 <= b < count])  8.93 us
    ppermute x4, starting transfers between devices, turned(): lax.ppermute(value, 'head', [(s, (s + steps) % count) for s in range(coun...  7.44 us
    ppermute x4, waiting for transfers between devices, turned(): lax.ppermute(value, 'head', [(s, (s + steps) % count) for s in range(coun...  5.96 us
  transfers between devices with their start and end apart: 31, of which 15 were waited for; matrix products, arithmetic and copies ran while one was open for 5% of the time, Pallas kernels for 0%

profile of v5, /device:TPU:8, one launch (start us, length us, event | category | flops | bytes accessed | tf_op | source)
XLA Modules:
  0.0 132.6 jit_solution(7692386406454046045)
XLA Ops:
  0.7 1.6 %collective-permute-start.10 = (bf16[512,384]{1,0:T(8,128)(2,1)}, bf16[512,384]{1,0:T(8,128)(2,1)S(1)}, u32[]{:S(2)}, u32[]{:S(2)}) collective-permute-start(bf16[512,384]{1,0:T(8,128)(2,1)} %refs_7_.1), channel_id=1, source_target_pairs={{0,16},{8,24},{16,0},{24,8},{32,48},{40,56},{48,32},{56,40},{64,80... | collective-permute-start | bytes 1179656 | tf_op jit(solution)/shard_map/ppermute | solution.py:132
  2.3 3.9 %collective-permute-start.11 = (bf16[512,384]{1,0:T(8,128)(2,1)}, bf16[512,384]{1,0:T(8,128)(2,1)S(1)}, u32[]{:S(2)}, u32[]{:S(2)}) collective-permute-start(bf16[512,384]{1,0:T(8,128)(2,1)} %refs_7_.1), channel_id=1, source_target_pairs={{16,32},{24,40},{32,16},{40,24},{48,64},{56,72},{64,48},{72,56},{8... | collective-permute-start | bytes 1179656 | tf_op jit(solution)/shard_map/ppermute | solution.py:132
  6.4 1.0 copy-done.1
  7.4 1.0 copy-done.3
  8.4 0.5 row_squares.1
  8.9 1.9 %collective-permute-start.1 = (f32[2,512]{1,0:T(2,128)S(1)}, f32[2,512]{1,0:T(2,128)S(1)}, u32[]{:S(2)}, u32[]{:S(2)}) collective-permute-start(f32[2,512]{1,0:T(2,128)S(1)} %row_squares.1), channel_id=1, source_target_pairs={{0,1},{1,0},{2,3},{3,2},{4,5},{5,4},{6,7},{7,6},{8,9},{9,8},{10,11... | collective-permute-start | bytes 12296 | tf_op jit(solution)/shard_map/ppermute | solution.py:149
  10.8 1.7 %collective-permute-done.1 = f32[2,512]{1,0:T(2,128)S(1)} collective-permute-done((f32[2,512]{1,0:T(2,128)S(1)}, f32[2,512]{1,0:T(2,128)S(1)}, u32[]{:S(2)}, u32[]{:S(2)}) %collective-permute-start.1) | collective-permute-done | bytes 4128 | tf_op jit(solution)/shard_map/ppermute | solution.py:149
  12.5 5.9 %collective-permute-start.2 = (f32[2,512]{1,0:T(2,128)S(1)}, f32[2,512]{1,0:T(2,128)S(1)}, u32[]{:S(2)}, u32[]{:S(2)}) collective-permute-start(f32[2,512]{1,0:T(2,128)S(1)} %add.130), channel_id=1, source_target_pairs={{0,7},{1,2},{2,1},{3,4},{4,3},{5,6},{6,5},{7,0},{8,15},{9,10},{10,... | collective-permute-start | bytes 12296 | tf_op jit(solution)/shard_map/ppermute | solution.py:149
  18.5 1.5 %collective-permute-done.2 = f32[2,512]{1,0:T(2,128)S(1)} collective-permute-done((f32[2,512]{1,0:T(2,128)S(1)}, f32[2,512]{1,0:T(2,128)S(1)}, u32[]{:S(2)}, u32[]{:S(2)}) %collective-permute-start.2) | collective-permute-done | bytes 4128 | tf_op jit(solution)/shard_map/ppermute | solution.py:149
  20.0 2.0 %collective-permute-start.3 = (f32[2,512]{1,0:T(2,128)S(1)}, f32[2,512]{1,0:T(2,128)S(1)}, u32[]{:S(2)}, u32[]{:S(2)}) collective-permute-start(f32[2,512]{1,0:T(2,128)S(1)} %add.131), channel_id=1, source_target_pairs={{0,3},{1,6},{2,5},{3,0},{4,7},{5,2},{6,1},{7,4},{8,11},{9,14},{10,... | collective-permute-start | bytes 12296 | tf_op jit(solution)/shard_map/ppermute | solution.py:149
  22.3 0.6 gather_fusion
  22.9 2.5 %collective-permute-done.3 = f32[2,512]{1,0:T(2,128)S(1)} collective-permute-done((f32[2,512]{1,0:T(2,128)S(1)}, f32[2,512]{1,0:T(2,128)S(1)}, u32[]{:S(2)}, u32[]{:S(2)}) %collective-permute-start.3) | collective-permute-done | bytes 4128 | tf_op jit(solution)/shard_map/ppermute | solution.py:149
  25.4 0.7 copy-done.16
  26.3 0.8 collective-permute-start.4
  27.1 3.4 %collective-permute-start.5 = (bf16[512,384]{1,0:T(8,128)(2,1)S(1)}, bf16[512,384]{1,0:T(8,128)(2,1)S(1)}, u32[]{:S(2)}, u32[]{:S(2)}) collective-permute-start(bf16[512,384]{1,0:T(8,128)(2,1)S(1)} %fusion.9.refs_0_), channel_id=1, source_target_pairs={{16,32},{24,40},{32,16},{40,24},{48,64},{56,72},{64,48},{72,56},{8... | collective-permute-start | bytes 1179656 | tf_op jit(solution)/shard_map/ppermute | solution.py:132
  30.5 1.9 %collective-permute-start.14 = (bf16[512,384]{1,0:T(8,128)(2,1)S(1)}, bf16[512,384]{1,0:T(8,128)(2,1)S(1)}, u32[]{:S(2)}, u32[]{:S(2)}) collective-permute-start(bf16[512,384]{1,0:T(8,128)(2,1)S(1)} %broadcast_select_fusion), channel_id=1, source_target_pairs={{8,16},{16,8},{24,32},{32,24},{40,48},{48,40},{56,64},{64,56},{72,... | collective-permute-start | bytes 1179656 | tf_op jit(solution)/shard_map/ppermute | solution.py:160
  32.5 1.7 %collective-permute-start.12 = (bf16[512,384]{1,0:T(8,128)(2,1)S(1)}, bf16[512,384]{1,0:T(8,128)(2,1)S(1)}, u32[]{:S(2)}, u32[]{:S(2)}) collective-permute-start(bf16[512,384]{1,0:T(8,128)(2,1)S(1)} %collective-permute-done.10.refs_8_), channel_id=1, source_target_pairs={{0,8},{8,0},{16,24},{24,16},{32,40},{40,32},{48,56},{56,48},{64,72... | collective-permute-start | bytes 1179656 | tf_op jit(solution)/shard_map/ppermute | solution.py:154
  34.4 0.5 collective-permute-start.6
  34.9 5.2 %collective-permute-done.5.refs_2_ = bf16[512,384]{1,0:T(8,128)(2,1)S(1)} collective-permute-done((bf16[512,384]{1,0:T(8,128)(2,1)S(1)}, bf16[512,384]{1,0:T(8,128)(2,1)S(1)}, u32[]{:S(2)}, u32[]{:S(2)}) %collective-permute-start.5) | collective-permute-done | bytes 393248 | tf_op jit(solution)/shard_map/ppermute | solution.py:132
  40.1 2.1 %collective-permute-start.9 = (bf16[512,384]{1,0:T(8,128)(2,1)S(1)}, bf16[512,384]{1,0:T(8,128)(2,1)}, u32[]{:S(2)}, u32[]{:S(2)}) collective-permute-start(bf16[512,384]{1,0:T(8,128)(2,1)S(1)} %broadcast_select_fusion.1), channel_id=1, source_target_pairs={{8,16},{16,8},{24,32},{32,24},{40,48},{48,40},{56,64},{64,56},{72,... | collective-permute-start | bytes 1179656 | tf_op jit(solution)/shard_map/ppermute | solution.py:160
  42.2 0.9 collective-permute-done.14.refs_13_
  43.1 0.7 collective-permute-start.8
  44.3 0.6 copy.21
  44.9 0.7 copy-done.15
  45.6 1.0 fusion.18.refs_14_
  46.6 5.0 %collective-permute-done.9.refs_6_ = bf16[512,384]{1,0:T(8,128)(2,1)} collective-permute-done((bf16[512,384]{1,0:T(8,128)(2,1)S(1)}, bf16[512,384]{1,0:T(8,128)(2,1)}, u32[]{:S(2)}, u32[]{:S(2)}) %collective-permute-start.9) | collective-permute-done | bytes 393248 | tf_op jit(solution)/shard_map/ppermute | solution.py:160
  51.6 23.1 %head_attention.1 = (bf16[512,384]{1,0:T(8,128)(2,1)}, f32[512,384]{1,0:T(8,128)}, bf16[512,384]{1,0:T(8,128)(2,1)}, bf16[512,384]{1,0:T(8,128)(2,1)}, bf16[512,...) custom-call(f32[28,512]{1,0:T(8,128)} %bitcast.28, ...), custom_call_target="tpu_custom_call" | custom-call | flops 8999999488 | bytes 12000000 | tf_op jit(solution)/shard_map/head_attention/pallas_call | solution.py:105
  74.8 1.9 %collective-permute-start.17 = (bf16[512,384]{1,0:T(8,128)(2,1)}, bf16[512,384]{1,0:T(8,128)(2,1)S(1)}, u32[]{:S(2)}, u32[]{:S(2)}) collective-permute-start(bf16[512,384]{1,0:T(8,128)(2,1)} %get-tuple-element.42), channel_id=1, source_target_pairs={{8,16},{16,8},{24,32},{32,24},{40,48},{48,40},{56,64},{64,56},{72,... | collective-permute-start | bytes 1179656 | tf_op jit(solution)/shard_map/ppermute | solution.py:160
  76.8 0.6 collective-permute-start.19
  77.4 5.7 %collective-permute-start.22 = (bf16[512,384]{1,0:T(8,128)(2,1)}, bf16[512,384]{1,0:T(8,128)(2,1)S(1)}, u32[]{:S(2)}, u32[]{:S(2)}) collective-permute-start(bf16[512,384]{1,0:T(8,128)(2,1)} %get-tuple-element.47), channel_id=1, source_target_pairs={{8,16},{16,8},{24,32},{32,24},{40,48},{48,40},{56,64},{64,56},{72,... | collective-permute-start | bytes 1179656 | tf_op jit(solution)/shard_map/ppermute | solution.py:160
  83.2 3.0 %collective-permute-done.17 = bf16[512,384]{1,0:T(8,128)(2,1)S(1)} collective-permute-done((bf16[512,384]{1,0:T(8,128)(2,1)}, bf16[512,384]{1,0:T(8,128)(2,1)S(1)}, u32[]{:S(2)}, u32[]{:S(2)}) %collective-permute-start.17) | collective-permute-done | bytes 393248 | tf_op jit(solution)/shard_map/ppermute | solution.py:160
  86.2 1.5 %fusion.3 = (bf16[512,384]{1,0:T(8,128)(2,1)S(1)}, bf16[512,384]{1,0:T(8,128)(2,1)S(1)}) fusion(bf16[512,384]{1,0:T(8,128)(2,1)S(1)} %collective-permute-done.17, bf16[512,384]{1,0:T(8,128)(2,1)S(1)} %collective-permute-done.19, bf16[512,384]{1,0:T(8,128)(2,1)} %get-tuple-element.43, pred[]{:T(512)S(6)} %gt.9, ...), kind=kLoop, calls=%fused_computation.14 | loop fusion | flops 2555904 | bytes 2752513 | tf_op jit(solution)/shard_map/convert_element_type | solution.py:175
  87.9 2.3 %collective-permute-start.20 = (bf16[512,384]{1,0:T(8,128)(2,1)S(1)}, bf16[512,384]{1,0:T(8,128)(2,1)S(1)}, u32[]{:S(2)}, u32[]{:S(2)}) collective-permute-start(bf16[512,384]{1,0:T(8,128)(2,1)S(1)} %get-tuple-element.68), channel_id=1, source_target_pairs={{16,32},{24,40},{32,16},{40,24},{48,64},{56,72},{64,48},{72,56},{8... | collective-permute-start | bytes 1179656 | tf_op jit(solution)/shard_map/ppermute | solution.py:132
  90.5 0.8 copy-done.13
  91.7 7.7 %collective-permute-done.18 = bf16[512,384]{1,0:T(8,128)(2,1)S(1)} collective-permute-done((bf16[512,384]{1,0:T(8,128)(2,1)S(1)}, bf16[512,384]{1,0:T(8,128)(2,1)S(1)}, u32[]{:S(2)}, u32[]{:S(2)}) %collective-permute-start.18) | collective-permute-done | bytes 393248 | tf_op jit(solution)/shard_map/ppermute | solution.py:132
  99.4 4.0 %collective-permute-done.20 = bf16[512,384]{1,0:T(8,128)(2,1)S(1)} collective-permute-done((bf16[512,384]{1,0:T(8,128)(2,1)S(1)}, bf16[512,384]{1,0:T(8,128)(2,1)S(1)}, u32[]{:S(2)}, u32[]{:S(2)}) %collective-permute-start.20) | collective-permute-done | bytes 393248 | tf_op jit(solution)/shard_map/ppermute | solution.py:132
  103.4 0.4 fusion.11
  103.8 3.5 %collective-permute-start.24 = (f32[2,512]{1,0:T(2,128)S(1)}, f32[2,512]{1,0:T(2,128)S(1)}, u32[]{:S(2)}, u32[]{:S(2)}) collective-permute-start(f32[2,512]{1,0:T(2,128)S(1)} %pad_maximum_fusion), channel_id=1, source_target_pairs={{0,7},{1,0},{2,1},{3,2},{4,3},{5,4},{6,5},{7,6},{8,15},{9,8},{10,9... | collective-permute-start | bytes 12296 | tf_op jit(solution)/shard_map/ppermute | solution.py:137
  107.3 1.3 collective-permute-done.24
  108.7 3.5 %collective-permute-done.25 = f32[2,512]{1,0:T(2,128)S(1)} collective-permute-done((f32[2,512]{1,0:T(2,128)S(1)}, f32[2,512]{1,0:T(2,128)S(1)}, u32[]{:S(2)}, u32[]{:S(2)}) %collective-permute-start.25) | collective-permute-done | bytes 4128 | tf_op jit(solution)/shard_map/ppermute | solution.py:137
  112.2 0.8 collective-permute-start.26
  112.9 3.1 %collective-permute-start.27 = (f32[2,512]{1,0:T(2,128)S(1)}, f32[2,512]{1,0:T(2,128)S(1)}, u32[]{:S(2)}, u32[]{:S(2)}) collective-permute-start(f32[2,512]{1,0:T(2,128)S(1)} %get-tuple-element.65), channel_id=1, source_target_pairs={{0,3},{1,4},{2,5},{3,6},{4,7},{5,0},{6,1},{7,2},{8,11},{9,12},{10,... | collective-permute-start | bytes 12296 | tf_op jit(solution)/shard_map/ppermute | solution.py:137
  116.2 2.2 %collective-permute-start.30 = (bf16[512,384]{1,0:T(8,128)(2,1)S(1)}, bf16[512,384]{1,0:T(8,128)(2,1)S(1)}, u32[]{:S(2)}, u32[]{:S(2)}) collective-permute-start(bf16[512,384]{1,0:T(8,128)(2,1)S(1)} %get-tuple-element.57), channel_id=1, source_target_pairs={{16,32},{24,40},{32,16},{40,24},{48,64},{56,72},{64,48},{72,56},{8... | collective-permute-start | bytes 1179656 | tf_op jit(solution)/shard_map/ppermute | solution.py:132
  118.4 1.1 collective-permute-done.27
  119.6 1.5 %fusion.15 = (bf16[512,384]{1,0:T(8,128)(2,1)}, bf16[512,384]{1,0:T(8,128)(2,1)}) fusion(bf16[512,384]{1,0:T(8,128)(2,1)S(1)} %copy-done.4, f32[512]{0:T(512)S(1)} %bitcast.40, f32[512]{0:T(512)S(1)} %multiply_multiply_fusion, f32[384]{0:T(512)S(1)} %copy-done.16, f32[512]{0:T(512)S(1)} %bitcast.35, bf16[512,384]{1,0:T(8,128)(2,1)S(1)} %collective-permute-done.20, ...), kind=kLoop, calls=%fused_computation.26 | loop fusion | flops 4521984 | bytes 3947520 | tf_op jit(solution)/shard_map/convert_element_type | solution.py:236
  121.1 6.5 %collective-permute-done.29 = bf16[512,384]{1,0:T(8,128)(2,1)S(1)} collective-permute-done((bf16[512,384]{1,0:T(8,128)(2,1)S(1)}, bf16[512,384]{1,0:T(8,128)(2,1)S(1)}, u32[]{:S(2)}, u32[]{:S(2)}) %collective-permute-start.29) | collective-permute-done | bytes 393248 | tf_op jit(solution)/shard_map/ppermute | solution.py:132
  127.6 4.0 %collective-permute-done.30 = bf16[512,384]{1,0:T(8,128)(2,1)S(1)} collective-permute-done((bf16[512,384]{1,0:T(8,128)(2,1)S(1)}, bf16[512,384]{1,0:T(8,128)(2,1)S(1)}, u32[]{:S(2)}, u32[]{:S(2)}) %collective-permute-start.30) | collective-permute-done | bytes 393248 | tf_op jit(solution)/shard_map/ppermute | solution.py:132
  131.6 0.9 add_convert_fusion
  (90 shorter events, 2.9 us)
Async XLA Ops:
  0.6 17.8 %copy-start = (s32[32,7,4,4]{0,3,2,1:T(4,128)S(1)}, s32[32,7,4,4]{0,3,2,1:T(4,128)}, u32[]{:S(2)}) copy-start(s32[32,7,4,4]{0,3,2,1:T(4,128)} %param.12) | copy-start | bytes 43012
  0.6 5.7 %collective-permute-start = (bf16[512,384]{1,0:T(8,128)(2,1)}, bf16[512,384]{1,0:T(8,128)(2,1)}, u32[]{:S(2)}, u32[]{:S(2)}) collective-permute-start(bf16[512,384]{1,0:T(8,128)(2,1)} %refs_7_.1), channel_id=1, source_target_pairs={{0,8},{8,0},{16,24},{24,16},{32,40},{40,32},{48,56},{56,48},{64,72... | collective-permute-start | bytes 1179656 | tf_op jit(solution)/shard_map/ppermute | solution.py:154
  0.7 29.7 %collective-permute-start.10 = (bf16[512,384]{1,0:T(8,128)(2,1)}, bf16[512,384]{1,0:T(8,128)(2,1)S(1)}, u32[]{:S(2)}, u32[]{:S(2)}) collective-permute-start(bf16[512,384]{1,0:T(8,128)(2,1)} %refs_7_.1), channel_id=1, source_target_pairs={{0,16},{8,24},{16,0},{24,8},{32,48},{40,56},{48,32},{56,40},{64,80... | collective-permute-start | bytes 1179656 | tf_op jit(solution)/shard_map/ppermute | solution.py:132
  2.3 28.1 %collective-permute-start.11 = (bf16[512,384]{1,0:T(8,128)(2,1)}, bf16[512,384]{1,0:T(8,128)(2,1)S(1)}, u32[]{:S(2)}, u32[]{:S(2)}) collective-permute-start(bf16[512,384]{1,0:T(8,128)(2,1)} %refs_7_.1), channel_id=1, source_target_pairs={{16,32},{24,40},{32,16},{40,24},{48,64},{56,72},{64,48},{72,56},{8... | collective-permute-start | bytes 1179656 | tf_op jit(solution)/shard_map/ppermute | solution.py:132
  6.4 1.0 copy-start.1
  7.4 1.0 copy-start.3
  8.4 17.1 %copy-start.4 = (bf16[512,384]{1,0:T(8,128)(2,1)S(1)}, bf16[512,384]{1,0:T(8,128)(2,1)}, u32[]{:S(2)}) copy-start(bf16[512,384]{1,0:T(8,128)(2,1)} %refs_1_) | copy-start | bytes 1179652
  8.9 3.6 %collective-permute-start.1 = (f32[2,512]{1,0:T(2,128)S(1)}, f32[2,512]{1,0:T(2,128)S(1)}, u32[]{:S(2)}, u32[]{:S(2)}) collective-permute-start(f32[2,512]{1,0:T(2,128)S(1)} %row_squares.1), channel_id=1, source_target_pairs={{0,1},{1,0},{2,3},{3,2},{4,5},{5,4},{6,7},{7,6},{8,9},{9,8},{10,11... | collective-permute-start | bytes 12296 | tf_op jit(solution)/shard_map/ppermute | solution.py:149
  12.5 7.4 %collective-permute-start.2 = (f32[2,512]{1,0:T(2,128)S(1)}, f32[2,512]{1,0:T(2,128)S(1)}, u32[]{:S(2)}, u32[]{:S(2)}) collective-permute-start(f32[2,512]{1,0:T(2,128)S(1)} %add.130), channel_id=1, source_target_pairs={{0,7},{1,2},{2,1},{3,4},{4,3},{5,6},{6,5},{7,0},{8,15},{9,10},{10,... | collective-permute-start | bytes 12296 | tf_op jit(solution)/shard_map/ppermute | solution.py:149
  20.0 5.4 %collective-permute-start.3 = (f32[2,512]{1,0:T(2,128)S(1)}, f32[2,512]{1,0:T(2,128)S(1)}, u32[]{:S(2)}, u32[]{:S(2)}) collective-permute-start(f32[2,512]{1,0:T(2,128)S(1)} %add.131), channel_id=1, source_target_pairs={{0,3},{1,6},{2,5},{3,0},{4,7},{5,2},{6,1},{7,4},{8,11},{9,14},{10,... | collective-permute-start | bytes 12296 | tf_op jit(solution)/shard_map/ppermute | solution.py:149
  26.3 8.1 %copy-start.7 = (bf16[512,384]{1,0:T(8,128)(2,1)}, bf16[512,384]{1,0:T(8,128)(2,1)S(1)}, u32[]{:S(2)}) copy-start(bf16[512,384]{1,0:T(8,128)(2,1)S(1)} %fusion.9.refs_0_) | copy-start | bytes 1179652
  26.3 8.1 %collective-permute-start.4 = (bf16[512,384]{1,0:T(8,128)(2,1)S(1)}, bf16[512,384]{1,0:T(8,128)(2,1)S(1)}, u32[]{:S(2)}, u32[]{:S(2)}) collective-permute-start(bf16[512,384]{1,0:T(8,128)(2,1)S(1)} %fusion.9.refs_0_), channel_id=1, source_target_pairs={{0,16},{8,24},{16,0},{24,8},{32,48},{40,56},{48,32},{56,40},{64,80... | collective-permute-start | bytes 1179656 | tf_op jit(solution)/shard_map/ppermute | solution.py:132
  27.1 13.0 %collective-permute-start.5 = (bf16[512,384]{1,0:T(8,128)(2,1)S(1)}, bf16[512,384]{1,0:T(8,128)(2,1)S(1)}, u32[]{:S(2)}, u32[]{:S(2)}) collective-permute-start(bf16[512,384]{1,0:T(8,128)(2,1)S(1)} %fusion.9.refs_0_), channel_id=1, source_target_pairs={{16,32},{24,40},{32,16},{40,24},{48,64},{56,72},{64,48},{72,56},{8... | collective-permute-start | bytes 1179656 | tf_op jit(solution)/shard_map/ppermute | solution.py:132
  30.5 2.0 %copy-start.8 = (bf16[512,384]{1,0:T(8,128)(2,1)}, bf16[512,384]{1,0:T(8,128)(2,1)S(1)}, u32[]{:S(2)}) copy-start(bf16[512,384]{1,0:T(8,128)(2,1)S(1)} %collective-permute-done.10.refs_8_) | copy-start | bytes 1179652
  30.5 3.7 %copy-start.9 = (bf16[512,384]{1,0:T(8,128)(2,1)}, bf16[512,384]{1,0:T(8,128)(2,1)S(1)}, u32[]{:S(2)}) copy-start(bf16[512,384]{1,0:T(8,128)(2,1)S(1)} %collective-permute-done.11.refs_9_) | copy-start | bytes 1179652
  30.5 12.5 %collective-permute-start.14 = (bf16[512,384]{1,0:T(8,128)(2,1)S(1)}, bf16[512,384]{1,0:T(8,128)(2,1)S(1)}, u32[]{:S(2)}, u32[]{:S(2)}) collective-permute-start(bf16[512,384]{1,0:T(8,128)(2,1)S(1)} %broadcast_select_fusion), channel_id=1, source_target_pairs={{8,16},{16,8},{24,32},{32,24},{40,48},{48,40},{56,64},{64,56},{72,... | collective-permute-start | bytes 1179656 | tf_op jit(solution)/shard_map/ppermute | solution.py:160
  32.5 10.6 %collective-permute-start.12 = (bf16[512,384]{1,0:T(8,128)(2,1)S(1)}, bf16[512,384]{1,0:T(8,128)(2,1)S(1)}, u32[]{:S(2)}, u32[]{:S(2)}) collective-permute-start(bf16[512,384]{1,0:T(8,128)(2,1)S(1)} %collective-permute-done.10.refs_8_), channel_id=1, source_target_pairs={{0,8},{8,0},{16,24},{24,16},{32,40},{40,32},{48,56},{56,48},{64,72... | collective-permute-start | bytes 1179656 | tf_op jit(solution)/shard_map/ppermute | solution.py:154
  34.2 12.4 %collective-permute-start.13 = (bf16[512,384]{1,0:T(8,128)(2,1)S(1)}, bf16[512,384]{1,0:T(8,128)(2,1)}, u32[]{:S(2)}, u32[]{:S(2)}) collective-permute-start(bf16[512,384]{1,0:T(8,128)(2,1)S(1)} %collective-permute-done.11.refs_9_), channel_id=1, source_target_pairs={{0,8},{8,0},{16,24},{24,16},{32,40},{40,32},{48,56},{56,48},{64,72... | collective-permute-start | bytes 1179656 | tf_op jit(solution)/shard_map/ppermute | solution.py:154
  34.4 8.7 %copy-start.10 = (bf16[512,384]{1,0:T(8,128)(2,1)}, bf16[512,384]{1,0:T(8,128)(2,1)S(1)}, u32[]{:S(2)}) copy-start(bf16[512,384]{1,0:T(8,128)(2,1)S(1)} %collective-permute-done.4.refs_1_) | copy-start | bytes 1179652
  34.4 12.2 %collective-permute-start.6 = (bf16[512,384]{1,0:T(8,128)(2,1)S(1)}, bf16[512,384]{1,0:T(8,128)(2,1)}, u32[]{:S(2)}, u32[]{:S(2)}) collective-permute-start(bf16[512,384]{1,0:T(8,128)(2,1)S(1)} %fusion.9.refs_0_), channel_id=1, source_target_pairs={{0,8},{8,0},{16,24},{24,16},{32,40},{40,32},{48,56},{56,48},{64,72... | collective-permute-start | bytes 1179656 | tf_op jit(solution)/shard_map/ppermute | solution.py:154
  40.1 3.0 %copy-start.11 = (bf16[512,384]{1,0:T(8,128)(2,1)}, bf16[512,384]{1,0:T(8,128)(2,1)S(1)}, u32[]{:S(2)}) copy-start(bf16[512,384]{1,0:T(8,128)(2,1)S(1)} %collective-permute-done.5.refs_2_) | copy-start | bytes 1179652
  40.1 4.8 %copy-start.2 = (bf16[512,384]{1,0:T(8,128)(2,1)S(1)}, bf16[512,384]{1,0:T(8,128)(2,1)}, u32[]{:S(2)}) copy-start(bf16[512,384]{1,0:T(8,128)(2,1)} %refs_0_.1) | copy-start | bytes 1179652
  40.1 11.4 %collective-permute-start.9 = (bf16[512,384]{1,0:T(8,128)(2,1)S(1)}, bf16[512,384]{1,0:T(8,128)(2,1)}, u32[]{:S(2)}, u32[]{:S(2)}) collective-permute-start(bf16[512,384]{1,0:T(8,128)(2,1)S(1)} %broadcast_select_fusion.1), channel_id=1, source_target_pairs={{8,16},{16,8},{24,32},{32,24},{40,48},{48,40},{56,64},{64,56},{72,... | collective-permute-start | bytes 1179656 | tf_op jit(solution)/shard_map/ppermute | solution.py:160
  43.1 8.5 %collective-permute-start.7 = (bf16[512,384]{1,0:T(8,128)(2,1)S(1)}, bf16[512,384]{1,0:T(8,128)(2,1)}, u32[]{:S(2)}, u32[]{:S(2)}) collective-permute-start(bf16[512,384]{1,0:T(8,128)(2,1)S(1)} %collective-permute-done.4.refs_1_), channel_id=1, source_target_pairs={{0,8},{8,0},{16,24},{24,16},{32,40},{40,32},{48,56},{56,48},{64,72... | collective-permute-start | bytes 1179656 | tf_op jit(solution)/shard_map/ppermute | solution.py:154
  43.1 0.9 copy-start.19
  43.1 8.5 %collective-permute-start.8 = (bf16[512,384]{1,0:T(8,128)(2,1)S(1)}, bf16[512,384]{1,0:T(8,128)(2,1)}, u32[]{:S(2)}, u32[]{:S(2)}) collective-permute-start(bf16[512,384]{1,0:T(8,128)(2,1)S(1)} %collective-permute-done.5.refs_2_), channel_id=1, source_target_pairs={{0,8},{8,0},{16,24},{24,16},{32,40},{40,32},{48,56},{56,48},{64,72... | collective-permute-start | bytes 1179656 | tf_op jit(solution)/shard_map/ppermute | solution.py:154
  74.7 8.4 %collective-permute-start.16 = (bf16[512,384]{1,0:T(8,128)(2,1)}, bf16[512,384]{1,0:T(8,128)(2,1)S(1)}, u32[]{:S(2)}, u32[]{:S(2)}) collective-permute-start(bf16[512,384]{1,0:T(8,128)(2,1)} %get-tuple-element.41), channel_id=1, source_target_pairs={{0,8},{8,0},{16,24},{24,16},{32,40},{40,32},{48,56},{56,48},{64,72... | collective-permute-start | bytes 1179656 | tf_op jit(solution)/shard_map/ppermute | solution.py:154
  74.8 11.4 %collective-permute-start.17 = (bf16[512,384]{1,0:T(8,128)(2,1)}, bf16[512,384]{1,0:T(8,128)(2,1)S(1)}, u32[]{:S(2)}, u32[]{:S(2)}) collective-permute-start(bf16[512,384]{1,0:T(8,128)(2,1)} %get-tuple-element.42), channel_id=1, source_target_pairs={{8,16},{16,8},{24,32},{32,24},{40,48},{48,40},{56,64},{64,56},{72,... | collective-permute-start | bytes 1179656 | tf_op jit(solution)/shard_map/ppermute | solution.py:160
  76.8 9.5 %collective-permute-start.19 = (bf16[512,384]{1,0:T(8,128)(2,1)}, bf16[512,384]{1,0:T(8,128)(2,1)S(1)}, u32[]{:S(2)}, u32[]{:S(2)}) collective-permute-start(bf16[512,384]{1,0:T(8,128)(2,1)} %get-tuple-element.44), channel_id=1, source_target_pairs={{0,8},{8,0},{16,24},{24,16},{32,40},{40,32},{48,56},{56,48},{64,72... | collective-permute-start | bytes 1179656 | tf_op jit(solution)/shard_map/ppermute | solution.py:154
  77.3 10.6 %collective-permute-start.21 = (bf16[512,384]{1,0:T(8,128)(2,1)}, bf16[512,384]{1,0:T(8,128)(2,1)S(1)}, u32[]{:S(2)}, u32[]{:S(2)}) collective-permute-start(bf16[512,384]{1,0:T(8,128)(2,1)} %get-tuple-element.46), channel_id=1, source_target_pairs={{0,8},{8,0},{16,24},{24,16},{32,40},{40,32},{48,56},{56,48},{64,72... | collective-permute-start | bytes 1179656 | tf_op jit(solution)/shard_map/ppermute | solution.py:154
  77.4 13.0 %collective-permute-start.22 = (bf16[512,384]{1,0:T(8,128)(2,1)}, bf16[512,384]{1,0:T(8,128)(2,1)S(1)}, u32[]{:S(2)}, u32[]{:S(2)}) collective-permute-start(bf16[512,384]{1,0:T(8,128)(2,1)} %get-tuple-element.47), channel_id=1, source_target_pairs={{8,16},{16,8},{24,32},{32,24},{40,48},{48,40},{56,64},{64,56},{72,... | collective-permute-start | bytes 1179656 | tf_op jit(solution)/shard_map/ppermute | solution.py:160
  83.1 7.3 %collective-permute-start.23 = (bf16[512,384]{1,0:T(8,128)(2,1)}, bf16[512,384]{1,0:T(8,128)(2,1)S(1)}, u32[]{:S(2)}, u32[]{:S(2)}) collective-permute-start(bf16[512,384]{1,0:T(8,128)(2,1)} %get-tuple-element.49), channel_id=1, source_target_pairs={{0,8},{8,0},{16,24},{24,16},{32,40},{40,32},{48,56},{56,48},{64,72... | collective-permute-start | bytes 1179656 | tf_op jit(solution)/shard_map/ppermute | solution.py:154
  86.2 5.4 %collective-permute-start.15 = (bf16[512,384]{1,0:T(8,128)(2,1)}, bf16[512,384]{1,0:T(8,128)(2,1)S(1)}, u32[]{:S(2)}, u32[]{:S(2)}) collective-permute-start(bf16[512,384]{1,0:T(8,128)(2,1)} %get-tuple-element.39), channel_id=1, source_target_pairs={{0,8},{8,0},{16,24},{24,16},{32,40},{40,32},{48,56},{56,48},{64,72... | collective-permute-start | bytes 1179656 | tf_op jit(solution)/shard_map/ppermute | solution.py:154
  86.2 4.0 %copy-start.5 = (f32[512,384]{1,0:T(8,128)S(1)}, f32[512,384]{1,0:T(8,128)}, u32[]{:S(2)}) copy-start(f32[512,384]{1,0:T(8,128)} %get-tuple-element.37) | copy-start | bytes 2359300
  87.8 11.6 %collective-permute-start.18 = (bf16[512,384]{1,0:T(8,128)(2,1)S(1)}, bf16[512,384]{1,0:T(8,128)(2,1)S(1)}, u32[]{:S(2)}, u32[]{:S(2)}) collective-permute-start(bf16[512,384]{1,0:T(8,128)(2,1)S(1)} %get-tuple-element.69), channel_id=1, source_target_pairs={{0,16},{8,24},{16,0},{24,8},{32,48},{40,56},{48,32},{56,40},{64,80... | collective-permute-start | bytes 1179656 | tf_op jit(solution)/shard_map/ppermute | solution.py:132
  87.9 15.5 %collective-permute-start.20 = (bf16[512,384]{1,0:T(8,128)(2,1)S(1)}, bf16[512,384]{1,0:T(8,128)(2,1)S(1)}, u32[]{:S(2)}, u32[]{:S(2)}) collective-permute-start(bf16[512,384]{1,0:T(8,128)(2,1)S(1)} %get-tuple-element.68), channel_id=1, source_target_pairs={{16,32},{24,40},{32,16},{40,24},{48,64},{56,72},{64,48},{72,56},{8... | collective-permute-start | bytes 1179656 | tf_op jit(solution)/shard_map/ppermute | solution.py:132
  90.2 1.0 copy-start.13
  90.2 1.1 copy-start.14
  91.3 12.1 %copy-start.6 = (bf16[512,384]{1,0:T(8,128)(2,1)S(1)}, bf16[512,384]{1,0:T(8,128)(2,1)}, u32[]{:S(2)}) copy-start(bf16[512,384]{1,0:T(8,128)(2,1)} %get-tuple-element.50) | copy-start | bytes 1179652
  103.4 12.6 %copy-start.17 = (bf16[512,384]{1,0:T(8,128)(2,1)S(1)}, bf16[512,384]{1,0:T(8,128)(2,1)}, u32[]{:S(2)}) copy-start(bf16[512,384]{1,0:T(8,128)(2,1)} %get-tuple-element.55) | copy-start | bytes 1179652
  103.8 4.9 %collective-permute-start.24 = (f32[2,512]{1,0:T(2,128)S(1)}, f32[2,512]{1,0:T(2,128)S(1)}, u32[]{:S(2)}, u32[]{:S(2)}) collective-permute-start(f32[2,512]{1,0:T(2,128)S(1)} %pad_maximum_fusion), channel_id=1, source_target_pairs={{0,7},{1,0},{2,1},{3,2},{4,3},{5,4},{6,5},{7,6},{8,15},{9,8},{10,9... | collective-permute-start | bytes 12296 | tf_op jit(solution)/shard_map/ppermute | solution.py:137
  107.3 4.8 %collective-permute-start.25 = (f32[2,512]{1,0:T(2,128)S(1)}, f32[2,512]{1,0:T(2,128)S(1)}, u32[]{:S(2)}, u32[]{:S(2)}) collective-permute-start(f32[2,512]{1,0:T(2,128)S(1)} %pad_maximum_fusion), channel_id=1, source_target_pairs={{0,1},{1,2},{2,3},{3,4},{4,5},{5,6},{6,7},{7,0},{8,9},{9,10},{10,1... | collective-permute-start | bytes 12296 | tf_op jit(solution)/shard_map/ppermute | solution.py:137
  112.2 6.2 %collective-permute-start.26 = (f32[2,512]{1,0:T(2,128)S(1)}, f32[2,512]{1,0:T(2,128)S(1)}, u32[]{:S(2)}, u32[]{:S(2)}) collective-permute-start(f32[2,512]{1,0:T(2,128)S(1)} %get-tuple-element.64), channel_id=1, source_target_pairs={{0,5},{1,6},{2,7},{3,0},{4,1},{5,2},{6,3},{7,4},{8,13},{9,14},{10,... | collective-permute-start | bytes 12296 | tf_op jit(solution)/shard_map/ppermute | solution.py:137
  112.9 6.6 %collective-permute-start.27 = (f32[2,512]{1,0:T(2,128)S(1)}, f32[2,512]{1,0:T(2,128)S(1)}, u32[]{:S(2)}, u32[]{:S(2)}) collective-permute-start(f32[2,512]{1,0:T(2,128)S(1)} %get-tuple-element.65), channel_id=1, source_target_pairs={{0,3},{1,4},{2,5},{3,6},{4,7},{5,0},{6,1},{7,2},{8,11},{9,12},{10,... | collective-permute-start | bytes 12296 | tf_op jit(solution)/shard_map/ppermute | solution.py:137
  116.1 5.0 %collective-permute-start.28 = (bf16[512,384]{1,0:T(8,128)(2,1)S(1)}, bf16[512,384]{1,0:T(8,128)(2,1)S(1)}, u32[]{:S(2)}, u32[]{:S(2)}) collective-permute-start(bf16[512,384]{1,0:T(8,128)(2,1)S(1)} %copy-done.17), channel_id=1, source_target_pairs={{0,8},{8,0},{16,24},{24,16},{32,40},{40,32},{48,56},{56,48},{64,72... | collective-permute-start | bytes 1179656 | tf_op jit(solution)/shard_map/ppermute | solution.py:154
  116.1 11.5 %collective-permute-start.29 = (bf16[512,384]{1,0:T(8,128)(2,1)S(1)}, bf16[512,384]{1,0:T(8,128)(2,1)S(1)}, u32[]{:S(2)}, u32[]{:S(2)}) collective-permute-start(bf16[512,384]{1,0:T(8,128)(2,1)S(1)} %get-tuple-element.56), channel_id=1, source_target_pairs={{0,16},{8,24},{16,0},{24,8},{32,48},{40,56},{48,32},{56,40},{64,80... | collective-permute-start | bytes 1179656 | tf_op jit(solution)/shard_map/ppermute | solution.py:132
  116.2 15.5 %collective-permute-start.30 = (bf16[512,384]{1,0:T(8,128)(2,1)S(1)}, bf16[512,384]{1,0:T(8,128)(2,1)S(1)}, u32[]{:S(2)}, u32[]{:S(2)}) collective-permute-start(bf16[512,384]{1,0:T(8,128)(2,1)S(1)} %get-tuple-element.57), channel_id=1, source_target_pairs={{16,32},{24,40},{32,16},{40,24},{48,64},{56,72},{64,48},{72,56},{8... | collective-permute-start | bytes 1179656 | tf_op jit(solution)/shard_map/ppermute | solution.py:132
  119.6 12.1 %copy-start.12 = (bf16[512,384]{1,0:T(8,128)(2,1)S(1)}, bf16[512,384]{1,0:T(8,128)(2,1)}, u32[]{:S(2)}) copy-start(bf16[512,384]{1,0:T(8,128)(2,1)} %get-tuple-element.60) | copy-start | bytes 1179652
  (3 other events, 2.2 us)
